TPU v7x, 256 devices: a whole 4x4x8 slice. The times are simulated.
256 devices in a mesh: dp: 32 (over y, x, core), sub: 8 (over z).
Axes of the slice: x: 4, y: 4, z: 8, core: 2. Of those that a mesh axis runs over, the one named last changes fastest.
Arguments:
- tokens: bfloat16 [32768, 1024], P('dp', 'sub'), may hold values from -6 to 6
- lengths: int32 [1024, 2], P('dp'), may hold values from 1 to 24, 32 in all within a row
- dest: int32 [1024], P('dp'), may hold values from 0 to 31, as said below
- w_query: bfloat16 [1024, 1024], P(None, 'sub'), may hold values from -0.1875 to 0.1875
- w_key: bfloat16 [1024, 1024], P(None, 'sub'), may hold values from -0.1875 to 0.1875
- w_value: bfloat16 [1024, 1024], P(None, 'sub'), may hold values from -0.1875 to 0.1875
- w_out: bfloat16 [1024, 1024], P('sub'), may hold values from -0.1875 to 0.1875
- w_up: bfloat16 [1024, 8192], P(None, 'sub'), may hold values from -0.1875 to 0.1875
- w_down: bfloat16 [8192, 1024], P('sub'), may hold values from -0.0625 to 0.0625
- final_gain: float32 [1024], replicated, may hold values from 0.1 to 1.9
- projection: bfloat16 [1024, 1024], replicated, may hold values from -0.1875 to 0.1875
Outputs:
- pq_rows: float32 [16, 2048, 64], P('sub', 'dp')
- covariance: float32 [1024, 1024], P(('dp', 'sub'))
Inputs may be any that keep to these rules, and one draw needn't show every extreme that they name: `dest`: every index of dp is the destination of exactly 32 blocks; the 32 blocks of one index of dp send at most 2 blocks to one destination, and exactly 2 to some. The lengths of each block sum to 32.
All inputs are finite; a program needn't handle non-finite values.
Results may differ from a plain program's by a relative error of at most 0.013.
Values may be sent and summed in bfloat16 or wider, within the bound.
No kernel may reach another device: no remote copies, remote signals or barrier semaphores. Data moves between devices by JAX's collectives and lax.ppermute only.
A program may use at most 64 MiB of HBM per device.

v0:
```python
import math

import jax
import jax.numpy as jnp
from jax import lax
from jax.sharding import PartitionSpec as P

HDIM = 64
SUBW = 64


epsilon = 1e-05


def normalize(rows):
    center = jnp.mean(rows, axis=-1, keepdims=True)
    shifted = rows - center
    spread = jnp.mean(shifted * shifted, axis=-1, keepdims=True)
    return shifted / jnp.sqrt(spread + epsilon)


def segment_ids(block_lens, block_rows):
    ends = jnp.cumsum(block_lens, axis=-1)
    position = jnp.arange(block_rows, dtype=jnp.int32)
    return jnp.sum((ends[:, None, :] <= position[None, :, None]).astype(jnp.int32), axis=-1)


def attend(query_rows, key_rows, value_rows, segment):
    scores = jnp.einsum(
        "bqhd,bkhd->bhqk", query_rows, key_rows, preferred_element_type=jnp.float32
    ) / math.sqrt(HDIM)
    matches = segment[:, None, :, None] == segment[:, None, None, :]
    raised = jnp.where(matches, jnp.exp(scores), 0.0)
    weights = (raised / jnp.sum(raised, axis=-1, keepdims=True)).astype(jnp.bfloat16)
    context = jnp.einsum("bhqk,bkhd->bqhd", weights, value_rows, preferred_element_type=jnp.float32)
    return context.astype(jnp.bfloat16)


def on_device(
    tokens, lengths, dest, w_query, w_key, w_value, w_out, w_up, w_down, final_gain, projection
):
    dp_count = lax.axis_size("dp")
    sub_count = lax.axis_size("sub")
    block_count, per_block = lengths.shape
    local_rows, local_width = tokens.shape
    block_rows = local_rows // block_count
    width = local_width * sub_count
    capacity = max(2, 2 * block_count // dp_count)
    slot_count = dp_count * capacity
    matches = dest[:, None] == dest[None, :]
    ordinal = jnp.arange(block_count, dtype=jnp.int32)
    earlier = ordinal[:, None] > ordinal[None, :]
    earlier_count = jnp.sum((matches & earlier).astype(jnp.int32), axis=1)
    target = dest * capacity + earlier_count
    placing = jnp.arange(slot_count, dtype=jnp.int32)[:, None] == target[None, :]
    send_rows = jnp.dot(
        placing.astype(jnp.bfloat16),
        tokens.reshape(block_count, block_rows * local_width),
        preferred_element_type=jnp.float32,
    ).astype(jnp.bfloat16)
    send_lens = jnp.sum(placing.astype(jnp.int32)[:, :, None] * lengths[None, :, :], axis=1)
    recv_rows, recv_lens = (
        lax.all_to_all(send_rows, "dp", split_axis=0, concat_axis=0, tiled=True),
        lax.all_to_all(send_lens, "dp", split_axis=0, concat_axis=0, tiled=True),
    )
    filled = (jnp.sum(recv_lens, axis=1) > 0).astype(jnp.int32)
    before = jnp.cumsum(filled) - filled
    picking = (ordinal[:, None] == before[None, :]) & (filled[None, :] > 0)
    packed = jnp.dot(
        picking.astype(jnp.bfloat16), recv_rows, preferred_element_type=jnp.float32
    ).astype(jnp.bfloat16)
    block_lens = jnp.sum(picking.astype(jnp.int32)[:, :, None] * recv_lens[None, :, :], axis=1)
    packed = packed.reshape(block_count * block_rows, local_width)
    row_major = lax.all_to_all(packed, "sub", split_axis=0, concat_axis=1, tiled=True)
    own_blocks = block_count // sub_count
    own_lens = lax.dynamic_slice_in_dim(
        block_lens, lax.axis_index("sub") * own_blocks, own_blocks, 0
    )
    segment = segment_ids(block_lens, block_rows)
    residual = row_major.astype(jnp.float32)
    normed = normalize(residual).astype(jnp.bfloat16)
    heads_local = w_query.shape[1] // HDIM
    w_qkv = jnp.concatenate((w_query, w_key, w_value), axis=1)
    projected = jnp.dot(
        lax.all_gather(normed, "sub", axis=0, tiled=True), w_qkv, preferred_element_type=jnp.float32
    ).astype(jnp.bfloat16)
    projected = projected.reshape(block_count, block_rows, 3, heads_local, HDIM)
    context = attend(projected[:, :, 0], projected[:, :, 1], projected[:, :, 2], segment)
    context = context.reshape(block_count * block_rows, local_width)
    hidden1 = residual + lax.psum_scatter(
        jnp.dot(context, w_out, preferred_element_type=jnp.float32).astype(jnp.bfloat16),
        "sub",
        scatter_dimension=0,
        tiled=True,
    ).astype(jnp.float32)
    normed2 = normalize(hidden1).astype(jnp.bfloat16)
    inner = jnp.maximum(
        jnp.dot(
            lax.all_gather(normed2, "sub", axis=0, tiled=True),
            w_up,
            preferred_element_type=jnp.float32,
        ),
        0.0,
    ).astype(jnp.bfloat16)
    hidden2 = hidden1 + lax.psum_scatter(
        jnp.dot(inner, w_down, preferred_element_type=jnp.float32).astype(jnp.bfloat16),
        "sub",
        scatter_dimension=0,
        tiled=True,
    ).astype(jnp.float32)
    finished = normalize(hidden2) * final_gain
    own_segment = segment_ids(own_lens, block_rows)
    onehot = (own_segment[..., None] == jnp.arange(per_block, dtype=jnp.int32)).astype(jnp.float32)
    totals = jnp.einsum(
        "brs,brd->bsd",
        onehot,
        finished.reshape(own_blocks, block_rows, width),
        precision=lax.Precision.HIGHEST,
    )
    pooled = (totals / own_lens[..., None].astype(jnp.float32)).reshape(
        own_blocks * per_block, width
    )
    sentence_total = float(pooled.shape[0] * dp_count * sub_count)
    column_mean = lax.psum(jnp.sum(pooled, axis=0), ("dp", "sub")) / sentence_total
    centred = pooled - column_mean
    covariance = lax.psum_scatter(
        jnp.dot(centred.T, centred, precision=lax.Precision.HIGHEST) / sentence_total,
        ("dp", "sub"),
        scatter_dimension=0,
        tiled=True,
    )
    rounded = centred.astype(jnp.bfloat16)
    rotated = jnp.dot(rounded, projection, preferred_element_type=jnp.float32)
    rotated = rotated.reshape(rounded.shape[0], width // SUBW, SUBW).transpose(1, 0, 2)
    pq_rows = lax.all_to_all(
        rotated.astype(jnp.bfloat16), "sub", split_axis=0, concat_axis=1, tiled=True
    ).astype(rotated.dtype)
    return (pq_rows, covariance)


def solution(mesh):
    in_specs = (
        P("dp", "sub"),
        P("dp", None),
        P("dp"),
        P(None, "sub"),
        P(None, "sub"),
        P(None, "sub"),
        P("sub", None),
        P(None, "sub"),
        P("sub", None),
        P(),
        P(),
    )
    out_specs = (P("sub", "dp", None), P(("dp", "sub"), None))
    return jax.shard_map(
        on_device, mesh=mesh, in_specs=in_specs, out_specs=out_specs, check_vma=False
    )
```

profile of v0, /device:TPU:1, one launch (start us, length us, event | category | flops | bytes accessed | tf_op | source)
XLA Modules:
  0.0 602.7 jit_solution(9616798349515988405)
XLA Ops:
  10.4 8.6 %all-to-all-start = ((s32[32,2,2]{1,2,0:T(2,128)}), s32[32,2,2]{1,2,0:T(2,128)S(1)}, u32[]{:S(2)}, u32[]{:S(2)}) async-start(s32[32,2,2]{1,2,0:T(2,128)} %copy.51), calls=%async_computation | async-start | bytes 65536 | tf_op jit(solution)/shard_map/all_to_all | solution.py:64
  21.7 4.6 all-to-all-done
  26.3 3.9 all-to-all-start.1
  30.8 11.1 %all-to-all-done.1 = bf16[32,2,4096]{2,1,0:T(2,128)(2,1)S(1)} async-done(((bf16[32,2,4096]{2,1,0:T(2,128)(2,1)}), bf16[32,2,4096]{2,1,0:T(2,128)(2,1)S(1)}, u32[]{:S(2)}, u32[]{:S(2)}) %all-to-all-start.1) | async-done | bytes 524320 | tf_op jit(solution)/shard_map/all_to_all | solution.py:63
  42.4 18.8 %all_to_all.43 = bf16[8,128,128]{2,1,0:T(8,128)(2,1)S(1)} all-to-all(bf16[8,128,128]{2,1,0:T(8,128)(2,1)S(1)} %all_to_all.36), channel_id=1, replica_groups=mesh['dp'=32,'sub'=8] {'sub'}, dimensions={0} | all-to-all | bytes 524288 | tf_op jit(solution)/shard_map/all_to_all | solution.py:74
  63.1 31.1 %all-gather.3.cloned.1.call-done = bf16[1024,1024]{1,0:T(8,128)(2,1)} async-done(((bf16[128,1024]{1,0:T(8,128)(2,1)}), bf16[1024,1024]{1,0:T(8,128)(2,1)}) %all-gather.3.cloned.1.call-update) | async-done | bytes 2097168 | tf_op jit(solution)/shard_map/all_gather | solution.py:85
  94.2 3.9 convolution_convert_fusion.4
  98.1 4.0 reshape.229
  102.1 2.7 fusion.34
  104.8 1.4 fusion.1
  106.2 1.9 fusion.2
  109.0 3.0 convolution_convert_fusion.3
  112.0 40.3 %reduce-scatter.3.cloned.1.call-done = bf16[128,1024]{1,0:T(8,128)(2,1)} async-done(((bf16[1024,1024]{1,0:T(8,128)(2,1)}), bf16[128,1024]{1,0:T(8,128)(2,1)}) %reduce-scatter.3.cloned.1.call-update) | async-done | bytes 262160 | tf_op jit(solution)/shard_map/reduce_scatter | solution.py:90
  154.8 40.4 %all-gather.5.cloned.1.call-done = bf16[1024,1024]{1,0:T(8,128)(2,1)} async-done(((bf16[128,1024]{1,0:T(8,128)(2,1)}), bf16[1024,1024]{1,0:T(8,128)(2,1)}) %all-gather.5.cloned.1.call-update) | async-done | bytes 2097168 | tf_op jit(solution)/shard_map/all_gather | solution.py:99
  195.1 8.0 %convolution_convert_fusion.2 = bf16[1024,1024]{1,0:T(8,128)(2,1)} fusion(bf16[1024,1024]{1,0:T(8,128)(2,1)S(1)} %copy-done, bf16[1024,1024]{1,0:T(8,128)(2,1)} %all-gather.5.cloned.1.call-done, bf16[1024,1024]{1,0:T(8,128)(2,1)} %param.18), kind=kOutput, calls=%fused_computation.4 | convolution fusion | flops 4298113024 | bytes 8388608 | tf_op jit(solution)/shard_map/dot_general | solution.py:106
  203.5 40.1 %reduce-scatter.5.cloned.1.call-done = bf16[128,1024]{1,0:T(8,128)(2,1)} async-done(((bf16[1024,1024]{1,0:T(8,128)(2,1)}), bf16[128,1024]{1,0:T(8,128)(2,1)}) %reduce-scatter.5.cloned.1.call-update) | async-done | bytes 262160 | tf_op jit(solution)/shard_map/reduce_scatter | solution.py:105
  247.3 78.9 %psum.7 = f32[1024]{0:T(1024)S(1)} all-reduce(f32[1024]{0:T(1024)S(1)} %get-tuple-element.9), channel_id=1, replica_groups=mesh['dp'=32,'sub'=8] {'dp','sub'}, use_global_device_ids=true, to_apply=%region_19.20 | all-reduce | flops 1024 | bytes 8192 | tf_op jit(solution)/shard_map/psum | solution.py:124
  326.2 5.1 bitcast_multiply_fusion
  331.3 3.9 copy.61
  335.3 2.5 fusion.3
  338.5 4.5 all-to-all-start.3
  343.1 6.6 %all-to-all-done.3 = bf16[8,2,512]{2,1,0:T(2,128)(2,1)S(1)} async-done(((bf16[8,2,512]{2,1,0:T(2,128)(2,1)}), bf16[8,2,512]{2,1,0:T(2,128)(2,1)S(1)}, u32[]{:S(2)}, u32[]{:S(2)}) %all-to-all-start.3) | async-done | bytes 16416 | tf_op jit(solution)/shard_map/all_to_all | solution.py:135
  350.4 244.3 %all-reduce.3.cloned.1.call-done = f32[1024,1024]{1,0:T(8,128)} async-done(((f32[1024,1024]{1,0:T(8,128)}), f32[1024,1024]{1,0:T(8,128)}) %all-reduce.3.cloned.1.call-update) | async-done | bytes 4194320
  594.8 1.4 constant_dynamic-slice_fusion
  (69 shorter events, 17.5 us)
Async XLA Ops:
  7.2 188.0 %copy-start = (bf16[1024,1024]{1,0:T(8,128)(2,1)S(1)}, bf16[1024,1024]{1,0:T(8,128)(2,1)}, u32[]{:S(2)}) copy-start(bf16[1024,1024]{1,0:T(8,128)(2,1)} %param.19) | copy-start | bytes 6291460
  10.4 15.8 %all-to-all-start = ((s32[32,2,2]{1,2,0:T(2,128)}), s32[32,2,2]{1,2,0:T(2,128)S(1)}, u32[]{:S(2)}, u32[]{:S(2)}) async-start(s32[32,2,2]{1,2,0:T(2,128)} %copy.51), calls=%async_computation | async-start | bytes 65536 | tf_op jit(solution)/shard_map/all_to_all | solution.py:64
  26.3 15.6 %all-to-all-start.1 = ((bf16[32,2,4096]{2,1,0:T(2,128)(2,1)}), bf16[32,2,4096]{2,1,0:T(2,128)(2,1)S(1)}, u32[]{:S(2)}, u32[]{:S(2)}) async-start(bf16[32,2,4096]{2,1,0:T(2,128)(2,1)} %all_to_all.33), calls=%async_computation.1 | async-start | bytes 1048576 | tf_op jit(solution)/shard_map/all_to_all | solution.py:63
  30.2 64.0 %all-gather.3.cloned.1.call-start = ((), (), s32[]{:S(2)}) async-start(), calls=%async_computation.6 | async-start | bytes 2359296 | tf_op jit(solution)/shard_map/all_gather | solution.py:85
  62.5 89.8 %reduce-scatter.3.cloned.1.call-start = ((), (), s32[]{:S(2)}) async-start(), calls=%async_computation.7 | async-start | bytes 2359296 | tf_op jit(solution)/shard_map/reduce_scatter | solution.py:90
  112.0 83.1 %all-gather.5.cloned.1.call-start = ((), (), s32[]{:S(2)}) async-start(), calls=%async_computation.8 | async-start | bytes 2359296 | tf_op jit(solution)/shard_map/all_gather | solution.py:99
  154.5 89.1 %reduce-scatter.5.cloned.1.call-start = ((), (), s32[]{:S(2)}) async-start(), calls=%async_computation.9 | async-start | bytes 2359296 | tf_op jit(solution)/shard_map/reduce_scatter | solution.py:105
  203.1 42.7 %copy-start.1 = (f32[1024]{0:T(1024)S(1)}, f32[1024]{0:T(1024)}, u32[]{:S(2)}) copy-start(f32[1024]{0:T(1024)} %param.20) | copy-start | bytes 12292
  203.2 391.6 %all-reduce.3.cloned.1.call-start = ((), (), s32[]{:S(2)}) async-start(), calls=%async_computation.10 | async-start | bytes 8388608
  338.5 11.2 %all-to-all-start.3 = ((bf16[8,2,512]{2,1,0:T(2,128)(2,1)}), bf16[8,2,512]{2,1,0:T(2,128)(2,1)S(1)}, u32[]{:S(2)}, u32[]{:S(2)}) async-start(bf16[8,2,512]{2,1,0:T(2,128)(2,1)} %reshape.242), calls=%async_computation.5 | async-start | bytes 32768 | tf_op jit(solution)/shard_map/all_to_all | solution.py:135
Sparse Core Ops, SparseCore 0:
  62.6 31.5 all-gather.2
  112.1 40.1 reduce-scatter.2
  154.7 40.4 all-gather.4
  203.3 40.2 reduce-scatter.4
  331.5 263.2 all-reduce.2
where the time goes:
time: 604 us; the launch traced here: 603 us
  waiting for transfers between devices  419 us (69%)
  blocking collectives  97.7 us (16%)
  matrix products  26.8 us (4%)
  starting transfers between devices  17.5 us (3%)
  local copies, waits for them, and re-layouts  17.3 us (3%)
  between operations  14 us (2%)
  other arithmetic  10.8 us (2%)
    unnamed x6, waiting for transfers between devices  244 us
    psum x1, blocking collectives, on_device(): lax.psum(jnp.sum(pooled, axis=0), ('dp', 'sub')) / sentence_total  78.9 us
    all_gather x1, waiting for transfers between devices, on_device(): lax.all_gather(normed2, 'sub', axis=0, tiled=True)  40.4 us
    reduce_scatter x1, waiting for transfers between devices, on_device(): lax.psum_scatter(jnp.dot(context, w_out, preferred_element_type=jnp.float...  40.3 us
    reduce_scatter x1, waiting for transfers between devices, on_device(): lax.psum_scatter(jnp.dot(inner, w_down, preferred_element_type=jnp.float3...  40.1 us
    all_gather x1, waiting for transfers between devices, on_device(): lax.all_gather(normed, 'sub', axis=0, tiled=True)  31.1 us
    all_to_all x1, blocking collectives, on_device(): lax.all_to_all(packed, 'sub', split_axis=0, concat_axis=1, tiled=True)  18.8 us
  transfers between devices with their start and end apart: 8, of which 8 were waited for; matrix products, arithmetic and copies ran while one was open for 2% of the time, Pallas kernels for 0%

commit v1 on v0

v1 whole, which is shorter than its diff:
```python
import functools
import math

import jax
import jax.numpy as jnp
from jax import lax
from jax.experimental import pallas as pl
from jax.experimental.pallas import tpu as pltpu
from jax.sharding import PartitionSpec as P

HDIM = 64
SUBW = 64
LANES = 128
SLOTS = 2

epsilon = 1e-05
BF = jnp.bfloat16
F32 = jnp.float32
HIGH = lax.Precision.HIGHEST


def normalize(rows):
    center = jnp.mean(rows, axis=-1, keepdims=True)
    shifted = rows - center
    spread = jnp.mean(shifted * shifted, axis=-1, keepdims=True)
    return shifted * lax.rsqrt(spread + epsilon)


def dot(a, b, dims=((1,), (0,)), precision=None):
    return lax.dot_general(a, b, (dims, ((), ())), precision=precision, preferred_element_type=F32)


def attention_kernel(x_ref, wq_ref, wk_ref, wv_ref, wo_ref, row_ref, col_ref, out_ref):
    rows = jnp.concatenate([x_ref[k] for k in range(x_ref.shape[0])], axis=-1).astype(F32)
    normed = normalize(rows).astype(BF)
    query = dot(normed, wq_ref[...]).astype(BF)
    key = dot(normed, wk_ref[...]).astype(BF)
    value = dot(normed, wv_ref[...]).astype(BF)
    matches = row_ref[...] == col_ref[...]
    heads = []
    for h in range(query.shape[1] // HDIM):
        cut = slice(h * HDIM, (h + 1) * HDIM)
        scores = dot(query[:, cut], key[:, cut], ((1,), (1,))) / math.sqrt(HDIM)
        raised = jnp.where(matches, jnp.exp(scores), 0.0)
        weights = (raised / jnp.sum(raised, axis=-1, keepdims=True)).astype(BF)
        heads.append(dot(weights, value[:, cut]).astype(BF))
    context = jnp.concatenate(heads, axis=-1)
    out_ref[...] = dot(context, wo_ref[...]).astype(BF)


def attention(gathered, w_query, w_key, w_value, w_out, keys):
    parts, rows, part = gathered.shape
    chunk = 128
    width = w_out.shape[1]
    whole = lambda a: pl.BlockSpec(a.shape, lambda i: (0,) * a.ndim)
    return pl.pallas_call(
        attention_kernel,
        grid=(rows // chunk,),
        in_specs=[
            pl.BlockSpec((parts, chunk, part), lambda i: (0, i, 0)),
            whole(w_query),
            whole(w_key),
            whole(w_value),
            whole(w_out),
            pl.BlockSpec((chunk, 1), lambda i: (i, 0)),
            pl.BlockSpec((1, chunk), lambda i: (0, i)),
        ],
        out_specs=pl.BlockSpec((chunk, width), lambda i: (i, 0)),
        out_shape=jax.ShapeDtypeStruct((rows, width), BF),
        compiler_params=pltpu.CompilerParams(vmem_limit_bytes=32 << 20),
        name="attention",
    )(gathered, w_query, w_key, w_value, w_out, keys[:, None], keys[None, :])


def pool_kernel(hidden_ref, gain_ref, member_ref, length_ref, out_ref):
    finished = normalize(hidden_ref[...]) * gain_ref[...]
    out_ref[...] = dot(member_ref[...], finished, precision=HIGH) / length_ref[...]


def moments_kernel(sub_ref, pooled_ref, proj_ref, code_ref, out_ref):
    me = sub_ref[0]
    pooled = pooled_ref[...]
    sentences, width = pooled.shape
    groups = out_ref.shape[0]
    per_group = width // groups
    own = out_ref.shape[1] // width - 3
    mean = jnp.mean(pooled, axis=0, keepdims=True)
    centred = pooled - mean
    feature = lax.broadcasted_iota(jnp.int32, (width, own * groups), 0)
    wanted = lax.broadcasted_iota(jnp.int32, (width, own * groups), 1)
    chosen = (wanted % groups) * per_group + me * own + wanted // groups
    pick = (feature == chosen).astype(F32)
    picked = dot(centred, pick, precision=HIGH)
    moments = dot(picked, centred, ((0,), (0,)), precision=HIGH)
    for j in range(own):
        out_ref[:, j * width:(j + 1) * width] = moments[j * groups:(j + 1) * groups].astype(BF)
    high = mean.astype(BF)
    low = (mean - high.astype(F32)).astype(BF)
    out_ref[:, own * width:(own + 1) * width] = jnp.broadcast_to(high, (groups, width))
    out_ref[:, (own + 1) * width:(own + 2) * width] = jnp.broadcast_to(low, (groups, width))
    rotated = dot(centred.astype(BF), proj_ref[...]).astype(BF)
    lanes = rotated.shape[1]
    kinds = 4
    target = lax.broadcasted_iota(jnp.int32, (kinds * groups, sentences), 0)
    target = (target % groups) * kinds + target // groups
    place = (target == code_ref[...]).astype(BF)
    placed = dot(place, rotated).astype(BF)
    filled = dot(place, jnp.ones((sentences, lanes), BF)).astype(BF)
    start = (own + 2) * width
    for k in range(kinds):
        out_ref[:, start + k * lanes:start + (k + 1) * lanes] = placed[k * groups:(k + 1) * groups]
        out_ref[:, start + (kinds + k) * lanes:start + (kinds + k + 1) * lanes] = filled[k * groups:(k + 1) * groups]


def combine_kernel(where_ref, recv_ref, proj_ref, pq_ref, cov_ref):
    first = where_ref[0]
    groups = recv_ref.shape[0]
    own, width = cov_ref.shape
    sentences = pq_ref.shape[1]
    total = float(groups * sentences)
    high = recv_ref[:, own * width:(own + 1) * width].astype(F32)
    low = recv_ref[:, (own + 1) * width:(own + 2) * width].astype(F32)
    means = high + low
    away = means - jnp.mean(means, axis=0, keepdims=True)
    feature = lax.broadcasted_iota(jnp.int32, (width, LANES), 0)
    lane = lax.broadcasted_iota(jnp.int32, (width, LANES), 1)
    pick = ((feature == first + lane) & (lane < own)).astype(F32)
    picked = dot(away, pick, precision=HIGH)
    between = dot(picked, away, ((0,), (0,)), precision=HIGH)
    for j in range(own):
        within = jnp.sum(recv_ref[:, j * width:(j + 1) * width].astype(F32), axis=0, keepdims=True)
        cov_ref[j:j + 1, :] = (within + float(sentences) * between[j:j + 1]) / total
    shift = dot(away, proj_ref[...].astype(F32), precision=HIGH)
    lanes = shift.shape[1]
    start = (own + 2) * width
    kinds = 4
    source = lax.broadcasted_iota(jnp.int32, (groups, groups), 0)
    other = lax.broadcasted_iota(jnp.int32, (groups, groups), 1)
    ahead = (source < other).astype(BF)
    same = (source == other).astype(BF)
    flags = [
        recv_ref[:, start + (kinds + 2 * c) * lanes:start + (kinds + 2 * c + 1) * lanes] for c in range(SLOTS)
    ]
    flat = [dot(f[:, :8], same, ((0,), (0,)))[:1] for f in flags]
    before = dot((flags[0] + flags[1])[:, :8], ahead, ((0,), (0,)))[:1]
    place = lax.broadcasted_iota(jnp.int32, (sentences, groups), 0)
    result = jnp.zeros((sentences, lanes), F32)
    for c in range(SLOTS):
        for k in range(2):
            rows = recv_ref[:, start + (2 * c + k) * lanes:start + (2 * c + k + 1) * lanes].astype(F32) + shift
            position = (2.0 * before + float(k)).astype(jnp.int32)
            chosen = jnp.where((place == position) & (flat[c] > 0.5), 1.0, 0.0)
            result = result + dot(chosen, rows, precision=HIGH)
        before = before + flat[c]
    for q in range(pq_ref.shape[0]):
        pq_ref[q] = result[:, q * SUBW:(q + 1) * SUBW]


def small_call(kernel, outs, args, scalar=None, name=None):
    specs = [pl.BlockSpec(memory_space=pltpu.VMEM) for _ in args]
    if scalar is not None:
        specs = [pl.BlockSpec(memory_space=pltpu.SMEM)] + specs
        args = (scalar,) + tuple(args)
    single = not isinstance(outs, (tuple, list))
    return pl.pallas_call(
        kernel,
        in_specs=specs,
        out_specs=pl.BlockSpec(memory_space=pltpu.VMEM) if single else [pl.BlockSpec(memory_space=pltpu.VMEM) for _ in outs],
        out_shape=outs,
        compiler_params=pltpu.CompilerParams(vmem_limit_bytes=32 << 20),
        name=name,
    )(*args)


def on_device(
    tokens, lengths, dest, w_query, w_key, w_value, w_out, w_up, w_down, final_gain, projection
):
    dp_count = lax.axis_size("dp")
    sub_count = lax.axis_size("sub")
    dp_at = lax.axis_index("dp")
    sub_at = lax.axis_index("sub")
    block_count, per_block = lengths.shape
    local_rows, local_width = tokens.shape
    block_rows = local_rows // block_count
    width = local_width * sub_count
    own_blocks = block_count // sub_count
    own_rows = own_blocks * block_rows

    ends = jnp.cumsum(lengths, axis=-1)
    position = jnp.arange(block_rows, dtype=jnp.int32)
    segment = jnp.sum((ends[:, None, :] <= position[None, :, None]).astype(jnp.int32), axis=-1)
    ordinal = jnp.arange(block_count, dtype=jnp.int32)
    keys = (ordinal[:, None] * per_block + segment).reshape(local_rows)
    own_lens = lax.dynamic_slice_in_dim(lengths, sub_at * own_blocks, own_blocks, 0)
    own_keys = lax.dynamic_slice_in_dim(keys, sub_at * own_rows, own_rows, 0)
    own_sentences = own_blocks * per_block
    member = (
        own_keys[None, :] == sub_at * own_sentences + jnp.arange(own_sentences, dtype=jnp.int32)[:, None]
    ).astype(F32)
    matches = dest[:, None] == dest[None, :]
    earlier = ordinal[:, None] > ordinal[None, :]
    earlier_count = jnp.sum((matches & earlier).astype(jnp.int32), axis=1)
    code = (dest * SLOTS + earlier_count)[:, None] * per_block + jnp.arange(per_block, dtype=jnp.int32)[None, :]
    code = code.reshape(1, block_count * per_block)

    gathered = lax.all_gather(tokens, "sub", axis=0, tiled=False)
    residual = lax.dynamic_slice_in_dim(gathered, sub_at * own_rows, own_rows, 1)
    residual = residual.transpose(1, 0, 2).reshape(own_rows, width).astype(F32)
    attended = attention(gathered, w_query, w_key, w_value, w_out, keys)
    hidden1 = residual + lax.psum_scatter(attended, "sub", scatter_dimension=0, tiled=True).astype(F32)
    normed2 = normalize(hidden1).astype(BF)
    inner = jnp.maximum(
        jnp.dot(lax.all_gather(normed2, "sub", axis=0, tiled=True), w_up, preferred_element_type=F32), 0.0
    ).astype(BF)
    hidden2 = hidden1 + lax.psum_scatter(
        jnp.dot(inner, w_down, preferred_element_type=F32).astype(BF), "sub", scatter_dimension=0, tiled=True
    ).astype(F32)
    pooled = small_call(
        pool_kernel,
        jax.ShapeDtypeStruct((own_sentences, width), F32),
        (hidden2, final_gain[None, :], member, own_lens.reshape(own_sentences, 1).astype(F32)),
        name="pool",
    )
    pooled = lax.all_to_all(
        jnp.broadcast_to(pooled[None], (sub_count, own_sentences, width)),
        "sub", split_axis=0, concat_axis=0, tiled=True,
    ).reshape(sub_count * own_sentences, width)
    sentences = sub_count * own_sentences
    cov_rows = width // (dp_count * sub_count)
    columns = width // sub_count
    proj = lax.dynamic_slice_in_dim(projection, sub_at * columns, columns, 1)
    sent = small_call(
        moments_kernel,
        jax.ShapeDtypeStruct((dp_count, (cov_rows + 3) * width), BF),
        (pooled, proj, code),
        scalar=sub_at.reshape(1),
        name="moments",
    )
    received = lax.all_to_all(sent, "dp", split_axis=0, concat_axis=0, tiled=True)
    return small_call(
        combine_kernel,
        (
            jax.ShapeDtypeStruct((columns // SUBW, sentences, SUBW), F32),
            jax.ShapeDtypeStruct((cov_rows, width), F32),
        ),
        (received, proj),
        scalar=((dp_at * sub_count + sub_at) * cov_rows).reshape(1),
        name="combine",
    )


def solution(mesh):
    in_specs = (
        P("dp", "sub"),
        P("dp", None),
        P("dp"),
        P(None, "sub"),
        P(None, "sub"),
        P(None, "sub"),
        P("sub", None),
        P(None, "sub"),
        P("sub", None),
        P(),
        P(),
    )
    out_specs = (P("sub", "dp", None), P(("dp", "sub"), None))
    return jax.shard_map(
        on_device, mesh=mesh, in_specs=in_specs, out_specs=out_specs, check_vma=False
    )
```

time: 604 us -> 258 us (0.43)
  waiting for transfers between devices: 419 us -> 181 us
  blocking collectives: 97.7 us -> 0 us
  matrix products: 26.8 us -> 8.03 us
  Pallas kernels: 0 us -> 14 us
    unnamed x6 -> x4, waiting for transfers between devices: 244 us -> 0.73 us
    psum x1 -> x0, blocking collectives: 78.9 us -> none  [on_device(): lax.psum(jnp.sum(pooled, axis=0), ('dp', 'sub')) / sentence_total]
    dot_general x10 -> x1, matrix products: 26.8 us -> 8.03 us  [on_device(): jnp.dot(inner, w_down, preferred_element_type=F32).astype(BF)]
    all_to_all x1 -> x0, blocking collectives: 18.8 us -> none  [on_device(): lax.all_to_all(packed, 'sub', split_axis=0, concat_axis=1, tiled=True)]
    pallas_call x0 -> x4, Pallas kernels: none -> 14 us  [the longest x1 9.79 us: attention(): pl.pallas_call(attention_kernel, grid=(rows // chunk,), in_specs=[pl.Bloc...]
    all_gather x1, waiting for transfers between devices: 31.1 us -> 41.6 us  [on_device(): gathered = lax.all_gather(tokens, 'sub', axis=0, tiled=False)]
    all_to_all x3 -> x2, waiting for transfers between devices: 22.4 us -> 19.1 us  [the longest x1 10.9 us: on_device(): lax.all_to_all(sent, 'dp', split_axis=0, concat_axis=0, tiled=True)]
    all_to_all x3 -> x2, starting transfers between devices: 17.1 us -> 17.5 us  [the longest x1 12.9 us: on_device(): lax.all_to_all(sent, 'dp', split_axis=0, concat_axis=0, tiled=True)]
  transfers between devices with their start and end apart: 8 -> 6, of which waited for: 8 -> 6; matrix products, arithmetic and copies ran while one was open for 2% -> 1% of each run, Pallas kernels for 0% -> 0%
where the time goes in v1:
time: 258 us; the launch traced here: 257 us
  waiting for transfers between devices  181 us (70%)
  starting transfers between devices  17.7 us (7%)
  local copies, waits for them, and re-layouts  14.6 us (6%)
  Pallas kernels  14 us (5%)
  between operations  13.9 us (5%)
  matrix products  8.03 us (3%)
  other arithmetic  7.59 us (3%)
    all_gather x1, waiting for transfers between devices, on_device(): gathered = lax.all_gather(tokens, 'sub', axis=0, tiled=False)  41.6 us
    all_gather x1, waiting for transfers between devices, on_device(): lax.all_gather(normed2, 'sub', axis=0, tiled=True)  40.4 us
    reduce_scatter x1, waiting for transfers between devices, on_device(): lax.psum_scatter(attended, 'sub', scatter_dimension=0, tiled=True)  40.4 us
    reduce_scatter x1, waiting for transfers between devices, on_device(): lax.psum_scatter(jnp.dot(inner, w_down, preferred_element_type=F32).astyp...  39.1 us
    all_to_all x1, starting transfers between devices, on_device(): lax.all_to_all(sent, 'dp', split_axis=0, concat_axis=0, tiled=True)  12.9 us
    unnamed x25, local copies, waits for them, and re-layouts  11.4 us
    all_to_all x1, waiting for transfers between devices, on_device(): lax.all_to_all(sent, 'dp', split_axis=0, concat_axis=0, tiled=True)  10.9 us
    pallas_call x1, Pallas kernels, attention(): pl.pallas_call(attention_kernel, grid=(rows // chunk,), in_specs=[pl.Bloc...  9.79 us
  transfers between devices with their start and end apart: 6, of which 6 were waited for; matrix products, arithmetic and copies ran while one was open for 1% of the time, Pallas kernels for 0%

profile of v1, /device:TPU:1, one launch (start us, length us, event | category | flops | bytes accessed | tf_op | source)
XLA Modules:
  0.0 257.1 jit_solution(13398605305404695519)
XLA Ops:
  9.4 41.6 %all-gather.6.cloned.1.call-done = bf16[8192,128]{1,0:T(8,128)(2,1)} async-done(((bf16[1024,128]{1,0:T(8,128)(2,1)}), bf16[8192,128]{1,0:T(8,128)(2,1)}) %all-gather.6.cloned.1.call-update) | async-done | bytes 2097168 | tf_op jit(solution)/shard_map/all_gather | solution.py:206
  51.0 1.6 copy-done.2
  52.6 0.9 copy-done.3
  54.5 0.9 copy-done.5
  55.5 0.9 copy-done.6
  56.4 9.8 %attention.1 = bf16[1024,1024]{1,0:T(8,128)(2,1)S(1)} custom-call(bf16[8,1024,128]{2,1,0:T(8,128)(2,1)S(1)} %bitcast.33, bf16[1024,128]{1,0:T(8,128)(2,1)S(1)} %copy-done.3, bf16[1024,128]{1,0:T(8,128)(2,1)S(1)} %copy-done.4, bf16[1024,128]{1,0:T(8,128)(2,1)S(1)} %copy-done.5, bf16[128,1024]{1,0:T(8,128)(2,1)S(1)} %copy-done.6, s32[1024,1]{1,0:T(8,128)S(1)} %add.120.row_ref, ...), custom_call_target="tpu_custom_call" | custom-call | tf_op jit(solution)/shard_map/attention/pallas_call | solution.py:56
  66.2 1.3 copy-done.1
  67.6 40.4 %reduce-scatter.3.cloned.1.call-done = bf16[128,1024]{1,0:T(8,128)(2,1)} async-done(((bf16[1024,1024]{1,0:T(8,128)(2,1)}), bf16[128,1024]{1,0:T(8,128)(2,1)}) %reduce-scatter.3.cloned.1.call-update) | async-done | bytes 262160 | tf_op jit(solution)/shard_map/reduce_scatter | solution.py:210
  108.0 1.2 fusion.2
  109.2 1.2 multiply_reduce_fusion
  110.4 1.9 multiply_convert_fusion
  112.4 40.4 %all-gather.4.cloned.1.call-done = bf16[1024,1024]{1,0:T(8,128)(2,1)} async-done(((bf16[128,1024]{1,0:T(8,128)(2,1)}), bf16[1024,1024]{1,0:T(8,128)(2,1)}) %all-gather.4.cloned.1.call-update) | async-done | bytes 2097168 | tf_op jit(solution)/shard_map/all_gather | solution.py:213
  152.8 8.0 %convolution_convert_fusion = bf16[1024,1024]{1,0:T(8,128)(2,1)} fusion(bf16[1024,1024]{1,0:T(8,128)(2,1)S(1)} %copy-done, bf16[1024,1024]{1,0:T(8,128)(2,1)} %all-gather.4.cloned.1.call-done, bf16[1024,1024]{1,0:T(8,128)(2,1)} %param.18), kind=kOutput, calls=%fused_computation.1 | convolution fusion | flops 4298113024 | bytes 8388608 | tf_op jit(solution)/shard_map/dot_general | solution.py:216
  162.0 39.1 %reduce-scatter.5.cloned.1.call-done = bf16[128,1024]{1,0:T(8,128)(2,1)} async-done(((bf16[1024,1024]{1,0:T(8,128)(2,1)}), bf16[128,1024]{1,0:T(8,128)(2,1)}) %reduce-scatter.5.cloned.1.call-update) | async-done | bytes 262160 | tf_op jit(solution)/shard_map/reduce_scatter | solution.py:215
  201.1 1.1 convert_add_fusion.hidden_ref
  203.5 4.6 %all-to-all-start = ((f32[8,8,1024]{2,1,0:T(8,128)}), f32[8,8,1024]{2,1,0:T(8,128)S(1)}, u32[]{:S(2)}, u32[]{:S(2)}) async-start(f32[8,8,1024]{2,1,0:T(8,128)} %broadcast_in_dim.5), calls=%async_computation.2 | async-start | bytes 524288 | tf_op jit(solution)/shard_map/all_to_all | solution.py:224
  208.3 1.0 constant_dynamic-slice_fusion.proj_ref
  209.3 8.2 %all-to-all-done = f32[8,8,1024]{2,1,0:T(8,128)S(1)} async-done(((f32[8,8,1024]{2,1,0:T(8,128)}), f32[8,8,1024]{2,1,0:T(8,128)S(1)}, u32[]{:S(2)}, u32[]{:S(2)}) %all-to-all-start) | async-done | bytes 262176 | tf_op jit(solution)/shard_map/all_to_all | solution.py:224
  217.5 1.3 moments.1
  220.2 1.1 reshape.135
  221.3 12.9 %all-to-all-start.1 = ((bf16[32,2,3584]{2,1,0:T(2,128)(2,1)}), bf16[32,2,3584]{2,1,0:T(2,128)(2,1)}, u32[]{:S(2)}, u32[]{:S(2)}) async-start(bf16[32,2,3584]{2,1,0:T(2,128)(2,1)} %reshape.135), calls=%async_computation.3 | async-start | bytes 917504 | tf_op jit(solution)/shard_map/all_to_all | solution.py:239
  234.2 10.9 %all-to-all-done.1 = bf16[32,2,3584]{2,1,0:T(2,128)(2,1)} async-done(((bf16[32,2,3584]{2,1,0:T(2,128)(2,1)}), bf16[32,2,3584]{2,1,0:T(2,128)(2,1)}, u32[]{:S(2)}, u32[]{:S(2)}) %all-to-all-start.1) | async-done | bytes 458784 | tf_op jit(solution)/shard_map/all_to_all | solution.py:239
  245.1 2.9 %reshape.136 = bf16[32,1,7168]{2,1,0:T(2,128)(2,1)S(1)} reshape(bf16[32,2,3584]{2,1,0:T(2,128)(2,1)} %all-to-all-done.1) | data formatting | bytes 917504
  248.2 2.4 combine.1
  (49 shorter events, 7.5 us)
Async XLA Ops:
  7.2 145.6 %copy-start = (bf16[1024,1024]{1,0:T(8,128)(2,1)S(1)}, bf16[1024,1024]{1,0:T(8,128)(2,1)}, u32[]{:S(2)}) copy-start(bf16[1024,1024]{1,0:T(8,128)(2,1)} %param.19) | copy-start | bytes 6291460
  7.2 43.9 %all-gather.6.cloned.1.call-start = ((), (), s32[]{:S(2)}) async-start(), calls=%async_computation.7 | async-start | bytes 2359296 | tf_op jit(solution)/shard_map/all_gather | solution.py:206
  7.9 100.1 %reduce-scatter.3.cloned.1.call-start = ((), (), s32[]{:S(2)}) async-start(), calls=%async_computation.4 | async-start | bytes 2359296 | tf_op jit(solution)/shard_map/reduce_scatter | solution.py:210
  51.0 1.6 copy-start.2
  52.6 0.9 copy-start.3
  53.6 0.9 copy-start.4
  54.5 0.9 copy-start.5
  55.5 0.9 copy-start.6
  66.2 1.3 copy-start.1
  67.6 85.2 %all-gather.4.cloned.1.call-start = ((), (), s32[]{:S(2)}) async-start(), calls=%async_computation.5 | async-start | bytes 2359296 | tf_op jit(solution)/shard_map/all_gather | solution.py:213
  112.3 88.8 %reduce-scatter.5.cloned.1.call-start = ((), (), s32[]{:S(2)}) async-start(), calls=%async_computation.6 | async-start | bytes 2359296 | tf_op jit(solution)/shard_map/reduce_scatter | solution.py:215
  160.8 0.7 copy-start.9
  160.8 0.9 copy-start.10
  160.8 40.3 %copy-start.8 = (bf16[128,1024]{1,0:T(8,128)(2,1)S(1)}, bf16[128,1024]{1,0:T(8,128)(2,1)}, u32[]{:S(2)}) copy-start(bf16[128,1024]{1,0:T(8,128)(2,1)} %reduce-scatter.3.cloned.1.call-done) | copy-start | bytes 786436
  160.8 41.4 %copy-start.7 = (f32[1024]{0:T(1024)S(1)}, f32[1024]{0:T(1024)}, u32[]{:S(2)}) copy-start(f32[1024]{0:T(1024)} %param.20) | copy-start | bytes 12292
  203.5 14.0 %all-to-all-start = ((f32[8,8,1024]{2,1,0:T(8,128)}), f32[8,8,1024]{2,1,0:T(8,128)S(1)}, u32[]{:S(2)}, u32[]{:S(2)}) async-start(f32[8,8,1024]{2,1,0:T(8,128)} %broadcast_in_dim.5), calls=%async_computation.2 | async-start | bytes 524288 | tf_op jit(solution)/shard_map/all_to_all | solution.py:224
  221.3 23.8 %all-to-all-start.1 = ((bf16[32,2,3584]{2,1,0:T(2,128)(2,1)}), bf16[32,2,3584]{2,1,0:T(2,128)(2,1)}, u32[]{:S(2)}, u32[]{:S(2)}) async-start(bf16[32,2,3584]{2,1,0:T(2,128)(2,1)} %reshape.135), calls=%async_computation.3 | async-start | bytes 917504 | tf_op jit(solution)/shard_map/all_to_all | solution.py:239
Sparse Core Ops, SparseCore 0:
  9.8 41.1 all-gather.5
  67.7 40.2 reduce-scatter.2
  112.4 40.2 all-gather.3
  160.9 40.1 reduce-scatter.4

commit v2 on v1

v2 whole, which is shorter than its diff:
```python
import functools
import math

import jax
import jax.numpy as jnp
from jax import lax
from jax.experimental import pallas as pl
from jax.experimental.pallas import tpu as pltpu
from jax.sharding import PartitionSpec as P

HDIM = 64
SUBW = 64
LANES = 128
SLOTS = 2
KINDS = 4
PACK = 8

epsilon = 1e-05
BF = jnp.bfloat16
F32 = jnp.float32
HIGH = lax.Precision.HIGHEST
VMEM_LIMIT = 48 << 20


def normalize(rows):
    center = jnp.mean(rows, axis=-1, keepdims=True)
    shifted = rows - center
    spread = jnp.mean(shifted * shifted, axis=-1, keepdims=True)
    return shifted * lax.rsqrt(spread + epsilon)


def dot(a, b, dims=((1,), (0,)), precision=None):
    return lax.dot_general(a, b, (dims, ((), ())), precision=precision, preferred_element_type=F32)


def cost(flops, size):
    return pl.CostEstimate(flops=flops, bytes_accessed=size, transcendentals=0)


def attention_kernel(parts, order_ref, *refs):
    pieces, (w_ref, wo_ref, row_ref, col_ref), outs = refs[:parts], refs[parts:parts + 4], refs[parts + 4:]
    rows_ref = outs[-1]
    me = order_ref[0]
    half = parts // 2
    part = pieces[0].shape[1]
    for k in range(parts):
        at = lax.rem(me + (k if k <= half else parts - (k - half)), parts)
        rows_ref[:, pl.ds(pl.multiple_of(at * part, part), part)] = pieces[k][...]
    rows = rows_ref[...].astype(F32)
    if len(outs) > 2:
        outs[1][...] = rows
    normed = normalize(rows).astype(BF)
    projected = dot(normed, w_ref[...]).astype(BF)
    local = wo_ref.shape[0]
    matches = row_ref[...] == col_ref[...]
    heads = []
    for h in range(local // HDIM):
        query, key, value = (
            projected[:, t * local + h * HDIM:t * local + (h + 1) * HDIM] for t in range(3)
        )
        scores = dot(query, key, ((1,), (1,))) / math.sqrt(HDIM)
        raised = jnp.where(matches, jnp.exp(scores), 0.0)
        weights = (raised / jnp.sum(raised, axis=-1, keepdims=True)).astype(BF)
        heads.append(dot(weights, value).astype(BF))
    context = jnp.concatenate(heads, axis=-1)
    outs[0][...] = dot(context, wo_ref[...])


def attention(pieces, w_qkv, w_out, keys, me, chunks, chunk, with_rows=False):
    parts = len(pieces)
    part = pieces[0].shape[1]
    width = w_out.shape[1]
    count = len(chunks)
    order = jnp.stack([me] + [lax.rem(me + c + parts, parts) for c in chunks]).astype(jnp.int32)
    whole = lambda a: pl.BlockSpec(a.shape, lambda i, o: (0,) * a.ndim)
    outs = [jax.ShapeDtypeStruct((count * chunk, width), F32)]
    if with_rows:
        outs.append(jax.ShapeDtypeStruct((count * chunk, width), F32))
    result = pl.pallas_call(
        functools.partial(attention_kernel, parts),
        grid_spec=pltpu.PrefetchScalarGridSpec(
            num_scalar_prefetch=1,
            grid=(count,),
            in_specs=[pl.BlockSpec((chunk, part), lambda i, o: (o[1 + i], 0)) for _ in range(parts)]
            + [
                whole(w_qkv),
                whole(w_out),
                pl.BlockSpec((chunk, 1), lambda i, o: (o[1 + i], 0)),
                pl.BlockSpec((1, chunk), lambda i, o: (0, o[1 + i])),
            ],
            out_specs=[pl.BlockSpec((chunk, width), lambda i, o: (i, 0)) for _ in outs],
            scratch_shapes=[pltpu.VMEM((chunk, width), BF)],
        ),
        out_shape=outs,
        compiler_params=pltpu.CompilerParams(vmem_limit_bytes=VMEM_LIMIT),
        cost_estimate=cost(count * 2 * chunk * width * 4 * w_out.shape[0], 3 << 20),
        name="attention",
    )(order, *pieces, w_qkv, w_out, keys[:, None], keys[None, :])
    return result if with_rows else result[0]


def middle_kernel(rows_ref, own_ref, right_ref, left_ref, hidden_ref, normed_ref):
    hidden = rows_ref[...] + (own_ref[...] + right_ref[...].astype(F32) + left_ref[...].astype(F32))
    hidden_ref[...] = hidden
    normed_ref[...] = normalize(hidden).astype(BF)


def feed_kernel(cuts, own_ref, pair_ref, up_ref, down_ref, gup_ref, gdown_ref, out_ref, send_ref, acc_ref):
    step = pl.program_id(0)
    count = own_ref.shape[0]
    rows = jnp.concatenate([own_ref[...], pair_ref[...]], axis=0)

    def add(up, down):
        inner = jnp.maximum(dot(rows, up), 0.0).astype(BF)
        return dot(inner, down)

    @pl.when(step == 0)
    def _():
        acc_ref[...] = jnp.zeros_like(acc_ref)

    @pl.when(step < cuts)
    def _():
        acc_ref[...] += add(up_ref[...], down_ref[...])

    @pl.when(step >= cuts)
    def _():
        up = gup_ref[...].reshape(-1, gup_ref.shape[-1])
        down = gdown_ref[...].reshape(-1, gdown_ref.shape[-1])
        acc_ref[...] += add(up, down)

    @pl.when(step == pl.num_programs(0) - 1)
    def _():
        out_ref[...] = acc_ref[:count]
        send_ref[...] = acc_ref[count:].astype(BF)


def feed(own, pair, w_up, w_down, gathered):
    spread, planes, both, width = gathered.shape
    rows = both // 2
    count = own.shape[0]
    hidden = w_up.shape[1]
    cuts = 2
    cut = hidden // cuts
    whole = lambda a: pl.BlockSpec(a.shape, lambda i: (0,) * a.ndim)
    late = lambda i: jnp.maximum(i - cuts, 0)
    early = lambda i: jnp.minimum(i, cuts - 1)
    return pl.pallas_call(
        functools.partial(feed_kernel, cuts),
        grid=(cuts * (planes + 1),),
        in_specs=[
            whole(own),
            whole(pair),
            pl.BlockSpec((width, cut), lambda i: (0, early(i))),
            pl.BlockSpec((cut, width), lambda i: (early(i), 0)),
            pl.BlockSpec((spread, 1, rows, cut), lambda i: (0, late(i) // cuts, 0, late(i) % cuts)),
            pl.BlockSpec((spread // cuts, 1, rows, width), lambda i: (late(i) % cuts, late(i) // cuts, 1, 0)),
        ],
        out_specs=[whole(own), whole(own)],
        out_shape=[jax.ShapeDtypeStruct(own.shape, F32), jax.ShapeDtypeStruct(own.shape, BF)],
        scratch_shapes=[pltpu.VMEM((2 * count, width), F32)],
        compiler_params=pltpu.CompilerParams(vmem_limit_bytes=VMEM_LIMIT),
        cost_estimate=cost(8 * count * width * hidden * (planes + 1), 4 * (planes + 1) * width * hidden),
        name="feed",
    )(own, pair, w_up, w_down, gathered, gathered)


def pool_kernel(hidden_ref, own_ref, pair_ref, gain_ref, member_ref, length_ref, out_ref):
    hidden = hidden_ref[...] + (own_ref[...] + pair_ref[...].astype(F32))
    finished = normalize(hidden) * gain_ref[...]
    pooled = dot(member_ref[...], finished, precision=HIGH) / length_ref[...]
    out_ref[...] = jnp.broadcast_to(pooled[None], out_ref.shape)


def moments_kernel(sub_ref, pooled_ref, proj_ref, code_ref, out_ref):
    me = sub_ref[0]
    parts, few, width = pooled_ref.shape
    sentences = parts * few
    pooled = pooled_ref[...].reshape(sentences, width)
    total = out_ref.shape[0]
    groups = total // PACK
    per_group = width // groups
    own = per_group // parts
    mean = jnp.mean(pooled, axis=0, keepdims=True)
    centred = pooled - mean
    feature = lax.broadcasted_iota(jnp.int32, (width, total), 0)
    wanted = lax.broadcasted_iota(jnp.int32, (width, total), 1)
    chosen = (wanted // PACK) * per_group + me * own + wanted % PACK
    pick = jnp.where((feature == chosen) & (wanted % PACK < own), 1.0, 0.0)
    picked = dot(centred, pick, precision=HIGH)
    moments = dot(picked, centred, ((0,), (0,)), precision=HIGH)
    rotated = dot(centred.astype(BF), proj_ref[...]).astype(BF)
    lanes = rotated.shape[1]
    row = lax.broadcasted_iota(jnp.int32, (total, sentences), 0)
    pieces = []
    flags = []
    ones = jnp.ones((sentences, lanes), BF)
    for k in range(KINDS):
        place = (row % PACK == own + 2) & ((row // PACK) * KINDS + k == code_ref[...])
        place = jnp.where(place, 1.0, 0.0).astype(BF)
        pieces.append(dot(place, rotated))
        flags.append(dot(place, ones))
    sides = jnp.concatenate(pieces + flags, axis=-1)
    high = mean.astype(BF).astype(F32)
    low = mean - high
    line = lax.broadcasted_iota(jnp.int32, (total, 1), 0) % PACK
    means = jnp.where(line == own, high, 0.0) + jnp.where(line == own + 1, low, 0.0)
    out_ref[...] = (moments + means + sides).astype(BF)


def combine_kernel(where_ref, recv_ref, proj_ref, pq_ref, cov_ref):
    first = where_ref[0]
    own, width = cov_ref.shape
    recv = recv_ref[...]
    total = recv.shape[0]
    groups = total // PACK
    sentences = pq_ref.shape[1]
    count = float(groups * sentences)
    source = lax.broadcasted_iota(jnp.int32, (groups, total), 0)
    line = lax.broadcasted_iota(jnp.int32, (groups, total), 1)
    pick_mean = (line == source * PACK + own) | (line == source * PACK + own + 1)
    means = dot(jnp.where(pick_mean, 1.0, 0.0).astype(BF), recv)
    sides = dot(jnp.where(line == source * PACK + own + 2, 1.0, 0.0).astype(BF), recv)
    line = lax.broadcasted_iota(jnp.int32, (PACK, total), 1) % PACK
    within = dot(jnp.where(line == lax.broadcasted_iota(jnp.int32, (PACK, total), 0), 1.0, 0.0).astype(BF), recv)
    away = means - jnp.mean(means, axis=0, keepdims=True)
    feature = lax.broadcasted_iota(jnp.int32, (width, LANES), 0)
    lane = lax.broadcasted_iota(jnp.int32, (width, LANES), 1)
    pick = jnp.where((feature == first + lane) & (lane < own), 1.0, 0.0)
    picked = dot(away, pick, precision=HIGH)
    between = dot(picked, away, ((0,), (0,)), precision=HIGH)
    cov_ref[...] = (within[:own] + float(sentences) * between[:own]) / count
    shift = dot(away, proj_ref[...].astype(F32), precision=HIGH)
    lanes = shift.shape[1]
    one = lax.broadcasted_iota(jnp.int32, (groups, groups), 0)
    other = lax.broadcasted_iota(jnp.int32, (groups, groups), 1)
    ahead = jnp.where(one < other, 1.0, 0.0).astype(BF)
    same = jnp.where(one == other, 1.0, 0.0).astype(BF)
    filled = [sides[:, (KINDS + 2 * c) * lanes:(KINDS + 2 * c + 1) * lanes] for c in range(SLOTS)]
    flat = [dot(f.astype(BF), same, ((0,), (0,)))[:1] for f in filled]
    before = dot((filled[0] + filled[1]).astype(BF), ahead, ((0,), (0,)))[:1]
    place = lax.broadcasted_iota(jnp.int32, (sentences, groups), 0)
    result = jnp.zeros((sentences, lanes), F32)
    for c in range(SLOTS):
        for k in range(2):
            rows = sides[:, (2 * c + k) * lanes:(2 * c + k + 1) * lanes] + shift
            position = (2.0 * before + float(k)).astype(jnp.int32)
            chosen = jnp.where((place == position) & (flat[c] > 0.5), 1.0, 0.0)
            result = result + dot(chosen, rows, precision=HIGH)
        before = before + flat[c]
    for q in range(pq_ref.shape[0]):
        pq_ref[q] = result[:, q * SUBW:(q + 1) * SUBW]


def small_call(kernel, outs, args, scalar=None, name=None):
    specs = [pl.BlockSpec(memory_space=pltpu.VMEM) for _ in args]
    if scalar is not None:
        specs = [pl.BlockSpec(memory_space=pltpu.SMEM)] + specs
        args = (scalar,) + tuple(args)
    single = not isinstance(outs, (tuple, list))
    return pl.pallas_call(
        kernel,
        in_specs=specs,
        out_specs=pl.BlockSpec(memory_space=pltpu.VMEM) if single else [pl.BlockSpec(memory_space=pltpu.VMEM) for _ in outs],
        out_shape=outs,
        compiler_params=pltpu.CompilerParams(vmem_limit_bytes=32 << 20),
        cost_estimate=cost(1 << 20, 1 << 20),
        name=name,
    )(*args)


def on_device(
    tokens, lengths, dest, w_query, w_key, w_value, w_out, w_up, w_down, final_gain, projection
):
    dp_count = lax.axis_size("dp")
    sub_count = lax.axis_size("sub")
    dp_at = lax.axis_index("dp")
    sub_at = lax.axis_index("sub")
    block_count, per_block = lengths.shape
    local_rows, local_width = tokens.shape
    block_rows = local_rows // block_count
    width = local_width * sub_count
    own_blocks = block_count // sub_count
    own_rows = own_blocks * block_rows
    half = sub_count // 2

    def move(array, by):
        return lax.ppermute(array, "sub", [(i, (i + by) % sub_count) for i in range(sub_count)])

    def swap(array):
        return lax.ppermute(array, "sub", [(i, i ^ 1) for i in range(sub_count)])

    rows = w_up.shape[0] // dp_count
    piece = jnp.concatenate(
        [lax.dynamic_slice_in_dim(w, dp_at * rows, rows, 0) for w in (w_up, w_down)], axis=0
    )
    others = jnp.concatenate([move(piece, by) for by in range(2, sub_count, 2)], axis=0)
    planes = half - 1

    ends = jnp.cumsum(lengths, axis=-1)
    position = jnp.arange(block_rows, dtype=jnp.int32)
    segment = jnp.sum((ends[:, None, :] <= position[None, :, None]).astype(jnp.int32), axis=-1)
    ordinal = jnp.arange(block_count, dtype=jnp.int32)
    keys = (ordinal[:, None] * per_block + segment).reshape(local_rows)
    own_lens = lax.dynamic_slice_in_dim(lengths, sub_at * own_blocks, own_blocks, 0)
    own_keys = lax.dynamic_slice_in_dim(keys, sub_at * own_rows, own_rows, 0)
    own_sentences = own_blocks * per_block
    member = (
        own_keys[None, :] == sub_at * own_sentences + jnp.arange(own_sentences, dtype=jnp.int32)[:, None]
    ).astype(F32)
    matches = dest[:, None] == dest[None, :]
    earlier = ordinal[:, None] > ordinal[None, :]
    earlier_count = jnp.sum((matches & earlier).astype(jnp.int32), axis=1)
    code = (dest * SLOTS + earlier_count)[:, None] * per_block + jnp.arange(per_block, dtype=jnp.int32)[None, :]
    code = code.reshape(1, block_count * per_block)
    w_qkv = jnp.concatenate((w_query, w_key, w_value), axis=1)
    columns = width // sub_count
    proj = lax.dynamic_slice_in_dim(projection, sub_at * columns, columns, 1)

    behind, before = [], []
    right = left = tokens
    for _ in range(half - 1):
        right, left = move(right, 1), move(left, -1)
        behind.append(right)
        before.append(left)
    middle = local_rows // 2
    far = jnp.concatenate([move(right[:middle], 1), move(left[middle:], -1)], axis=0)
    pieces = [tokens] + before + [far] + behind

    gathered = lax.all_gather(others, "dp", axis=0, tiled=True).reshape(dp_count, planes, 2 * rows, width)

    attend = functools.partial(attention, pieces, w_qkv, w_out, keys, sub_at, chunk=own_rows)
    part = attend(chunks=[half]).astype(BF)
    right, left = move(part[:own_rows // 2], 1), move(part[own_rows // 2:], -1)
    for away in range(half - 1, 0, -1):
        part = attend(chunks=[away, -away])
        ahead, back = part[:own_rows], part[own_rows:]
        if away == half - 1:
            right = jnp.concatenate([ahead[:own_rows // 2] + right.astype(F32), ahead[own_rows // 2:]], axis=0)
            left = jnp.concatenate([back[:own_rows // 2], back[own_rows // 2:] + left.astype(F32)], axis=0)
        else:
            right = ahead + right.astype(F32)
            left = back + left.astype(F32)
        right, left = move(right.astype(BF), 1), move(left.astype(BF), -1)
    part, residual = attend(chunks=[0], with_rows=True)
    own_shape = (own_rows, width)
    hidden1, normed2 = small_call(
        middle_kernel,
        (jax.ShapeDtypeStruct(own_shape, F32), jax.ShapeDtypeStruct(own_shape, BF)),
        (residual, part, right, left),
        name="middle",
    )
    fed, sent = feed(normed2, swap(normed2), w_up, w_down, gathered)
    pooled = small_call(
        pool_kernel,
        jax.ShapeDtypeStruct((sub_count, own_sentences, width), F32),
        (hidden1, fed, swap(sent), final_gain[None, :], member, own_lens.reshape(own_sentences, 1).astype(F32)),
        name="pool",
    )
    pooled = lax.all_to_all(pooled, "sub", split_axis=0, concat_axis=0, tiled=True)
    sentences = sub_count * own_sentences
    cov_rows = width // (dp_count * sub_count)
    sent = small_call(
        moments_kernel,
        jax.ShapeDtypeStruct((dp_count * PACK, width), BF),
        (pooled, proj, code),
        scalar=sub_at.reshape(1),
        name="moments",
    )
    received = lax.all_to_all(
        sent.reshape(dp_count, PACK, width), "dp", split_axis=0, concat_axis=0, tiled=True
    ).reshape(dp_count * PACK, width)
    return small_call(
        combine_kernel,
        (
            jax.ShapeDtypeStruct((columns // SUBW, sentences, SUBW), F32),
            jax.ShapeDtypeStruct((cov_rows, width), F32),
        ),
        (received, proj),
        scalar=((dp_at * sub_count + sub_at) * cov_rows).reshape(1),
        name="combine",
    )


def solution(mesh):
    in_specs = (
        P("dp", "sub"),
        P("dp", None),
        P("dp"),
        P(None, "sub"),
        P(None, "sub"),
        P(None, "sub"),
        P("sub", None),
        P(None, "sub"),
        P("sub", None),
        P(),
        P(),
    )
    out_specs = (P("sub", "dp", None), P(("dp", "sub"), None))
    return jax.shard_map(
        on_device, mesh=mesh, in_specs=in_specs, out_specs=out_specs, check_vma=False
    )
```

time: 258 us -> 204 us (0.79)
  waiting for transfers between devices: 181 us -> 54.3 us
  starting transfers between devices: 17.7 us -> 56 us
  Pallas kernels: 14 us -> 35.5 us
  local copies, waits for them, and re-layouts: 14.6 us -> 34.8 us
  matrix products: 8.03 us -> 0 us
    all_gather x2 -> x1, waiting for transfers between devices: 82 us -> 0.01 us  [on_device(): lax.all_gather(others, 'dp', axis=0, tiled=True)]
    reduce_scatter x2 -> x0, waiting for transfers between devices: 79.5 us -> none  [the longest x1 40.4 us: on_device(): lax.psum_scatter(attended, 'sub', scatter_dimension=0, tiled=True)]
    ppermute x0 -> x21, starting transfers between devices: none -> 34.6 us  [the longest x19 34.5 us: move(): lax.ppermute(array, 'sub', [(i, (i + by) % sub_count) for i in range(sub_...]
    ppermute x0 -> x21, waiting for transfers between devices: none -> 33.7 us  [the longest x19 21.6 us: move(): lax.ppermute(array, 'sub', [(i, (i + by) % sub_count) for i in range(sub_...]
    pallas_call x1 -> x6, Pallas kernels: 9.79 us -> 28.2 us  [the longest x5 16.7 us: attention(): pl.pallas_call(functools.partial(attention_kernel, parts), grid_spec=pltp...]
    unnamed x25 -> x87, local copies, waits for them, and re-layouts: 11.4 us -> 29.3 us
    dot_general x1 -> x0, matrix products: 8.03 us -> none  [on_device(): jnp.dot(inner, w_down, preferred_element_type=F32).astype(BF)]
    all_to_all x2, starting transfers between devices: 17.5 us -> 21.4 us  [the longest x1 17.2 us: on_device(): lax.all_to_all(sent.reshape(dp_count, PACK, width), 'dp', split_axis=0, c...]
  transfers between devices with their start and end apart: 6 -> 24, of which waited for: 6 -> 12; matrix products, arithmetic and copies ran while one was open for 1% -> 7% of each run, Pallas kernels for 0% -> 8%
where the time goes in v2:
time: 204 us; the launch traced here: 202 us
  starting transfers between devices  56 us (27%)
  waiting for transfers between devices  54.3 us (27%)
  Pallas kernels  35.5 us (17%)
  local copies, waits for them, and re-layouts  34.8 us (17%)
  between operations  14.5 us (7%)
  other arithmetic  7.22 us (4%)
    ppermute x19, starting transfers between devices, move(): lax.ppermute(array, 'sub', [(i, (i + by) % sub_count) for i in range(sub_...  34.5 us
    unnamed x87, local copies, waits for them, and re-layouts  29.3 us
    ppermute x19, waiting for transfers between devices, move(): lax.ppermute(array, 'sub', [(i, (i + by) % sub_count) for i in range(sub_...  21.6 us
    all_to_all x1, starting transfers between devices, on_device(): lax.all_to_all(sent.reshape(dp_count, PACK, width), 'dp', split_axis=0, c...  17.2 us
    pallas_call x5, Pallas kernels, attention(): pl.pallas_call(functools.partial(attention_kernel, parts), grid_spec=pltp...  16.7 us
    ppermute x2, waiting for transfers between devices, swap(): return lax.ppermute(array, 'sub', [(i, i ^ 1) for i in range(sub_count)])  12 us
    all_to_all x1, waiting for transfers between devices, on_device(): lax.all_to_all(sent.reshape(dp_count, PACK, width), 'dp', split_axis=0, c...  11.5 us
    pallas_call x1, Pallas kernels, feed(): pl.pallas_call(functools.partial(feed_kernel, cuts), grid=(cuts * (planes...  11.5 us
  transfers between devices with their start and end apart: 24, of which 12 were waited for; matrix products, arithmetic and copies ran while one was open for 7% of the time, Pallas kernels for 8%

profile of v2, /device:TPU:1, one launch (start us, length us, event | category | flops | bytes accessed | tf_op | source)
XLA Modules:
  0.0 202.4 jit_solution(16839576236339231670)
XLA Ops:
  8.3 6.9 %collective-permute-start.19 = (bf16[64,1024]{1,0:T(8,128)(2,1)S(1)}, bf16[64,1024]{1,0:T(8,128)(2,1)S(1)}, u32[]{:S(2)}, u32[]{:S(2)}) collective-permute-start(bf16[64,1024]{1,0:T(8,128)(2,1)S(1)} %pad_maximum_fusion.3), channel_id=1, source_target_pairs={{0,6},{1,7},{2,0},{3,1},{4,2},{5,3},{6,4},{7,5},{8,14},{9,15},{10,... | collective-permute-start | bytes 393224 | tf_op jit(solution)/shard_map/ppermute | solution.py:287
  18.5 7.8 %collective-permute-done.18 = bf16[64,1024]{1,0:T(8,128)(2,1)S(1)} collective-permute-done((bf16[64,1024]{1,0:T(8,128)(2,1)S(1)}, bf16[64,1024]{1,0:T(8,128)(2,1)S(1)}, u32[]{:S(2)}, u32[]{:S(2)}) %collective-permute-start.18) | collective-permute-done | bytes 131104 | tf_op jit(solution)/shard_map/ppermute | solution.py:287
  27.3 3.2 %collective-permute-start.3 = (bf16[1024,128]{1,0:T(8,128)(2,1)}, bf16[1024,128]{1,0:T(8,128)(2,1)S(1)}, u32[]{:S(2)}, u32[]{:S(2)}) collective-permute-start(bf16[1024,128]{1,0:T(8,128)(2,1)} %refs_0_.9), channel_id=1, source_target_pairs={{0,1},{1,2},{2,3},{3,4},{4,5},{5,6},{6,7},{7,0},{8,9},{9,10},{10,1... | collective-permute-start | bytes 786440 | tf_op jit(solution)/shard_map/ppermute | solution.py:287
  30.5 2.8 %collective-permute-start = (bf16[1024,128]{1,0:T(8,128)(2,1)}, bf16[1024,128]{1,0:T(8,128)(2,1)S(1)}, u32[]{:S(2)}, u32[]{:S(2)}) collective-permute-start(bf16[1024,128]{1,0:T(8,128)(2,1)} %refs_0_.9), channel_id=1, source_target_pairs={{0,7},{1,0},{2,1},{3,2},{4,3},{5,4},{6,5},{7,6},{8,15},{9,8},{10,9... | collective-permute-start | bytes 786440 | tf_op jit(solution)/shard_map/ppermute | solution.py:287
  34.1 5.0 %collective-permute-done.3.refs_5_ = bf16[1024,128]{1,0:T(8,128)(2,1)S(1)} collective-permute-done((bf16[1024,128]{1,0:T(8,128)(2,1)}, bf16[1024,128]{1,0:T(8,128)(2,1)S(1)}, u32[]{:S(2)}, u32[]{:S(2)}) %collective-permute-start.3) | collective-permute-done | bytes 262176 | tf_op jit(solution)/shard_map/ppermute | solution.py:287
  39.8 2.7 %collective-permute-start.1 = (bf16[1024,128]{1,0:T(8,128)(2,1)S(1)}, bf16[1024,128]{1,0:T(8,128)(2,1)}, u32[]{:S(2)}, u32[]{:S(2)}) collective-permute-start(bf16[1024,128]{1,0:T(8,128)(2,1)S(1)} %collective-permute-done.refs_1_), channel_id=1, source_target_pairs={{0,7},{1,0},{2,1},{3,2},{4,3},{5,4},{6,5},{7,6},{8,15},{9,8},{10,9... | collective-permute-start | bytes 786440 | tf_op jit(solution)/shard_map/ppermute | solution.py:287
  42.6 4.0 %collective-permute-done.4.refs_6_ = bf16[1024,128]{1,0:T(8,128)(2,1)} collective-permute-done((bf16[1024,128]{1,0:T(8,128)(2,1)S(1)}, bf16[1024,128]{1,0:T(8,128)(2,1)}, u32[]{:S(2)}, u32[]{:S(2)}) %collective-permute-start.4) | collective-permute-done | bytes 262176 | tf_op jit(solution)/shard_map/ppermute | solution.py:287
  47.6 2.7 %collective-permute-start.2 = (bf16[1024,128]{1,0:T(8,128)(2,1)}, bf16[1024,128]{1,0:T(8,128)(2,1)S(1)}, u32[]{:S(2)}, u32[]{:S(2)}) collective-permute-start(bf16[1024,128]{1,0:T(8,128)(2,1)} %collective-permute-done.1.refs_2_), channel_id=1, source_target_pairs={{0,7},{1,0},{2,1},{3,2},{4,3},{5,4},{6,5},{7,6},{8,15},{9,8},{10,9... | collective-permute-start | bytes 786440 | tf_op jit(solution)/shard_map/ppermute | solution.py:287
  55.1 3.0 %collective-permute-start.7 = (bf16[512,128]{1,0:T(8,128)(2,1)}, bf16[512,128]{1,0:T(8,128)(2,1)}, u32[]{:S(2)}, u32[]{:S(2)}) collective-permute-start(bf16[512,128]{1,0:T(8,128)(2,1)} %slice.57), channel_id=1, source_target_pairs={{0,7},{1,0},{2,1},{3,2},{4,3},{5,4},{6,5},{7,6},{8,15},{9,8},{10,9... | collective-permute-start | bytes 393224 | tf_op jit(solution)/shard_map/ppermute | solution.py:287
  67.4 2.6 %attention.9 = f32[128,1024]{1,0:T(8,128)S(1)} custom-call(s32[2]{0:T(128)S(1)} %get-tuple-element.25.order_ref, bf16[1024,128]{1,0:T(8,128)(2,1)S(1)} %copy-done.15, bf16[1024,128]{1,0:T(8,128)(2,1)S(1)} %copy-done.29, bf16[1024,128]{1,0:T(8,128)(2,1)} %collective-permute-done.1.refs_2_, bf16[1024,128]{1,0:T(8,128)(2,1)S(1)} %copy-done.7, ...), custom_call_target="tpu_custom_call" | custom-call | flops 134217728 | bytes 3145728 | tf_op jit(solution)/shard_map/attention/pallas_call | solution.py:79
  70.0 2.9 %collective-permute-start.12 = (bf16[64,1024]{1,0:T(8,128)(2,1)S(1)}, bf16[64,1024]{1,0:T(8,128)(2,1)S(1)}, u32[]{:S(2)}, u32[]{:S(2)}) collective-permute-start(bf16[64,1024]{1,0:T(8,128)(2,1)S(1)} %get-tuple-element.22), channel_id=1, source_target_pairs={{0,7},{1,0},{2,1},{3,2},{4,3},{5,4},{6,5},{7,6},{8,15},{9,8},{10,9... | collective-permute-start | bytes 393224 | tf_op jit(solution)/shard_map/ppermute | solution.py:287
  72.9 3.9 %attention.8 = f32[256,1024]{1,0:T(8,128)S(1)} custom-call(s32[3]{0:T(128)S(1)} %pad_add_fusion.3.order_ref, bf16[1024,128]{1,0:T(8,128)(2,1)S(1)} %copy-done.15, bf16[1024,128]{1,0:T(8,128)(2,1)S(1)} %copy-done.29, bf16[1024,128]{1,0:T(8,128)(2,1)} %collective-permute-done.1.refs_2_, bf16[1024,128]{1,0:T(8,128)(2,1)S(1)} %copy-done.7, ...), custom_call_target="tpu_custom_call" | custom-call | flops 268435456 | bytes 3145728 | tf_op jit(solution)/shard_map/attention/pallas_call | solution.py:79
  88.1 3.9 %attention.7 = f32[256,1024]{1,0:T(8,128)S(1)} custom-call(s32[3]{0:T(128)S(1)} %pad_add_fusion.2.order_ref, bf16[1024,128]{1,0:T(8,128)(2,1)S(1)} %copy-done.16, bf16[1024,128]{1,0:T(8,128)(2,1)S(1)} %copy-done.30, bf16[1024,128]{1,0:T(8,128)(2,1)} %collective-permute-done.1.refs_2_, bf16[1024,128]{1,0:T(8,128)(2,1)S(1)} %copy-done.8, ...), custom_call_target="tpu_custom_call" | custom-call | flops 268435456 | bytes 3145728 | tf_op jit(solution)/shard_map/attention/pallas_call | solution.py:79
  103.3 3.9 %attention.6 = f32[256,1024]{1,0:T(8,128)S(1)} custom-call(s32[3]{0:T(128)S(1)} %pad_add_fusion.1.order_ref, bf16[1024,128]{1,0:T(8,128)(2,1)S(1)} %copy-done.17, bf16[1024,128]{1,0:T(8,128)(2,1)S(1)} %copy-done.31, bf16[1024,128]{1,0:T(8,128)(2,1)} %collective-permute-done.1.refs_2_, bf16[1024,128]{1,0:T(8,128)(2,1)S(1)} %copy-done.9, ...), custom_call_target="tpu_custom_call" | custom-call | flops 268435456 | bytes 3145728 | tf_op jit(solution)/shard_map/attention/pallas_call | solution.py:79
  108.6 2.8 %collective-permute-start.15 = (bf16[128,1024]{1,0:T(8,128)(2,1)S(1)}, bf16[128,1024]{1,0:T(8,128)(2,1)S(1)}, u32[]{:S(2)}, u32[]{:S(2)}) collective-permute-start(bf16[128,1024]{1,0:T(8,128)(2,1)S(1)} %get-tuple-element.14), channel_id=1, source_target_pairs={{0,7},{1,0},{2,1},{3,2},{4,3},{5,4},{6,5},{7,6},{8,15},{9,8},{10,9... | collective-permute-start | bytes 786440 | tf_op jit(solution)/shard_map/ppermute | solution.py:287
  111.5 2.5 %attention.5 = (f32[128,1024]{1,0:T(8,128)S(1)}, f32[128,1024]{1,0:T(8,128)S(1)}) custom-call(s32[2]{0:T(128)S(1)} %get-tuple-element.24.order_ref, bf16[1024,128]{1,0:T(8,128)(2,1)S(1)} %copy-done.18, bf16[1024,128]{1,0:T(8,128)(2,1)S(1)} %copy-done.32, bf16[1024,128]{1,0:T(8,128)(2,1)} %collective-permute-done.1.refs_2_, bf16[1024,128]{1,0:T(8,128)(2,1)S(1)} %copy-done.10, ...), custom_call_target="tpu_custom_call" | custom-call | flops 134217728 | bytes 3145728 | tf_op jit(solution)/shard_map/attention/pallas_call | solution.py:79
  116.5 7.0 %collective-permute-done.16.pair_ref = bf16[128,1024]{1,0:T(8,128)(2,1)S(1)} collective-permute-done((bf16[128,1024]{1,0:T(8,128)(2,1)S(1)}, bf16[128,1024]{1,0:T(8,128)(2,1)S(1)}, u32[]{:S(2)}, u32[]{:S(2)}) %collective-permute-start.16) | collective-permute-done | bytes 262176 | tf_op jit(solution)/shard_map/ppermute | solution.py:290
  129.3 11.5 %feed.1 = (f32[128,1024]{1,0:T(8,128)S(1)}, bf16[128,1024]{1,0:T(8,128)(2,1)}) custom-call(bf16[128,1024]{1,0:T(8,128)(2,1)S(1)} %copy-done.36, bf16[128,1024]{1,0:T(8,128)(2,1)S(1)} %copy-done.38, bf16[1024,1024]{1,0:T(8,128)(2,1)S(1)} %copy-done.33, bf16[1024,1024]{1,0:T(8,128)(2,1)S(1)} %copy-done.34, bf16[32,3,64,1024]{3,2,1,0:T(8,128)(2,1)} %bitcast.16, ...), custom_call_target="tpu_custom_call" | custom-call | flops 4294967296 | bytes 16777216 | tf_op jit(solution)/shard_map/feed/pallas_call | solution.py:147
  141.2 5.0 %collective-permute-done.20.pair_ref = bf16[128,1024]{1,0:T(8,128)(2,1)S(1)} collective-permute-done((bf16[128,1024]{1,0:T(8,128)(2,1)}, bf16[128,1024]{1,0:T(8,128)(2,1)S(1)}, u32[]{:S(2)}, u32[]{:S(2)}) %collective-permute-start.20) | collective-permute-done | bytes 262176 | tf_op jit(solution)/shard_map/ppermute | solution.py:290
  147.5 4.2 %all-to-all-start = ((f32[8,8,1024]{2,1,0:T(8,128)}), f32[8,8,1024]{2,1,0:T(8,128)S(1)}, u32[]{:S(2)}, u32[]{:S(2)}) async-start(f32[8,8,1024]{2,1,0:T(8,128)} %pool.1), calls=%async_computation | async-start | bytes 524288 | tf_op jit(solution)/shard_map/all_to_all | solution.py:359
  152.0 9.0 %all-to-all-done.pooled_ref = f32[8,8,1024]{2,1,0:T(8,128)S(1)} async-done(((f32[8,8,1024]{2,1,0:T(8,128)}), f32[8,8,1024]{2,1,0:T(8,128)S(1)}, u32[]{:S(2)}, u32[]{:S(2)}) %all-to-all-start) | async-done | bytes 262176 | tf_op jit(solution)/shard_map/all_to_all | solution.py:359
  161.1 3.2 %moments.1 = bf16[256,1024]{1,0:T(8,128)(2,1)} custom-call(s32[1]{0:T(128)} %bitcast.1.sub_ref, f32[8,8,1024]{2,1,0:T(8,128)S(1)} %all-to-all-done.pooled_ref, bf16[1024,128]{1,0:T(8,128)(2,1)S(1)} %constant_dynamic-slice_fusion.proj_ref, s32[1,64]{1,0:T(1,128)S(1)} %add.175.code_ref), custom_call_target="tpu_custom_call" | custom-call | flops 1048576 | bytes 1048576 | tf_op jit(solution)/shard_map/moments/pallas_call | solution.py:260
  164.3 17.2 %all-to-all-start.1 = ((bf16[32,8,1024]{2,1,0:T(8,128)(2,1)}), bf16[32,8,1024]{2,1,0:T(8,128)(2,1)S(1)}, u32[]{:S(2)}, u32[]{:S(2)}) async-start(bf16[32,8,1024]{2,1,0:T(8,128)(2,1)} %bitcast.12), calls=%async_computation.1 | async-start | bytes 1048576 | tf_op jit(solution)/shard_map/all_to_all | solution.py:369
  181.5 11.5 %all-to-all-done.1 = bf16[32,8,1024]{2,1,0:T(8,128)(2,1)S(1)} async-done(((bf16[32,8,1024]{2,1,0:T(8,128)(2,1)}), bf16[32,8,1024]{2,1,0:T(8,128)(2,1)S(1)}, u32[]{:S(2)}, u32[]{:S(2)}) %all-to-all-start.1) | async-done | bytes 524320 | tf_op jit(solution)/shard_map/all_to_all | solution.py:369
  (160 shorter events, 58.5 us)
Async XLA Ops:
  7.2 117.0 %all-gather.2.cloned.1.call-start = ((), (), s32[]{:S(2)}) async-start(), calls=%async_computation.2 | async-start | bytes 12976128 | tf_op jit(solution)/shard_map/all_gather | solution.py:329
  8.3 10.2 %collective-permute-start.19 = (bf16[64,1024]{1,0:T(8,128)(2,1)S(1)}, bf16[64,1024]{1,0:T(8,128)(2,1)S(1)}, u32[]{:S(2)}, u32[]{:S(2)}) collective-permute-start(bf16[64,1024]{1,0:T(8,128)(2,1)S(1)} %pad_maximum_fusion.3), channel_id=1, source_target_pairs={{0,6},{1,7},{2,0},{3,1},{4,2},{5,3},{6,4},{7,5},{8,14},{9,15},{10,... | collective-permute-start | bytes 393224 | tf_op jit(solution)/shard_map/ppermute | solution.py:287
  15.2 11.1 %collective-permute-start.18 = (bf16[64,1024]{1,0:T(8,128)(2,1)S(1)}, bf16[64,1024]{1,0:T(8,128)(2,1)S(1)}, u32[]{:S(2)}, u32[]{:S(2)}) collective-permute-start(bf16[64,1024]{1,0:T(8,128)(2,1)S(1)} %pad_maximum_fusion.3), channel_id=1, source_target_pairs={{0,4},{1,5},{2,6},{3,7},{4,0},{5,1},{6,2},{7,3},{8,12},{9,13},{10,... | collective-permute-start | bytes 393224 | tf_op jit(solution)/shard_map/ppermute | solution.py:287
  16.2 10.3 %collective-permute-start.17 = (bf16[64,1024]{1,0:T(8,128)(2,1)S(1)}, bf16[64,1024]{1,0:T(8,128)(2,1)S(1)}, u32[]{:S(2)}, u32[]{:S(2)}) collective-permute-start(bf16[64,1024]{1,0:T(8,128)(2,1)S(1)} %pad_maximum_fusion.3), channel_id=1, source_target_pairs={{0,2},{1,3},{2,4},{3,5},{4,6},{5,7},{6,0},{7,1},{8,10},{9,11},{10,... | collective-permute-start | bytes 393224 | tf_op jit(solution)/shard_map/ppermute | solution.py:287
  27.3 11.8 %collective-permute-start.3 = (bf16[1024,128]{1,0:T(8,128)(2,1)}, bf16[1024,128]{1,0:T(8,128)(2,1)S(1)}, u32[]{:S(2)}, u32[]{:S(2)}) collective-permute-start(bf16[1024,128]{1,0:T(8,128)(2,1)} %refs_0_.9), channel_id=1, source_target_pairs={{0,1},{1,2},{2,3},{3,4},{4,5},{5,6},{6,7},{7,0},{8,9},{9,10},{10,1... | collective-permute-start | bytes 786440 | tf_op jit(solution)/shard_map/ppermute | solution.py:287
  30.5 9.3 %collective-permute-start = (bf16[1024,128]{1,0:T(8,128)(2,1)}, bf16[1024,128]{1,0:T(8,128)(2,1)S(1)}, u32[]{:S(2)}, u32[]{:S(2)}) collective-permute-start(bf16[1024,128]{1,0:T(8,128)(2,1)} %refs_0_.9), channel_id=1, source_target_pairs={{0,7},{1,0},{2,1},{3,2},{4,3},{5,4},{6,5},{7,6},{8,15},{9,8},{10,9... | collective-permute-start | bytes 786440 | tf_op jit(solution)/shard_map/ppermute | solution.py:287
  39.1 7.5 %collective-permute-start.4 = (bf16[1024,128]{1,0:T(8,128)(2,1)S(1)}, bf16[1024,128]{1,0:T(8,128)(2,1)}, u32[]{:S(2)}, u32[]{:S(2)}) collective-permute-start(bf16[1024,128]{1,0:T(8,128)(2,1)S(1)} %collective-permute-done.3.refs_5_), channel_id=1, source_target_pairs={{0,1},{1,2},{2,3},{3,4},{4,5},{5,6},{6,7},{7,0},{8,9},{9,10},{10,1... | collective-permute-start | bytes 786440 | tf_op jit(solution)/shard_map/ppermute | solution.py:287
  39.8 7.8 %collective-permute-start.1 = (bf16[1024,128]{1,0:T(8,128)(2,1)S(1)}, bf16[1024,128]{1,0:T(8,128)(2,1)}, u32[]{:S(2)}, u32[]{:S(2)}) collective-permute-start(bf16[1024,128]{1,0:T(8,128)(2,1)S(1)} %collective-permute-done.refs_1_), channel_id=1, source_target_pairs={{0,7},{1,0},{2,1},{3,2},{4,3},{5,4},{6,5},{7,6},{8,15},{9,8},{10,9... | collective-permute-start | bytes 786440 | tf_op jit(solution)/shard_map/ppermute | solution.py:287
  46.6 7.0 %collective-permute-start.5 = (bf16[1024,128]{1,0:T(8,128)(2,1)}, bf16[1024,128]{1,0:T(8,128)(2,1)S(1)}, u32[]{:S(2)}, u32[]{:S(2)}) collective-permute-start(bf16[1024,128]{1,0:T(8,128)(2,1)} %collective-permute-done.4.refs_6_), channel_id=1, source_target_pairs={{0,1},{1,2},{2,3},{3,4},{4,5},{5,6},{6,7},{7,0},{8,9},{9,10},{10,1... | collective-permute-start | bytes 786440 | tf_op jit(solution)/shard_map/ppermute | solution.py:287
  47.6 6.8 %collective-permute-start.2 = (bf16[1024,128]{1,0:T(8,128)(2,1)}, bf16[1024,128]{1,0:T(8,128)(2,1)S(1)}, u32[]{:S(2)}, u32[]{:S(2)}) collective-permute-start(bf16[1024,128]{1,0:T(8,128)(2,1)} %collective-permute-done.1.refs_2_), channel_id=1, source_target_pairs={{0,7},{1,0},{2,1},{3,2},{4,3},{5,4},{6,5},{7,6},{8,15},{9,8},{10,9... | collective-permute-start | bytes 786440 | tf_op jit(solution)/shard_map/ppermute | solution.py:287
  54.4 5.3 %collective-permute-start.6 = (bf16[512,128]{1,0:T(8,128)(2,1)}, bf16[512,128]{1,0:T(8,128)(2,1)}, u32[]{:S(2)}, u32[]{:S(2)}) collective-permute-start(bf16[512,128]{1,0:T(8,128)(2,1)} %slice.56), channel_id=1, source_target_pairs={{0,1},{1,2},{2,3},{3,4},{4,5},{5,6},{6,7},{7,0},{8,9},{9,10},{10,1... | collective-permute-start | bytes 393224 | tf_op jit(solution)/shard_map/ppermute | solution.py:287
  55.1 5.5 %collective-permute-start.7 = (bf16[512,128]{1,0:T(8,128)(2,1)}, bf16[512,128]{1,0:T(8,128)(2,1)}, u32[]{:S(2)}, u32[]{:S(2)}) collective-permute-start(bf16[512,128]{1,0:T(8,128)(2,1)} %slice.57), channel_id=1, source_target_pairs={{0,7},{1,0},{2,1},{3,2},{4,3},{5,4},{6,5},{7,6},{8,15},{9,8},{10,9... | collective-permute-start | bytes 393224 | tf_op jit(solution)/shard_map/ppermute | solution.py:287
  70.0 6.9 %collective-permute-start.12 = (bf16[64,1024]{1,0:T(8,128)(2,1)S(1)}, bf16[64,1024]{1,0:T(8,128)(2,1)S(1)}, u32[]{:S(2)}, u32[]{:S(2)}) collective-permute-start(bf16[64,1024]{1,0:T(8,128)(2,1)S(1)} %get-tuple-element.22), channel_id=1, source_target_pairs={{0,7},{1,0},{2,1},{3,2},{4,3},{5,4},{6,5},{7,6},{8,15},{9,8},{10,9... | collective-permute-start | bytes 393224 | tf_op jit(solution)/shard_map/ppermute | solution.py:287
  72.9 5.4 %collective-permute-start.8 = (bf16[64,1024]{1,0:T(8,128)(2,1)S(1)}, bf16[64,1024]{1,0:T(8,128)(2,1)S(1)}, u32[]{:S(2)}, u32[]{:S(2)}) collective-permute-start(bf16[64,1024]{1,0:T(8,128)(2,1)S(1)} %get-tuple-element.23), channel_id=1, source_target_pairs={{0,1},{1,2},{2,3},{3,4},{4,5},{5,6},{6,7},{7,0},{8,9},{9,10},{10,1... | collective-permute-start | bytes 393224 | tf_op jit(solution)/shard_map/ppermute | solution.py:287
  79.1 12.8 %collective-permute-start.13 = (bf16[128,1024]{1,0:T(8,128)(2,1)}, bf16[128,1024]{1,0:T(8,128)(2,1)}, u32[]{:S(2)}, u32[]{:S(2)}) collective-permute-start(bf16[128,1024]{1,0:T(8,128)(2,1)} %pad_maximum_fusion.2), channel_id=1, source_target_pairs={{0,7},{1,0},{2,1},{3,2},{4,3},{5,4},{6,5},{7,6},{8,15},{9,8},{10,9... | collective-permute-start | bytes 786440 | tf_op jit(solution)/shard_map/ppermute | solution.py:287
  81.1 10.9 %collective-permute-start.9 = (bf16[128,1024]{1,0:T(8,128)(2,1)}, bf16[128,1024]{1,0:T(8,128)(2,1)}, u32[]{:S(2)}, u32[]{:S(2)}) collective-permute-start(bf16[128,1024]{1,0:T(8,128)(2,1)} %pad_maximum_fusion.1), channel_id=1, source_target_pairs={{0,1},{1,2},{2,3},{3,4},{4,5},{5,6},{6,7},{7,0},{8,9},{9,10},{10,1... | collective-permute-start | bytes 786440 | tf_op jit(solution)/shard_map/ppermute | solution.py:287
  94.0 13.2 %collective-permute-start.14 = (bf16[128,1024]{1,0:T(8,128)(2,1)}, bf16[128,1024]{1,0:T(8,128)(2,1)}, u32[]{:S(2)}, u32[]{:S(2)}) collective-permute-start(bf16[128,1024]{1,0:T(8,128)(2,1)} %get-tuple-element.16), channel_id=1, source_target_pairs={{0,7},{1,0},{2,1},{3,2},{4,3},{5,4},{6,5},{7,6},{8,15},{9,8},{10,9... | collective-permute-start | bytes 786440 | tf_op jit(solution)/shard_map/ppermute | solution.py:287
  96.5 10.7 %collective-permute-start.10 = (bf16[128,1024]{1,0:T(8,128)(2,1)}, bf16[128,1024]{1,0:T(8,128)(2,1)}, u32[]{:S(2)}, u32[]{:S(2)}) collective-permute-start(bf16[128,1024]{1,0:T(8,128)(2,1)} %get-tuple-element.17), channel_id=1, source_target_pairs={{0,1},{1,2},{2,3},{3,4},{4,5},{5,6},{6,7},{7,0},{8,9},{9,10},{10,1... | collective-permute-start | bytes 786440 | tf_op jit(solution)/shard_map/ppermute | solution.py:287
  108.5 6.6 %collective-permute-start.11 = (bf16[128,1024]{1,0:T(8,128)(2,1)S(1)}, bf16[128,1024]{1,0:T(8,128)(2,1)S(1)}, u32[]{:S(2)}, u32[]{:S(2)}) collective-permute-start(bf16[128,1024]{1,0:T(8,128)(2,1)S(1)} %get-tuple-element.15), channel_id=1, source_target_pairs={{0,1},{1,2},{2,3},{3,4},{4,5},{5,6},{6,7},{7,0},{8,9},{9,10},{10,1... | collective-permute-start | bytes 786440 | tf_op jit(solution)/shard_map/ppermute | solution.py:287
  108.6 6.5 %collective-permute-start.15 = (bf16[128,1024]{1,0:T(8,128)(2,1)S(1)}, bf16[128,1024]{1,0:T(8,128)(2,1)S(1)}, u32[]{:S(2)}, u32[]{:S(2)}) collective-permute-start(bf16[128,1024]{1,0:T(8,128)(2,1)S(1)} %get-tuple-element.14), channel_id=1, source_target_pairs={{0,7},{1,0},{2,1},{3,2},{4,3},{5,4},{6,5},{7,6},{8,15},{9,8},{10,9... | collective-permute-start | bytes 786440 | tf_op jit(solution)/shard_map/ppermute | solution.py:287
  115.4 8.1 %collective-permute-start.16 = (bf16[128,1024]{1,0:T(8,128)(2,1)S(1)}, bf16[128,1024]{1,0:T(8,128)(2,1)S(1)}, u32[]{:S(2)}, u32[]{:S(2)}) collective-permute-start(bf16[128,1024]{1,0:T(8,128)(2,1)S(1)} %get-tuple-element.11.own_ref), channel_id=1, source_target_pairs={{0,1},{1,0},{2,3},{3,2},{4,5},{5,4},{6,7},{7,6},{8,9},{9,8},{10,11... | collective-permute-start | bytes 786440 | tf_op jit(solution)/shard_map/ppermute | solution.py:290
  140.8 5.4 %collective-permute-start.20 = (bf16[128,1024]{1,0:T(8,128)(2,1)}, bf16[128,1024]{1,0:T(8,128)(2,1)S(1)}, u32[]{:S(2)}, u32[]{:S(2)}) collective-permute-start(bf16[128,1024]{1,0:T(8,128)(2,1)} %get-tuple-element.13), channel_id=1, source_target_pairs={{0,1},{1,0},{2,3},{3,2},{4,5},{5,4},{6,7},{7,6},{8,9},{9,8},{10,11... | collective-permute-start | bytes 786440 | tf_op jit(solution)/shard_map/ppermute | solution.py:290
  147.5 13.6 %all-to-all-start = ((f32[8,8,1024]{2,1,0:T(8,128)}), f32[8,8,1024]{2,1,0:T(8,128)S(1)}, u32[]{:S(2)}, u32[]{:S(2)}) async-start(f32[8,8,1024]{2,1,0:T(8,128)} %pool.1), calls=%async_computation | async-start | bytes 524288 | tf_op jit(solution)/shard_map/all_to_all | solution.py:359
  164.3 28.7 %all-to-all-start.1 = ((bf16[32,8,1024]{2,1,0:T(8,128)(2,1)}), bf16[32,8,1024]{2,1,0:T(8,128)(2,1)S(1)}, u32[]{:S(2)}, u32[]{:S(2)}) async-start(bf16[32,8,1024]{2,1,0:T(8,128)(2,1)} %bitcast.12), calls=%async_computation.1 | async-start | bytes 1048576 | tf_op jit(solution)/shard_map/all_to_all | solution.py:369
  (42 other events, 254.9 us)
Sparse Core Ops, SparseCore 0:
  27.4 71.8 all-gather.1

commit v3 on v2

v3 whole, which is shorter than its diff:
```python
import functools
import math

import jax
import jax.numpy as jnp
from jax import lax
from jax.experimental import pallas as pl
from jax.experimental.pallas import tpu as pltpu
from jax.sharding import PartitionSpec as P

HDIM = 64
SUBW = 64
LANES = 128
SLOTS = 2
KINDS = 4
PACK = 8

epsilon = 1e-05
BF = jnp.bfloat16
F32 = jnp.float32
HIGH = lax.Precision.HIGHEST


def normalize(rows):
    center = jnp.mean(rows, axis=-1, keepdims=True)
    shifted = rows - center
    spread = jnp.mean(shifted * shifted, axis=-1, keepdims=True)
    return shifted * lax.rsqrt(spread + epsilon)


def dot(a, b, dims=((1,), (0,)), precision=None):
    return lax.dot_general(a, b, (dims, ((), ())), precision=precision, preferred_element_type=F32)


def split(array):
    high = array.astype(BF)
    return high, (array - high.astype(F32)).astype(BF)


def cost(flops, size):
    return pl.CostEstimate(flops=flops, bytes_accessed=size, transcendentals=0)


def attention_kernel(offsets, parts, chunk, with_base, me_ref, ends_ref, *refs):
    pieces, (w_ref, wo_ref), (out_ref, rows_ref, sems) = refs[:parts + 1], refs[parts + 1:parts + 3], refs[parts + 3:]
    me = me_ref[0]
    half = parts // 2
    part = pieces[0].shape[1]
    chunks = [lax.rem(me + (off + parts), parts) for off in offsets]

    def slot(i, away):
        at = lax.rem(me + (away + parts), parts)
        return rows_ref.at[i, :, pl.ds(pl.multiple_of(at * part, part), part)]

    def fetch(source, start, i, away, number):
        start = pl.multiple_of(start, chunk)
        return pltpu.make_async_copy(source.at[pl.ds(start, chunk), :], slot(i, away), sems.at[i, number])

    for i, c in enumerate(chunks):
        for k in range(half):
            fetch(pieces[k], c * chunk, i, k, k).start()
        for k in range(1, half):
            fetch(pieces[half + 1 + k], c * chunk, i, -k, half + k).start()

        @pl.when(c < half)
        def _():
            fetch(pieces[half], c * chunk, i, half, half).start()

        @pl.when(c >= half)
        def _():
            fetch(pieces[half + 1], (c - half) * chunk, i, half, half).start()

    for i, c in enumerate(chunks):
        for k in range(half):
            fetch(pieces[k], c * chunk, i, k, k).wait()
        for k in range(1, half):
            fetch(pieces[half + 1 + k], c * chunk, i, -k, half + k).wait()
        fetch(pieces[half], 0, i, half, half).wait()
    count = len(offsets)
    rows = rows_ref[...].reshape(count * chunk, -1).astype(F32)
    normed = normalize(rows).astype(BF)
    projected = dot(normed, w_ref[...]).astype(BF)
    local = wo_ref.shape[0]
    block_rows = chunk * parts // ends_ref.shape[0]
    blocks = chunk // block_rows
    per_block = ends_ref.shape[1]

    def keys(c, shape, axis):
        row = lax.broadcasted_iota(jnp.int32, shape, axis)
        block = row // block_rows
        key = block * per_block
        for b in range(blocks):
            for e in range(per_block - 1):
                end = ends_ref[c * blocks + b, e] + b * block_rows
                key = key + jnp.where((block == b) & (row >= end), 1, 0)
        return key

    lines = []
    for i, c in enumerate(chunks):
        mine = projected[i * chunk:(i + 1) * chunk]
        matches = keys(c, (chunk, 1), 0) == keys(c, (1, chunk), 1)
        heads = []
        for h in range(local // HDIM):
            query, key, value = (
                mine[:, t * local + h * HDIM:t * local + (h + 1) * HDIM] for t in range(3)
            )
            scores = dot(query, key, ((1,), (1,))) / math.sqrt(HDIM)
            raised = jnp.where(matches, jnp.exp(scores), 0.0)
            weights = (raised / jnp.sum(raised, axis=-1, keepdims=True)).astype(BF)
            heads.append(dot(weights, value).astype(BF))
        lines.append(jnp.concatenate(heads, axis=-1))
    context = jnp.concatenate(lines, axis=0)
    if with_base:
        out_ref[...] = rows + dot(context, wo_ref[...])
    else:
        out_ref[...] = context


def attention(pieces, w_qkv, w_out, ends, me, offsets, with_base=False):
    parts = len(pieces) - 1
    count, part = pieces[0].shape
    chunk = count // parts
    local, width = w_out.shape
    size = len(offsets)
    smem = pl.BlockSpec(memory_space=pltpu.SMEM)
    vmem = pl.BlockSpec(memory_space=pltpu.VMEM)
    hbm = pl.BlockSpec(memory_space=pltpu.HBM)
    pieces = [pltpu.with_memory_space_constraint(p, pltpu.HBM) for p in pieces]
    return pl.pallas_call(
        functools.partial(attention_kernel, offsets, parts, chunk, with_base),
        in_specs=[smem, smem] + [hbm] * len(pieces) + [vmem] * 2,
        out_specs=vmem,
        out_shape=jax.ShapeDtypeStruct((size * chunk, width if with_base else local), F32 if with_base else BF),
        scratch_shapes=[pltpu.VMEM((size, chunk, width), BF), pltpu.SemaphoreType.DMA((size, parts))],
        compiler_params=pltpu.CompilerParams(vmem_limit_bytes=16 << 20),
        cost_estimate=cost(size * 2 * chunk * width * 4 * local, 3 << 20),
        name="attention",
    )(me, ends, *pieces, w_qkv, w_out)


def first_join_kernel(context_ref, wo_ref, right_ref, left_ref):
    half = right_ref.shape[0]
    sums = dot(context_ref[...], wo_ref[...]).astype(BF)
    right_ref[...] = sums[:half]
    left_ref[...] = sums[half:]


def join_kernel(context_ref, wo_ref, right_ref, left_ref, right_out, left_out):
    chunk = right_out.shape[0]
    sums = dot(context_ref[...], wo_ref[...])
    ahead, back = sums[:chunk], sums[chunk:]
    half = right_ref.shape[0]
    right_out[:half] = (ahead[:half] + right_ref[...].astype(F32)).astype(BF)
    left_out[chunk - half:] = (back[chunk - half:] + left_ref[...].astype(F32)).astype(BF)
    if half < chunk:
        right_out[half:] = ahead[half:].astype(BF)
        left_out[:chunk - half] = back[:chunk - half].astype(BF)


def middle_kernel(base_ref, right_ref, left_ref, hidden_ref, normed_ref):
    hidden = base_ref[...] + (right_ref[...].astype(F32) + left_ref[...].astype(F32))
    hidden_ref[...] = hidden
    normed_ref[...] = normalize(hidden).astype(BF)


def feed_kernel(own_ref, pair_ref, hidden_ref, up_ref, down_ref, gathered_ref, out_ref, send_ref, ups, downs, sems):
    count = own_ref.shape[0]
    planes = gathered_ref.shape[1]
    rows = gathered_ref.shape[2] // 2
    copies = [(pltpu.make_async_copy(up_ref, ups.at[0], sems.at[0, 0]),
               pltpu.make_async_copy(down_ref, downs.at[0], sems.at[0, 1]))]
    spread = gathered_ref.shape[0]
    for p in range(planes):
        copies.append(tuple(
            pltpu.make_async_copy(
                gathered_ref.at[:, p, t * rows:(t + 1) * rows, :],
                into.at[p + 1].reshape(spread, rows, into.shape[-1]),
                sems.at[p + 1, t],
            )
            for t, into in enumerate((ups, downs))
        ))
    for up, down in copies:
        up.start()
        down.start()
    both = jnp.concatenate([own_ref[...], pair_ref[...]], axis=0)
    total = None
    for p, (up, down) in enumerate(copies):
        up.wait()
        inner = jnp.maximum(dot(both, ups[p]), 0.0).astype(BF)
        down.wait()
        part = dot(inner, downs[p])
        total = part if total is None else total + part
    out_ref[...] = hidden_ref[...] + total[:count]
    send_ref[...] = total[count:].astype(BF)


def feed(own, pair, hidden1, w_up, w_down, gathered):
    planes = gathered.shape[1]
    count, width = own.shape
    hidden = w_up.shape[1]
    vmem = pl.BlockSpec(memory_space=pltpu.VMEM)
    hbm = pl.BlockSpec(memory_space=pltpu.HBM)
    w_up, w_down, gathered = (
        pltpu.with_memory_space_constraint(w, pltpu.HBM) for w in (w_up, w_down, gathered)
    )
    return pl.pallas_call(
        feed_kernel,
        in_specs=[vmem, vmem, vmem, hbm, hbm, hbm],
        out_specs=[vmem, vmem],
        out_shape=[jax.ShapeDtypeStruct(own.shape, F32), jax.ShapeDtypeStruct(own.shape, BF)],
        scratch_shapes=[
            pltpu.VMEM((planes + 1,) + w_up.shape, BF),
            pltpu.VMEM((planes + 1,) + w_down.shape, BF),
            pltpu.SemaphoreType.DMA((planes + 1, 2)),
        ],
        compiler_params=pltpu.CompilerParams(vmem_limit_bytes=24 << 20),
        cost_estimate=cost(8 * count * width * hidden * (planes + 1), 4 * (planes + 1) * width * hidden),
        name="feed",
    )(own, pair, hidden1, w_up, w_down, gathered)


def pool_kernel(hidden_ref, pair_ref, gain_ref, member_ref, length_ref, out_ref):
    hidden = hidden_ref[...] + pair_ref[...].astype(F32)
    finished = normalize(hidden) * gain_ref[...]
    pooled = dot(member_ref[...], finished, precision=HIGH) / length_ref[...]
    out_ref[...] = jnp.broadcast_to(pooled[None], out_ref.shape)


def moments_kernel(sub_ref, pooled_ref, proj_ref, code_ref, out_ref):
    me = sub_ref[0]
    parts, few, width = pooled_ref.shape
    sentences = parts * few
    pooled = pooled_ref[...].reshape(sentences, width)
    total = out_ref.shape[0]
    groups = total // PACK
    per_group = width // groups
    own = per_group // parts
    mean = jnp.mean(pooled, axis=0, keepdims=True)
    centred = pooled - mean
    feature = lax.broadcasted_iota(jnp.int32, (width, total), 0)
    wanted = lax.broadcasted_iota(jnp.int32, (width, total), 1)
    chosen = (wanted // PACK) * per_group + me * own + wanted % PACK
    pick = jnp.where((feature == chosen) & (wanted % PACK < own), 1.0, 0.0).astype(BF)
    large, small = split(centred)
    picked_large, picked_small = dot(large, pick).astype(BF), dot(small, pick).astype(BF)
    first = ((0,), (0,))
    moments = dot(picked_large, large, first) + (dot(picked_large, small, first) + dot(picked_small, large, first))
    rotated = dot(large, proj_ref[...]).astype(BF)
    lanes = rotated.shape[1]
    row = lax.broadcasted_iota(jnp.int32, (total, sentences), 0)
    pieces = []
    flags = []
    ones = jnp.ones((sentences, lanes), BF)
    for k in range(KINDS):
        place = (row % PACK == own + 2) & ((row // PACK) * KINDS + k == code_ref[...])
        place = jnp.where(place, 1.0, 0.0).astype(BF)
        pieces.append(dot(place, rotated))
        flags.append(dot(place, ones))
    sides = jnp.concatenate(pieces + flags, axis=-1)
    high = mean.astype(BF).astype(F32)
    low = mean - high
    line = lax.broadcasted_iota(jnp.int32, (total, 1), 0) % PACK
    means = jnp.where(line == own, high, 0.0) + jnp.where(line == own + 1, low, 0.0)
    out_ref[...] = (moments + means + sides).astype(BF)


def combine_kernel(where_ref, recv_ref, proj_ref, pq_ref, cov_ref):
    first = where_ref[0]
    own, width = cov_ref.shape
    recv = recv_ref[...]
    total = recv.shape[0]
    groups = total // PACK
    sentences = pq_ref.shape[1]
    count = float(groups * sentences)
    source = lax.broadcasted_iota(jnp.int32, (groups, total), 0)
    line = lax.broadcasted_iota(jnp.int32, (groups, total), 1)
    pick_mean = (line == source * PACK + own) | (line == source * PACK + own + 1)
    means = dot(jnp.where(pick_mean, 1.0, 0.0).astype(BF), recv)
    sides = dot(jnp.where(line == source * PACK + own + 2, 1.0, 0.0).astype(BF), recv)
    line = lax.broadcasted_iota(jnp.int32, (PACK, total), 1) % PACK
    within = dot(jnp.where(line == lax.broadcasted_iota(jnp.int32, (PACK, total), 0), 1.0, 0.0).astype(BF), recv)
    away = means - jnp.mean(means, axis=0, keepdims=True)
    feature = lax.broadcasted_iota(jnp.int32, (width, LANES), 0)
    lane = lax.broadcasted_iota(jnp.int32, (width, LANES), 1)
    pick = jnp.where((feature == first + lane) & (lane < own), 1.0, 0.0).astype(BF)
    large, small = split(away)
    picked_large, picked_small = dot(large, pick).astype(BF), dot(small, pick).astype(BF)
    rows = ((0,), (0,))
    between = dot(picked_large, large, rows) + (dot(picked_large, small, rows) + dot(picked_small, large, rows))
    cov_ref[...] = (within[:own] + float(sentences) * between[:own]) / count
    shift = dot(large, proj_ref[...]) + dot(small, proj_ref[...])
    shift_large, shift_small = split(shift)
    lanes = shift.shape[1]
    one = lax.broadcasted_iota(jnp.int32, (groups, groups), 0)
    other = lax.broadcasted_iota(jnp.int32, (groups, groups), 1)
    ahead = jnp.where(one < other, 1.0, 0.0).astype(BF)
    same = jnp.where(one == other, 1.0, 0.0).astype(BF)
    filled = [sides[:, (KINDS + 2 * c) * lanes:(KINDS + 2 * c + 1) * lanes] for c in range(SLOTS)]
    flat = [dot(f.astype(BF), same, ((0,), (0,)))[:1] for f in filled]
    before = dot((filled[0] + filled[1]).astype(BF), ahead, ((0,), (0,)))[:1]
    place = lax.broadcasted_iota(jnp.int32, (sentences, groups), 0)
    result = jnp.zeros((sentences, lanes), F32)
    for c in range(SLOTS):
        for k in range(2):
            rows = sides[:, (2 * c + k) * lanes:(2 * c + k + 1) * lanes].astype(BF)
            position = (2.0 * before + float(k)).astype(jnp.int32)
            chosen = jnp.where((place == position) & (flat[c] > 0.5), 1.0, 0.0).astype(BF)
            result = result + (dot(chosen, rows) + (dot(chosen, shift_large) + dot(chosen, shift_small)))
        before = before + flat[c]
    for q in range(pq_ref.shape[0]):
        pq_ref[q] = result[:, q * SUBW:(q + 1) * SUBW]


def small_call(kernel, outs, args, scalar=None, name=None):
    specs = [pl.BlockSpec(memory_space=pltpu.VMEM) for _ in args]
    if scalar is not None:
        specs = [pl.BlockSpec(memory_space=pltpu.SMEM)] + specs
        args = (scalar,) + tuple(args)
    single = not isinstance(outs, (tuple, list))
    return pl.pallas_call(
        kernel,
        in_specs=specs,
        out_specs=pl.BlockSpec(memory_space=pltpu.VMEM) if single else [pl.BlockSpec(memory_space=pltpu.VMEM) for _ in outs],
        out_shape=outs,
        compiler_params=pltpu.CompilerParams(vmem_limit_bytes=16 << 20),
        cost_estimate=cost(1 << 20, 1 << 20),
        name=name,
    )(*args)


def on_device(
    tokens, lengths, dest, w_query, w_key, w_value, w_out, w_up, w_down, final_gain, projection
):
    dp_count = lax.axis_size("dp")
    sub_count = lax.axis_size("sub")
    dp_at = lax.axis_index("dp")
    sub_at = lax.axis_index("sub")
    block_count, per_block = lengths.shape
    local_rows, local_width = tokens.shape
    block_rows = local_rows // block_count
    width = local_width * sub_count
    own_blocks = block_count // sub_count
    own_rows = own_blocks * block_rows
    half = sub_count // 2

    def move(array, by):
        return lax.ppermute(array, "sub", [(i, (i + by) % sub_count) for i in range(sub_count)])

    def swap(array):
        return lax.ppermute(array, "sub", [(i, i ^ 1) for i in range(sub_count)])

    rows = w_up.shape[0] // dp_count
    piece = jnp.concatenate(
        [lax.dynamic_slice_in_dim(w, dp_at * rows, rows, 0) for w in (w_up, w_down)], axis=0
    )
    piece, tokens = lax.optimization_barrier((piece, tokens))
    others = [move(piece, by) for by in range(2, sub_count, 2)]
    planes = half - 1

    ends = jnp.cumsum(lengths, axis=-1)
    position = jnp.arange(block_rows, dtype=jnp.int32)
    segment = jnp.sum((ends[:, None, :] <= position[None, :, None]).astype(jnp.int32), axis=-1)
    ordinal = jnp.arange(block_count, dtype=jnp.int32)
    keys = (ordinal[:, None] * per_block + segment).reshape(local_rows)
    own_lens = lax.dynamic_slice_in_dim(lengths, sub_at * own_blocks, own_blocks, 0)
    own_keys = lax.dynamic_slice_in_dim(keys, sub_at * own_rows, own_rows, 0)
    own_sentences = own_blocks * per_block
    member = (
        own_keys[None, :] == sub_at * own_sentences + jnp.arange(own_sentences, dtype=jnp.int32)[:, None]
    ).astype(F32)
    matches = dest[:, None] == dest[None, :]
    earlier = ordinal[:, None] > ordinal[None, :]
    earlier_count = jnp.sum((matches & earlier).astype(jnp.int32), axis=1)
    code = (dest * SLOTS + earlier_count)[:, None] * per_block + jnp.arange(per_block, dtype=jnp.int32)[None, :]
    code = code.reshape(1, block_count * per_block)
    w_qkv = jnp.concatenate((w_query, w_key, w_value), axis=1)
    columns = width // sub_count
    proj = lax.dynamic_slice_in_dim(projection, sub_at * columns, columns, 1)

    behind, ahead = [], []
    right = left = tokens
    for step in range(half - 1):
        right, left = move(right, 1), move(left, -1)
        if step == 0:
            others = lax.optimization_barrier((others, right, left))[0]
        behind.append(right)
        ahead.append(left)
    middle = local_rows // 2
    far = [move(right[:middle], 1), move(left[middle:], -1)]
    pieces = [tokens] + ahead + far + behind

    gathered = lax.all_gather(jnp.concatenate(others, axis=0), "dp", axis=0, tiled=True)
    gathered = gathered.reshape(dp_count, planes, 2 * rows, width)

    attend = functools.partial(attention, pieces, w_qkv, w_out, ends, sub_at.reshape(1))
    own_shape = (own_rows, width)
    half_shape = (own_rows // 2, width)
    right, left = small_call(
        first_join_kernel,
        [jax.ShapeDtypeStruct(half_shape, BF)] * 2,
        (attend([half]), w_out),
        name="join",
    )
    right, left = move(right, 1), move(left, -1)
    for away in range(half - 1, 0, -1):
        right, left = small_call(
            join_kernel,
            [jax.ShapeDtypeStruct(own_shape, BF)] * 2,
            (attend([away, -away]), w_out, right, left),
            name="join",
        )
        right, left = move(right, 1), move(left, -1)
    base = attend([0], with_base=True)
    hidden1, normed2 = small_call(
        middle_kernel,
        (jax.ShapeDtypeStruct(own_shape, F32), jax.ShapeDtypeStruct(own_shape, BF)),
        (base, right, left),
        name="middle",
    )
    hidden2, sent = feed(normed2, swap(normed2), hidden1, w_up, w_down, gathered)
    pooled = small_call(
        pool_kernel,
        jax.ShapeDtypeStruct((sub_count, own_sentences, width), F32),
        (hidden2, swap(sent), final_gain[None, :], member, own_lens.reshape(own_sentences, 1).astype(F32)),
        name="pool",
    )
    pooled = lax.all_to_all(pooled, "sub", split_axis=0, concat_axis=0, tiled=True)
    sentences = sub_count * own_sentences
    cov_rows = width // (dp_count * sub_count)
    sent = small_call(
        moments_kernel,
        jax.ShapeDtypeStruct((dp_count * PACK, width), BF),
        (pooled, proj, code),
        scalar=sub_at.reshape(1),
        name="moments",
    )
    received = lax.all_to_all(
        sent.reshape(dp_count, PACK, width), "dp", split_axis=0, concat_axis=0, tiled=True
    ).reshape(dp_count * PACK, width)
    return small_call(
        combine_kernel,
        (
            jax.ShapeDtypeStruct((columns // SUBW, sentences, SUBW), F32),
            jax.ShapeDtypeStruct((cov_rows, width), F32),
        ),
        (received, proj),
        scalar=((dp_at * sub_count + sub_at) * cov_rows).reshape(1),
        name="combine",
    )


def solution(mesh):
    in_specs = (
        P("dp", "sub"),
        P("dp", None),
        P("dp"),
        P(None, "sub"),
        P(None, "sub"),
        P(None, "sub"),
        P("sub", None),
        P(None, "sub"),
        P("sub", None),
        P(),
        P(),
    )
    out_specs = (P("sub", "dp", None), P(("dp", "sub"), None))
    return jax.shard_map(
        on_device, mesh=mesh, in_specs=in_specs, out_specs=out_specs, check_vma=False
    )
```

time: 204 us -> 172 us (0.84)
  local copies, waits for them, and re-layouts: 34.8 us -> 10.7 us
  other arithmetic: 7.22 us -> 2.29 us
  waiting for transfers between devices: 54.3 us -> 51.9 us
    unnamed x87 -> x37, local copies, waits for them, and re-layouts: 29.3 us -> 6.73 us
    pallas_call x6, Pallas kernels: 28.2 us -> 24.7 us  [the longest x5 16.4 us: attention(): pl.pallas_call(functools.partial(attention_kernel, offsets, parts, chunk,...]
    convert_element_type x3 -> x0, other arithmetic: 3.32 us -> none  [the longest x2 3.29 us: on_device(): right, left = (move(right.astype(BF), 1), move(left.astype(BF), -1))]
    ppermute x2, starting transfers between devices: 0.1 us -> 3.13 us  [swap(): return lax.ppermute(array, 'sub', [(i, i ^ 1) for i in range(sub_count)])]
    ppermute x2, waiting for transfers between devices: 12 us -> 9.15 us  [swap(): return lax.ppermute(array, 'sub', [(i, i ^ 1) for i in range(sub_count)])]
    all_to_all x1, starting transfers between devices: 17.2 us -> 14.4 us  [on_device(): lax.all_to_all(sent.reshape(dp_count, PACK, width), 'dp', split_axis=0, c...]
    pallas_call x4 -> x8, Pallas kernels: 7.3 us -> 9.95 us  [small_call(): pl.pallas_call(kernel, in_specs=specs, out_specs=pl.BlockSpec(memory_spac...]
    all_to_all x1, starting transfers between devices: 4.22 us -> 6.74 us  [on_device(): lax.all_to_all(pooled, 'sub', split_axis=0, concat_axis=0, tiled=True)]
  transfers between devices with their start and end apart: 24 -> 24, of which waited for: 12 -> 17; matrix products, arithmetic and copies ran while one was open for 7% -> 4% of each run, Pallas kernels for 8% -> 12%
where the time goes in v3:
time: 172 us; the launch traced here: 171 us
  starting transfers between devices  57.5 us (33%)
  waiting for transfers between devices  51.9 us (30%)
  Pallas kernels  34.6 us (20%)
  between operations  14.3 us (8%)
  local copies, waits for them, and re-layouts  10.7 us (6%)
  other arithmetic  2.29 us (1%)
    ppermute x19, starting transfers between devices, move(): lax.ppermute(array, 'sub', [(i, (i + by) % sub_count) for i in range(sub_...  33.2 us
    ppermute x19, waiting for transfers between devices, move(): lax.ppermute(array, 'sub', [(i, (i + by) % sub_count) for i in range(sub_...  21.5 us
    pallas_call x5, Pallas kernels, attention(): pl.pallas_call(functools.partial(attention_kernel, offsets, parts, chunk,...  16.4 us
    all_to_all x1, starting transfers between devices, on_device(): lax.all_to_all(sent.reshape(dp_count, PACK, width), 'dp', split_axis=0, c...  14.4 us
    all_to_all x1, waiting for transfers between devices, on_device(): lax.all_to_all(sent.reshape(dp_count, PACK, width), 'dp', split_axis=0, c...  11.5 us
    pallas_call x8, Pallas kernels, small_call(): pl.pallas_call(kernel, in_specs=specs, out_specs=pl.BlockSpec(memory_spac...  9.95 us
    ppermute x2, waiting for transfers between devices, swap(): return lax.ppermute(array, 'sub', [(i, i ^ 1) for i in range(sub_count)])  9.15 us
    all_to_all x1, waiting for transfers between devices, on_device(): lax.all_to_all(pooled, 'sub', split_axis=0, concat_axis=0, tiled=True)  9.05 us
  transfers between devices with their start and end apart: 24, of which 17 were waited for; matrix products, arithmetic and copies ran while one was open for 4% of the time, Pallas kernels for 12%

profile of v3, /device:TPU:1, one launch (start us, length us, event | category | flops | bytes accessed | tf_op | source)
XLA Modules:
  0.0 171.4 jit_solution(586206197085130555)
XLA Ops:
  8.3 2.5 %collective-permute-start.3 = (bf16[1024,128]{1,0:T(8,128)(2,1)}, bf16[1024,128]{1,0:T(8,128)(2,1)S(1)}, u32[]{:S(2)}, u32[]{:S(2)}) collective-permute-start(bf16[1024,128]{1,0:T(8,128)(2,1)} %refs_0_.4), channel_id=1, source_target_pairs={{0,1},{1,2},{2,3},{3,4},{4,5},{5,6},{6,7},{7,0},{8,9},{9,10},{10,1... | collective-permute-start | bytes 786440 | tf_op jit(solution)/shard_map/ppermute | solution.py:347
  10.9 4.0 %collective-permute-start = (bf16[1024,128]{1,0:T(8,128)(2,1)}, bf16[1024,128]{1,0:T(8,128)(2,1)S(1)}, u32[]{:S(2)}, u32[]{:S(2)}) collective-permute-start(bf16[1024,128]{1,0:T(8,128)(2,1)} %refs_0_.4), channel_id=1, source_target_pairs={{0,7},{1,0},{2,1},{3,2},{4,3},{5,4},{6,5},{7,6},{8,15},{9,8},{10,9... | collective-permute-start | bytes 786440 | tf_op jit(solution)/shard_map/ppermute | solution.py:347
  14.9 3.9 %collective-permute-start.18 = (bf16[64,1024]{1,0:T(8,128)(2,1)S(1)}, bf16[64,1024]{1,0:T(8,128)(2,1)S(1)}, u32[]{:S(2)}, u32[]{:S(2)}) collective-permute-start(bf16[64,1024]{1,0:T(8,128)(2,1)S(1)} %pad_maximum_fusion.1), channel_id=1, source_target_pairs={{0,4},{1,5},{2,6},{3,7},{4,0},{5,1},{6,2},{7,3},{8,12},{9,13},{10,... | collective-permute-start | bytes 393224 | tf_op jit(solution)/shard_map/ppermute | solution.py:347
  18.8 3.6 %collective-permute-start.19 = (bf16[64,1024]{1,0:T(8,128)(2,1)S(1)}, bf16[64,1024]{1,0:T(8,128)(2,1)S(1)}, u32[]{:S(2)}, u32[]{:S(2)}) collective-permute-start(bf16[64,1024]{1,0:T(8,128)(2,1)S(1)} %pad_maximum_fusion.1), channel_id=1, source_target_pairs={{0,6},{1,7},{2,0},{3,1},{4,2},{5,3},{6,4},{7,5},{8,14},{9,15},{10,... | collective-permute-start | bytes 393224 | tf_op jit(solution)/shard_map/ppermute | solution.py:347
  22.4 3.2 %collective-permute-done.17 = bf16[64,1024]{1,0:T(8,128)(2,1)S(1)} collective-permute-done((bf16[64,1024]{1,0:T(8,128)(2,1)S(1)}, bf16[64,1024]{1,0:T(8,128)(2,1)S(1)}, u32[]{:S(2)}, u32[]{:S(2)}) %collective-permute-start.17) | collective-permute-done | bytes 131104 | tf_op jit(solution)/shard_map/ppermute | solution.py:347
  25.5 3.3 %collective-permute-done.18 = bf16[64,1024]{1,0:T(8,128)(2,1)S(1)} collective-permute-done((bf16[64,1024]{1,0:T(8,128)(2,1)S(1)}, bf16[64,1024]{1,0:T(8,128)(2,1)S(1)}, u32[]{:S(2)}, u32[]{:S(2)}) %collective-permute-start.18) | collective-permute-done | bytes 131104 | tf_op jit(solution)/shard_map/ppermute | solution.py:347
  28.8 3.2 %collective-permute-done.19 = bf16[64,1024]{1,0:T(8,128)(2,1)S(1)} collective-permute-done((bf16[64,1024]{1,0:T(8,128)(2,1)S(1)}, bf16[64,1024]{1,0:T(8,128)(2,1)S(1)}, u32[]{:S(2)}, u32[]{:S(2)}) %collective-permute-start.19) | collective-permute-done | bytes 131104 | tf_op jit(solution)/shard_map/ppermute | solution.py:347
  33.0 2.7 %collective-permute-start.1 = (bf16[1024,128]{1,0:T(8,128)(2,1)S(1)}, bf16[1024,128]{1,0:T(8,128)(2,1)S(1)}, u32[]{:S(2)}, u32[]{:S(2)}) collective-permute-start(bf16[1024,128]{1,0:T(8,128)(2,1)S(1)} %collective-permute-done.refs_1_), channel_id=1, source_target_pairs={{0,7},{1,0},{2,1},{3,2},{4,3},{5,4},{6,5},{7,6},{8,15},{9,8},{10,9... | collective-permute-start | bytes 786440 | tf_op jit(solution)/shard_map/ppermute | solution.py:347
  35.6 4.3 %collective-permute-done.4.refs_7_ = bf16[1024,128]{1,0:T(8,128)(2,1)S(1)} collective-permute-done((bf16[1024,128]{1,0:T(8,128)(2,1)S(1)}, bf16[1024,128]{1,0:T(8,128)(2,1)S(1)}, u32[]{:S(2)}, u32[]{:S(2)}) %collective-permute-start.4) | collective-permute-done | bytes 262176 | tf_op jit(solution)/shard_map/ppermute | solution.py:347
  44.5 3.0 %collective-permute-done.5.refs_8_ = bf16[1024,128]{1,0:T(8,128)(2,1)S(1)} collective-permute-done((bf16[1024,128]{1,0:T(8,128)(2,1)S(1)}, bf16[1024,128]{1,0:T(8,128)(2,1)S(1)}, u32[]{:S(2)}, u32[]{:S(2)}) %collective-permute-start.5) | collective-permute-done | bytes 262176 | tf_op jit(solution)/shard_map/ppermute | solution.py:347
  49.0 2.7 %collective-permute-start.7 = (bf16[512,128]{1,0:T(8,128)(2,1)}, bf16[512,128]{1,0:T(8,128)(2,1)}, u32[]{:S(2)}, u32[]{:S(2)}) collective-permute-start(bf16[512,128]{1,0:T(8,128)(2,1)} %slice.9), channel_id=1, source_target_pairs={{0,7},{1,0},{2,1},{3,2},{4,3},{5,4},{6,5},{7,6},{8,15},{9,8},{10,9... | collective-permute-start | bytes 393224 | tf_op jit(solution)/shard_map/ppermute | solution.py:347
  55.9 2.7 %attention.9.context_ref = bf16[128,128]{1,0:T(8,128)(2,1)S(1)} custom-call(s32[1]{0:T(128)} %bitcast.1.me_ref.sub_ref, s32[32,2]{1,0:T(8,128)S(1)} %reduce_window_sum.11.ends_ref, bf16[1024,128]{1,0:T(8,128)(2,1)} %refs_0_.4, bf16[1024,128]{1,0:T(8,128)(2,1)} %copy-done.10, bf16[1024,128]{1,0:T(8,128)(2,1)} %copy-done.12, bf16[1024,128]{1,0:T(8,128)(2,1)} %copy-done.8, ...), custom_call_target="tpu_custom_call" | custom-call | flops 134217728 | bytes 3145728 | tf_op jit(solution)/shard_map/attention/pallas_call | solution.py:129
  59.0 2.7 %collective-permute-start.9 = (bf16[64,1024]{1,0:T(8,128)(2,1)S(1)}, bf16[64,1024]{1,0:T(8,128)(2,1)S(1)}, u32[]{:S(2)}, u32[]{:S(2)}) collective-permute-start(bf16[64,1024]{1,0:T(8,128)(2,1)S(1)} %get-tuple-element.21), channel_id=1, source_target_pairs={{0,7},{1,0},{2,1},{3,2},{4,3},{5,4},{6,5},{7,6},{8,15},{9,8},{10,9... | collective-permute-start | bytes 393224 | tf_op jit(solution)/shard_map/ppermute | solution.py:347
  61.7 3.6 %attention.8.context_ref = bf16[256,128]{1,0:T(8,128)(2,1)S(1)} custom-call(s32[1]{0:T(128)} %bitcast.1.me_ref.sub_ref, s32[32,2]{1,0:T(8,128)S(1)} %reduce_window_sum.11.ends_ref, bf16[1024,128]{1,0:T(8,128)(2,1)} %refs_0_.4, bf16[1024,128]{1,0:T(8,128)(2,1)} %copy-done.10, bf16[1024,128]{1,0:T(8,128)(2,1)} %copy-done.12, bf16[1024,128]{1,0:T(8,128)(2,1)} %copy-done.8, ...), custom_call_target="tpu_custom_call" | custom-call | flops 268435456 | bytes 3145728 | tf_op jit(solution)/shard_map/attention/pallas_call | solution.py:129
  68.3 3.6 %attention.7.context_ref = bf16[256,128]{1,0:T(8,128)(2,1)S(1)} custom-call(s32[1]{0:T(128)} %bitcast.1.me_ref.sub_ref, s32[32,2]{1,0:T(8,128)S(1)} %reduce_window_sum.11.ends_ref, bf16[1024,128]{1,0:T(8,128)(2,1)} %refs_0_.4, bf16[1024,128]{1,0:T(8,128)(2,1)} %copy-done.10, bf16[1024,128]{1,0:T(8,128)(2,1)} %copy-done.12, bf16[1024,128]{1,0:T(8,128)(2,1)} %copy-done.8, ...), custom_call_target="tpu_custom_call" | custom-call | flops 268435456 | bytes 3145728 | tf_op jit(solution)/shard_map/attention/pallas_call | solution.py:129
  76.1 3.6 %attention.6.context_ref = bf16[256,128]{1,0:T(8,128)(2,1)S(1)} custom-call(s32[1]{0:T(128)} %bitcast.1.me_ref.sub_ref, s32[32,2]{1,0:T(8,128)S(1)} %reduce_window_sum.11.ends_ref, bf16[1024,128]{1,0:T(8,128)(2,1)} %refs_0_.4, bf16[1024,128]{1,0:T(8,128)(2,1)} %copy-done.10, bf16[1024,128]{1,0:T(8,128)(2,1)} %copy-done.12, bf16[1024,128]{1,0:T(8,128)(2,1)} %copy-done.8, ...), custom_call_target="tpu_custom_call" | custom-call | flops 268435456 | bytes 3145728 | tf_op jit(solution)/shard_map/attention/pallas_call | solution.py:129
  86.6 2.9 %attention.5.base_ref = f32[128,1024]{1,0:T(8,128)S(1)} custom-call(s32[1]{0:T(128)} %bitcast.1.me_ref.sub_ref, s32[32,2]{1,0:T(8,128)S(1)} %reduce_window_sum.11.ends_ref, bf16[1024,128]{1,0:T(8,128)(2,1)} %refs_0_.4, bf16[1024,128]{1,0:T(8,128)(2,1)} %copy-done.10, bf16[1024,128]{1,0:T(8,128)(2,1)} %copy-done.12, bf16[1024,128]{1,0:T(8,128)(2,1)} %copy-done.8, ...), custom_call_target="tpu_custom_call" | custom-call | flops 134217728 | bytes 3145728 | tf_op jit(solution)/shard_map/attention/pallas_call | solution.py:129
  95.8 5.4 %collective-permute-done.16.pair_ref = bf16[128,1024]{1,0:T(8,128)(2,1)S(1)} collective-permute-done((bf16[128,1024]{1,0:T(8,128)(2,1)S(1)}, bf16[128,1024]{1,0:T(8,128)(2,1)S(1)}, u32[]{:S(2)}, u32[]{:S(2)}) %collective-permute-start.16) | collective-permute-done | bytes 262176 | tf_op jit(solution)/shard_map/ppermute | solution.py:350
  103.5 8.2 %feed.1 = (f32[128,1024]{1,0:T(8,128)S(1)}, bf16[128,1024]{1,0:T(8,128)(2,1)}) custom-call(bf16[128,1024]{1,0:T(8,128)(2,1)S(1)} %get-tuple-element.28.own_ref, bf16[128,1024]{1,0:T(8,128)(2,1)S(1)} %copy-done.3, f32[128,1024]{1,0:T(8,128)S(1)} %get-tuple-element.29.hidden_ref, bf16[1024,1024]{1,0:T(8,128)(2,1)} %up_ref.1, bf16[1024,1024]{1,0:T(8,128)(2,1)} %down_ref.1, ...), custom_call_target="tpu_custom_call" | custom-call | flops 4294967296 | bytes 16777216 | tf_op jit(solution)/shard_map/feed/pallas_call | solution.py:206
  113.5 3.8 %collective-permute-done.20.pair_ref = bf16[128,1024]{1,0:T(8,128)(2,1)S(1)} collective-permute-done((bf16[128,1024]{1,0:T(8,128)(2,1)}, bf16[128,1024]{1,0:T(8,128)(2,1)S(1)}, u32[]{:S(2)}, u32[]{:S(2)}) %collective-permute-start.20) | collective-permute-done | bytes 262176 | tf_op jit(solution)/shard_map/ppermute | solution.py:350
  118.6 6.7 %all-to-all-start = ((f32[8,8,1024]{2,1,0:T(8,128)}), f32[8,8,1024]{2,1,0:T(8,128)S(1)}, u32[]{:S(2)}, u32[]{:S(2)}) async-start(f32[8,8,1024]{2,1,0:T(8,128)} %pool.1), calls=%async_computation | async-start | bytes 524288 | tf_op jit(solution)/shard_map/all_to_all | solution.py:427
  125.6 9.0 %all-to-all-done.pooled_ref = f32[8,8,1024]{2,1,0:T(8,128)S(1)} async-done(((f32[8,8,1024]{2,1,0:T(8,128)}), f32[8,8,1024]{2,1,0:T(8,128)S(1)}, u32[]{:S(2)}, u32[]{:S(2)}) %all-to-all-start) | async-done | bytes 262176 | tf_op jit(solution)/shard_map/all_to_all | solution.py:427
  136.7 14.4 %all-to-all-start.1 = ((bf16[32,8,1024]{2,1,0:T(8,128)(2,1)}), bf16[32,8,1024]{2,1,0:T(8,128)(2,1)S(1)}, u32[]{:S(2)}, u32[]{:S(2)}) async-start(bf16[32,8,1024]{2,1,0:T(8,128)(2,1)} %bitcast.4), calls=%async_computation.1 | async-start | bytes 1048576 | tf_op jit(solution)/shard_map/all_to_all | solution.py:437
  151.1 11.5 %all-to-all-done.1 = bf16[32,8,1024]{2,1,0:T(8,128)(2,1)S(1)} async-done(((bf16[32,8,1024]{2,1,0:T(8,128)(2,1)}), bf16[32,8,1024]{2,1,0:T(8,128)(2,1)S(1)}, u32[]{:S(2)}, u32[]{:S(2)}) %all-to-all-start.1) | async-done | bytes 524320 | tf_op jit(solution)/shard_map/all_to_all | solution.py:437
  (99 shorter events, 42.5 us)
Async XLA Ops:
  7.2 95.4 %all-gather.2.cloned.1.call-start = ((), (), s32[]{:S(2)}) async-start(), calls=%async_computation.2 | async-start | bytes 12976128 | tf_op jit(solution)/shard_map/all_gather | solution.py:392
  8.3 23.7 %collective-permute-start.3 = (bf16[1024,128]{1,0:T(8,128)(2,1)}, bf16[1024,128]{1,0:T(8,128)(2,1)S(1)}, u32[]{:S(2)}, u32[]{:S(2)}) collective-permute-start(bf16[1024,128]{1,0:T(8,128)(2,1)} %refs_0_.4), channel_id=1, source_target_pairs={{0,1},{1,2},{2,3},{3,4},{4,5},{5,6},{6,7},{7,0},{8,9},{9,10},{10,1... | collective-permute-start | bytes 786440 | tf_op jit(solution)/shard_map/ppermute | solution.py:347
  10.9 21.1 %collective-permute-start = (bf16[1024,128]{1,0:T(8,128)(2,1)}, bf16[1024,128]{1,0:T(8,128)(2,1)S(1)}, u32[]{:S(2)}, u32[]{:S(2)}) collective-permute-start(bf16[1024,128]{1,0:T(8,128)(2,1)} %refs_0_.4), channel_id=1, source_target_pairs={{0,7},{1,0},{2,1},{3,2},{4,3},{5,4},{6,5},{7,6},{8,15},{9,8},{10,9... | collective-permute-start | bytes 786440 | tf_op jit(solution)/shard_map/ppermute | solution.py:347
  14.9 10.7 %collective-permute-start.17 = (bf16[64,1024]{1,0:T(8,128)(2,1)S(1)}, bf16[64,1024]{1,0:T(8,128)(2,1)S(1)}, u32[]{:S(2)}, u32[]{:S(2)}) collective-permute-start(bf16[64,1024]{1,0:T(8,128)(2,1)S(1)} %pad_maximum_fusion.1), channel_id=1, source_target_pairs={{0,2},{1,3},{2,4},{3,5},{4,6},{5,7},{6,0},{7,1},{8,10},{9,11},{10,... | collective-permute-start | bytes 393224 | tf_op jit(solution)/shard_map/ppermute | solution.py:347
  14.9 13.9 %collective-permute-start.18 = (bf16[64,1024]{1,0:T(8,128)(2,1)S(1)}, bf16[64,1024]{1,0:T(8,128)(2,1)S(1)}, u32[]{:S(2)}, u32[]{:S(2)}) collective-permute-start(bf16[64,1024]{1,0:T(8,128)(2,1)S(1)} %pad_maximum_fusion.1), channel_id=1, source_target_pairs={{0,4},{1,5},{2,6},{3,7},{4,0},{5,1},{6,2},{7,3},{8,12},{9,13},{10,... | collective-permute-start | bytes 393224 | tf_op jit(solution)/shard_map/ppermute | solution.py:347
  18.8 13.2 %collective-permute-start.19 = (bf16[64,1024]{1,0:T(8,128)(2,1)S(1)}, bf16[64,1024]{1,0:T(8,128)(2,1)S(1)}, u32[]{:S(2)}, u32[]{:S(2)}) collective-permute-start(bf16[64,1024]{1,0:T(8,128)(2,1)S(1)} %pad_maximum_fusion.1), channel_id=1, source_target_pairs={{0,6},{1,7},{2,0},{3,1},{4,2},{5,3},{6,4},{7,5},{8,14},{9,15},{10,... | collective-permute-start | bytes 393224 | tf_op jit(solution)/shard_map/ppermute | solution.py:347
  32.9 7.0 %collective-permute-start.4 = (bf16[1024,128]{1,0:T(8,128)(2,1)S(1)}, bf16[1024,128]{1,0:T(8,128)(2,1)S(1)}, u32[]{:S(2)}, u32[]{:S(2)}) collective-permute-start(bf16[1024,128]{1,0:T(8,128)(2,1)S(1)} %collective-permute-done.3.refs_6_), channel_id=1, source_target_pairs={{0,1},{1,2},{2,3},{3,4},{4,5},{5,6},{6,7},{7,0},{8,9},{9,10},{10,1... | collective-permute-start | bytes 786440 | tf_op jit(solution)/shard_map/ppermute | solution.py:347
  33.0 8.7 %collective-permute-start.1 = (bf16[1024,128]{1,0:T(8,128)(2,1)S(1)}, bf16[1024,128]{1,0:T(8,128)(2,1)S(1)}, u32[]{:S(2)}, u32[]{:S(2)}) collective-permute-start(bf16[1024,128]{1,0:T(8,128)(2,1)S(1)} %collective-permute-done.refs_1_), channel_id=1, source_target_pairs={{0,7},{1,0},{2,1},{3,2},{4,3},{5,4},{6,5},{7,6},{8,15},{9,8},{10,9... | collective-permute-start | bytes 786440 | tf_op jit(solution)/shard_map/ppermute | solution.py:347
  39.9 7.6 %collective-permute-start.5 = (bf16[1024,128]{1,0:T(8,128)(2,1)S(1)}, bf16[1024,128]{1,0:T(8,128)(2,1)S(1)}, u32[]{:S(2)}, u32[]{:S(2)}) collective-permute-start(bf16[1024,128]{1,0:T(8,128)(2,1)S(1)} %collective-permute-done.4.refs_7_), channel_id=1, source_target_pairs={{0,1},{1,2},{2,3},{3,4},{4,5},{5,6},{6,7},{7,0},{8,9},{9,10},{10,1... | collective-permute-start | bytes 786440 | tf_op jit(solution)/shard_map/ppermute | solution.py:347
  41.7 6.6 %collective-permute-start.2 = (bf16[1024,128]{1,0:T(8,128)(2,1)S(1)}, bf16[1024,128]{1,0:T(8,128)(2,1)S(1)}, u32[]{:S(2)}, u32[]{:S(2)}) collective-permute-start(bf16[1024,128]{1,0:T(8,128)(2,1)S(1)} %collective-permute-done.1.refs_2_), channel_id=1, source_target_pairs={{0,7},{1,0},{2,1},{3,2},{4,3},{5,4},{6,5},{7,6},{8,15},{9,8},{10,9... | collective-permute-start | bytes 786440 | tf_op jit(solution)/shard_map/ppermute | solution.py:347
  48.2 7.1 %collective-permute-start.6 = (bf16[512,128]{1,0:T(8,128)(2,1)}, bf16[512,128]{1,0:T(8,128)(2,1)S(1)}, u32[]{:S(2)}, u32[]{:S(2)}) collective-permute-start(bf16[512,128]{1,0:T(8,128)(2,1)} %slice.8), channel_id=1, source_target_pairs={{0,1},{1,2},{2,3},{3,4},{4,5},{5,6},{6,7},{7,0},{8,9},{9,10},{10,1... | collective-permute-start | bytes 393224 | tf_op jit(solution)/shard_map/ppermute | solution.py:347
  49.0 6.3 %collective-permute-start.7 = (bf16[512,128]{1,0:T(8,128)(2,1)}, bf16[512,128]{1,0:T(8,128)(2,1)}, u32[]{:S(2)}, u32[]{:S(2)}) collective-permute-start(bf16[512,128]{1,0:T(8,128)(2,1)} %slice.9), channel_id=1, source_target_pairs={{0,7},{1,0},{2,1},{3,2},{4,3},{5,4},{6,5},{7,6},{8,15},{9,8},{10,9... | collective-permute-start | bytes 393224 | tf_op jit(solution)/shard_map/ppermute | solution.py:347
  58.9 6.4 %collective-permute-start.8 = (bf16[64,1024]{1,0:T(8,128)(2,1)S(1)}, bf16[64,1024]{1,0:T(8,128)(2,1)S(1)}, u32[]{:S(2)}, u32[]{:S(2)}) collective-permute-start(bf16[64,1024]{1,0:T(8,128)(2,1)S(1)} %get-tuple-element.20), channel_id=1, source_target_pairs={{0,1},{1,2},{2,3},{3,4},{4,5},{5,6},{6,7},{7,0},{8,9},{9,10},{10,1... | collective-permute-start | bytes 393224 | tf_op jit(solution)/shard_map/ppermute | solution.py:347
  59.0 6.3 %collective-permute-start.9 = (bf16[64,1024]{1,0:T(8,128)(2,1)S(1)}, bf16[64,1024]{1,0:T(8,128)(2,1)S(1)}, u32[]{:S(2)}, u32[]{:S(2)}) collective-permute-start(bf16[64,1024]{1,0:T(8,128)(2,1)S(1)} %get-tuple-element.21), channel_id=1, source_target_pairs={{0,7},{1,0},{2,1},{3,2},{4,3},{5,4},{6,5},{7,6},{8,15},{9,8},{10,9... | collective-permute-start | bytes 393224 | tf_op jit(solution)/shard_map/ppermute | solution.py:347
  65.6 6.5 %collective-permute-start.10 = (bf16[128,1024]{1,0:T(8,128)(2,1)S(1)}, bf16[128,1024]{1,0:T(8,128)(2,1)S(1)}, u32[]{:S(2)}, u32[]{:S(2)}) collective-permute-start(bf16[128,1024]{1,0:T(8,128)(2,1)S(1)} %get-tuple-element.22), channel_id=1, source_target_pairs={{0,1},{1,2},{2,3},{3,4},{4,5},{5,6},{6,7},{7,0},{8,9},{9,10},{10,1... | collective-permute-start | bytes 786440 | tf_op jit(solution)/shard_map/ppermute | solution.py:347
  67.2 5.2 %collective-permute-start.11 = (bf16[128,1024]{1,0:T(8,128)(2,1)S(1)}, bf16[128,1024]{1,0:T(8,128)(2,1)S(1)}, u32[]{:S(2)}, u32[]{:S(2)}) collective-permute-start(bf16[128,1024]{1,0:T(8,128)(2,1)S(1)} %get-tuple-element.23), channel_id=1, source_target_pairs={{0,7},{1,0},{2,1},{3,2},{4,3},{5,4},{6,5},{7,6},{8,15},{9,8},{10,9... | collective-permute-start | bytes 786440 | tf_op jit(solution)/shard_map/ppermute | solution.py:347
  73.4 7.0 %collective-permute-start.12 = (bf16[128,1024]{1,0:T(8,128)(2,1)}, bf16[128,1024]{1,0:T(8,128)(2,1)S(1)}, u32[]{:S(2)}, u32[]{:S(2)}) collective-permute-start(bf16[128,1024]{1,0:T(8,128)(2,1)} %get-tuple-element.24), channel_id=1, source_target_pairs={{0,1},{1,2},{2,3},{3,4},{4,5},{5,6},{6,7},{7,0},{8,9},{9,10},{10,1... | collective-permute-start | bytes 786440 | tf_op jit(solution)/shard_map/ppermute | solution.py:347
  75.7 5.8 %collective-permute-start.13 = (bf16[128,1024]{1,0:T(8,128)(2,1)}, bf16[128,1024]{1,0:T(8,128)(2,1)}, u32[]{:S(2)}, u32[]{:S(2)}) collective-permute-start(bf16[128,1024]{1,0:T(8,128)(2,1)} %get-tuple-element.25), channel_id=1, source_target_pairs={{0,7},{1,0},{2,1},{3,2},{4,3},{5,4},{6,5},{7,6},{8,15},{9,8},{10,9... | collective-permute-start | bytes 786440 | tf_op jit(solution)/shard_map/ppermute | solution.py:347
  83.5 7.0 %collective-permute-start.14 = (bf16[128,1024]{1,0:T(8,128)(2,1)}, bf16[128,1024]{1,0:T(8,128)(2,1)S(1)}, u32[]{:S(2)}, u32[]{:S(2)}) collective-permute-start(bf16[128,1024]{1,0:T(8,128)(2,1)} %get-tuple-element.26), channel_id=1, source_target_pairs={{0,1},{1,2},{2,3},{3,4},{4,5},{5,6},{6,7},{7,0},{8,9},{9,10},{10,1... | collective-permute-start | bytes 786440 | tf_op jit(solution)/shard_map/ppermute | solution.py:347
  86.0 5.8 %collective-permute-start.15 = (bf16[128,1024]{1,0:T(8,128)(2,1)}, bf16[128,1024]{1,0:T(8,128)(2,1)}, u32[]{:S(2)}, u32[]{:S(2)}) collective-permute-start(bf16[128,1024]{1,0:T(8,128)(2,1)} %get-tuple-element.27), channel_id=1, source_target_pairs={{0,7},{1,0},{2,1},{3,2},{4,3},{5,4},{6,5},{7,6},{8,15},{9,8},{10,9... | collective-permute-start | bytes 786440 | tf_op jit(solution)/shard_map/ppermute | solution.py:347
  94.0 7.2 %collective-permute-start.16 = (bf16[128,1024]{1,0:T(8,128)(2,1)S(1)}, bf16[128,1024]{1,0:T(8,128)(2,1)S(1)}, u32[]{:S(2)}, u32[]{:S(2)}) collective-permute-start(bf16[128,1024]{1,0:T(8,128)(2,1)S(1)} %get-tuple-element.28.own_ref), channel_id=1, source_target_pairs={{0,1},{1,0},{2,3},{3,2},{4,5},{5,4},{6,7},{7,6},{8,9},{9,8},{10,11... | collective-permute-start | bytes 786440 | tf_op jit(solution)/shard_map/ppermute | solution.py:350
  111.8 5.5 %collective-permute-start.20 = (bf16[128,1024]{1,0:T(8,128)(2,1)}, bf16[128,1024]{1,0:T(8,128)(2,1)S(1)}, u32[]{:S(2)}, u32[]{:S(2)}) collective-permute-start(bf16[128,1024]{1,0:T(8,128)(2,1)} %get-tuple-element.35), channel_id=1, source_target_pairs={{0,1},{1,0},{2,3},{3,2},{4,5},{5,4},{6,7},{7,6},{8,9},{9,8},{10,11... | collective-permute-start | bytes 786440 | tf_op jit(solution)/shard_map/ppermute | solution.py:350
  118.6 16.1 %all-to-all-start = ((f32[8,8,1024]{2,1,0:T(8,128)}), f32[8,8,1024]{2,1,0:T(8,128)S(1)}, u32[]{:S(2)}, u32[]{:S(2)}) async-start(f32[8,8,1024]{2,1,0:T(8,128)} %pool.1), calls=%async_computation | async-start | bytes 524288 | tf_op jit(solution)/shard_map/all_to_all | solution.py:427
  136.7 26.0 %all-to-all-start.1 = ((bf16[32,8,1024]{2,1,0:T(8,128)(2,1)}), bf16[32,8,1024]{2,1,0:T(8,128)(2,1)S(1)}, u32[]{:S(2)}, u32[]{:S(2)}) async-start(bf16[32,8,1024]{2,1,0:T(8,128)(2,1)} %bitcast.4), calls=%async_computation.1 | async-start | bytes 1048576 | tf_op jit(solution)/shard_map/all_to_all | solution.py:437
  (17 other events, 305.6 us)
Sparse Core Ops, SparseCore 0:
  33.0 69.5 all-gather.1

commit v4 on v3

--- a/solution.py
+++ b/solution.py
@@ -12,6 +12,7 @@
 SUBW = 64
 LANES = 128
 SLOTS = 2
+CORES = 2
 KINDS = 4
 PACK = 8
 
@@ -133,7 +134,7 @@
         out_shape=jax.ShapeDtypeStruct((size * chunk, width if with_base else local), F32 if with_base else BF),
         scratch_shapes=[pltpu.VMEM((size, chunk, width), BF), pltpu.SemaphoreType.DMA((size, parts))],
         compiler_params=pltpu.CompilerParams(vmem_limit_bytes=16 << 20),
-        cost_estimate=cost(size * 2 * chunk * width * 4 * local, 3 << 20),
+        cost_estimate=cost(40 * size * 2 * chunk * width * 4 * local, 3 << 20),
         name="attention",
     )(me, ends, *pieces, w_qkv, w_out)
 
@@ -145,16 +146,14 @@
     left_ref[...] = sums[half:]
 
 
-def join_kernel(context_ref, wo_ref, right_ref, left_ref, right_out, left_out):
-    chunk = right_out.shape[0]
-    sums = dot(context_ref[...], wo_ref[...])
-    ahead, back = sums[:chunk], sums[chunk:]
-    half = right_ref.shape[0]
-    right_out[:half] = (ahead[:half] + right_ref[...].astype(F32)).astype(BF)
-    left_out[chunk - half:] = (back[chunk - half:] + left_ref[...].astype(F32)).astype(BF)
+def join_kernel(at, start, context_ref, wo_ref, recv_ref, out_ref):
+    chunk, half = out_ref.shape[0], recv_ref.shape[0]
+    sums = dot(context_ref[at * chunk:(at + 1) * chunk], wo_ref[...])
+    rows = slice(start, start + half)
+    out_ref[rows] = (sums[rows] + recv_ref[...].astype(F32)).astype(BF)
     if half < chunk:
-        right_out[half:] = ahead[half:].astype(BF)
-        left_out[:chunk - half] = back[:chunk - half].astype(BF)
+        rest = slice(half - start, chunk - start)
+        out_ref[rest] = sums[rest].astype(BF)
 
 
 def middle_kernel(base_ref, right_ref, left_ref, hidden_ref, normed_ref):
@@ -226,37 +225,40 @@
     out_ref[...] = jnp.broadcast_to(pooled[None], out_ref.shape)
 
 
-def moments_kernel(sub_ref, pooled_ref, proj_ref, code_ref, out_ref):
-    me = sub_ref[0]
+def moments_kernel(own, where_ref, pooled_ref, proj_ref, code_ref, out_ref):
+    first, core = where_ref[0], where_ref[1]
     parts, few, width = pooled_ref.shape
     sentences = parts * few
     pooled = pooled_ref[...].reshape(sentences, width)
     total = out_ref.shape[0]
-    groups = total // PACK
-    per_group = width // groups
-    own = per_group // parts
+    per_chip = width // (total // PACK)
     mean = jnp.mean(pooled, axis=0, keepdims=True)
-    centred = pooled - mean
+    large, small = split(pooled - mean)
     feature = lax.broadcasted_iota(jnp.int32, (width, total), 0)
     wanted = lax.broadcasted_iota(jnp.int32, (width, total), 1)
-    chosen = (wanted // PACK) * per_group + me * own + wanted % PACK
+    chosen = (wanted // PACK) * per_chip + first + wanted % PACK
     pick = jnp.where((feature == chosen) & (wanted % PACK < own), 1.0, 0.0).astype(BF)
-    large, small = split(centred)
     picked_large, picked_small = dot(large, pick).astype(BF), dot(small, pick).astype(BF)
-    first = ((0,), (0,))
-    moments = dot(picked_large, large, first) + (dot(picked_large, small, first) + dot(picked_small, large, first))
+    rows = ((0,), (0,))
+    moments = dot(picked_large, large, rows) + (dot(picked_large, small, rows) + dot(picked_small, large, rows))
     rotated = dot(large, proj_ref[...]).astype(BF)
     lanes = rotated.shape[1]
     row = lax.broadcasted_iota(jnp.int32, (total, sentences), 0)
-    pieces = []
-    flags = []
+    column = lax.broadcasted_iota(jnp.int32, (total, sentences), 1)
+    target = ((row // PACK) * CORES + core) * KINDS
+    half = sentences // CORES
     ones = jnp.ones((sentences, lanes), BF)
-    for k in range(KINDS):
-        place = (row % PACK == own + 2) & ((row // PACK) * KINDS + k == code_ref[...])
-        place = jnp.where(place, 1.0, 0.0).astype(BF)
-        pieces.append(dot(place, rotated))
-        flags.append(dot(place, ones))
-    sides = jnp.concatenate(pieces + flags, axis=-1)
+    sides = []
+    for a in range(CORES):
+        mine = (column // half == a) & (row % PACK == own + 2)
+        there = (column // half == a) & (row % PACK == own + 3)
+        for k in range(KINDS):
+            hit = target + k == code_ref[...]
+            sides.append(
+                dot(jnp.where(mine & hit, 1.0, 0.0).astype(BF), rotated)
+                + dot(jnp.where(there & hit, 1.0, 0.0).astype(BF), ones)
+            )
+    sides = jnp.concatenate(sides, axis=-1)
     high = mean.astype(BF).astype(F32)
     low = mean - high
     line = lax.broadcasted_iota(jnp.int32, (total, 1), 0) % PACK
@@ -269,14 +271,14 @@
     own, width = cov_ref.shape
     recv = recv_ref[...]
     total = recv.shape[0]
-    groups = total // PACK
+    chips = total // PACK
     sentences = pq_ref.shape[1]
-    count = float(groups * sentences)
-    source = lax.broadcasted_iota(jnp.int32, (groups, total), 0)
-    line = lax.broadcasted_iota(jnp.int32, (groups, total), 1)
-    pick_mean = (line == source * PACK + own) | (line == source * PACK + own + 1)
-    means = dot(jnp.where(pick_mean, 1.0, 0.0).astype(BF), recv)
-    sides = dot(jnp.where(line == source * PACK + own + 2, 1.0, 0.0).astype(BF), recv)
+    each = float(CORES * sentences)
+    source = lax.broadcasted_iota(jnp.int32, (chips, total), 0)
+    line = lax.broadcasted_iota(jnp.int32, (chips, total), 1) - source * PACK
+    means = dot(jnp.where((line == own) | (line == own + 1), 1.0, 0.0).astype(BF), recv)
+    sides = dot(jnp.where(line == own + 2, 1.0, 0.0).astype(BF), recv).astype(BF)
+    there = dot(jnp.where(line == own + 3, 1.0, 0.0).astype(BF), recv).astype(BF)
     line = lax.broadcasted_iota(jnp.int32, (PACK, total), 1) % PACK
     within = dot(jnp.where(line == lax.broadcasted_iota(jnp.int32, (PACK, total), 0), 1.0, 0.0).astype(BF), recv)
     away = means - jnp.mean(means, axis=0, keepdims=True)
@@ -287,26 +289,27 @@
     picked_large, picked_small = dot(large, pick).astype(BF), dot(small, pick).astype(BF)
     rows = ((0,), (0,))
     between = dot(picked_large, large, rows) + (dot(picked_large, small, rows) + dot(picked_small, large, rows))
-    cov_ref[...] = (within[:own] + float(sentences) * between[:own]) / count
+    cov_ref[...] = (within[:own] + each * between[:own]) / (each * float(chips))
     shift = dot(large, proj_ref[...]) + dot(small, proj_ref[...])
     shift_large, shift_small = split(shift)
     lanes = shift.shape[1]
-    one = lax.broadcasted_iota(jnp.int32, (groups, groups), 0)
-    other = lax.broadcasted_iota(jnp.int32, (groups, groups), 1)
+    one = lax.broadcasted_iota(jnp.int32, (chips, chips), 0)
+    other = lax.broadcasted_iota(jnp.int32, (chips, chips), 1)
     ahead = jnp.where(one < other, 1.0, 0.0).astype(BF)
     same = jnp.where(one == other, 1.0, 0.0).astype(BF)
-    filled = [sides[:, (KINDS + 2 * c) * lanes:(KINDS + 2 * c + 1) * lanes] for c in range(SLOTS)]
-    flat = [dot(f.astype(BF), same, ((0,), (0,)))[:1] for f in filled]
-    before = dot((filled[0] + filled[1]).astype(BF), ahead, ((0,), (0,)))[:1]
-    place = lax.broadcasted_iota(jnp.int32, (sentences, groups), 0)
+    kinds = [a * KINDS + 2 * c for a in range(CORES) for c in range(SLOTS)]
+    filled = [there[:, k * lanes:(k + 1) * lanes] for k in kinds]
+    flat = [dot(f, same, ((0,), (0,)))[:1] for f in filled]
+    before = sum(dot(f, ahead, ((0,), (0,)))[:1] for f in filled)
+    place = lax.broadcasted_iota(jnp.int32, (sentences, chips), 0)
     result = jnp.zeros((sentences, lanes), F32)
-    for c in range(SLOTS):
+    for kind, here in zip(kinds, flat):
         for k in range(2):
-            rows = sides[:, (2 * c + k) * lanes:(2 * c + k + 1) * lanes].astype(BF)
             position = (2.0 * before + float(k)).astype(jnp.int32)
-            chosen = jnp.where((place == position) & (flat[c] > 0.5), 1.0, 0.0).astype(BF)
-            result = result + (dot(chosen, rows) + (dot(chosen, shift_large) + dot(chosen, shift_small)))
-        before = before + flat[c]
+            chosen = jnp.where((place == position) & (here > 0.5), 1.0, 0.0).astype(BF)
+            block = sides[:, (kind + k) * lanes:(kind + k + 1) * lanes]
+            result = result + (dot(chosen, block) + (dot(chosen, shift_large) + dot(chosen, shift_small)))
+        before = before + here
     for q in range(pq_ref.shape[0]):
         pq_ref[q] = result[:, q * SUBW:(q + 1) * SUBW]
 
@@ -354,8 +357,11 @@
         [lax.dynamic_slice_in_dim(w, dp_at * rows, rows, 0) for w in (w_up, w_down)], axis=0
     )
     piece, tokens = lax.optimization_barrier((piece, tokens))
-    others = [move(piece, by) for by in range(2, sub_count, 2)]
-    planes = half - 1
+    across = lax.ppermute(
+        piece, "sub", [(i, (i + (half - 1 if i % 2 else 1 - half)) % sub_count) for i in range(sub_count)]
+    )
+    others = [move(piece, 2), move(piece, -2), across]
+    planes = len(others)
 
     ends = jnp.cumsum(lengths, axis=-1)
     position = jnp.arange(block_rows, dtype=jnp.int32)
@@ -373,6 +379,11 @@
     earlier_count = jnp.sum((matches & earlier).astype(jnp.int32), axis=1)
     code = (dest * SLOTS + earlier_count)[:, None] * per_block + jnp.arange(per_block, dtype=jnp.int32)[None, :]
     code = code.reshape(1, block_count * per_block)
+    chips = dp_count // CORES
+    siblings = [[q * CORES + c for c in range(CORES)] for q in range(chips)]
+    other = lax.ppermute(code, "dp", [(i, i ^ 1) for i in range(dp_count)])
+    core = dp_at % CORES
+    code = jnp.where(core == 0, jnp.concatenate((code, other), axis=1), jnp.concatenate((other, code), axis=1))
     w_qkv = jnp.concatenate((w_query, w_key, w_value), axis=1)
     columns = width // sub_count
     proj = lax.dynamic_slice_in_dim(projection, sub_at * columns, columns, 1)
@@ -385,8 +396,8 @@
             others = lax.optimization_barrier((others, right, left))[0]
         behind.append(right)
         ahead.append(left)
-    middle = local_rows // 2
-    far = [move(right[:middle], 1), move(left[middle:], -1)]
+    halfway = local_rows // 2
+    far = [move(right[:halfway], 1), move(left[halfway:], -1)]
     pieces = [tokens] + ahead + far + behind
 
     gathered = lax.all_gather(jnp.concatenate(others, axis=0), "dp", axis=0, tiled=True)
@@ -403,13 +414,14 @@
     )
     right, left = move(right, 1), move(left, -1)
     for away in range(half - 1, 0, -1):
-        right, left = small_call(
-            join_kernel,
-            [jax.ShapeDtypeStruct(own_shape, BF)] * 2,
-            (attend([away, -away]), w_out, right, left),
+        context = attend([away, -away])
+        join = lambda at, start, recv: small_call(
+            functools.partial(join_kernel, at, start),
+            jax.ShapeDtypeStruct(own_shape, BF),
+            (context, w_out, recv),
             name="join",
         )
-        right, left = move(right, 1), move(left, -1)
+        right, left = move(join(0, 0, right), 1), move(join(1, own_rows - left.shape[0], left), -1)
     base = attend([0], with_base=True)
     hidden1, normed2 = small_call(
         middle_kernel,
@@ -425,18 +437,20 @@
         name="pool",
     )
     pooled = lax.all_to_all(pooled, "sub", split_axis=0, concat_axis=0, tiled=True)
+    pooled = lax.all_gather(pooled, "dp", axis=0, tiled=True, axis_index_groups=siblings)
     sentences = sub_count * own_sentences
     cov_rows = width // (dp_count * sub_count)
     sent = small_call(
-        moments_kernel,
-        jax.ShapeDtypeStruct((dp_count * PACK, width), BF),
+        functools.partial(moments_kernel, cov_rows),
+        jax.ShapeDtypeStruct((chips * PACK, width), BF),
         (pooled, proj, code),
-        scalar=sub_at.reshape(1),
+        scalar=jnp.stack([(core * sub_count + sub_at) * cov_rows, core]).astype(jnp.int32),
         name="moments",
     )
     received = lax.all_to_all(
-        sent.reshape(dp_count, PACK, width), "dp", split_axis=0, concat_axis=0, tiled=True
-    ).reshape(dp_count * PACK, width)
+        sent.reshape(chips, PACK, width), "dp", split_axis=0, concat_axis=0, tiled=True,
+        axis_index_groups=[[q * CORES + c for q in range(chips)] for c in range(CORES)],
+    ).reshape(chips * PACK, width)
     return small_call(
         combine_kernel,
         (

time: 172 us -> 170 us (0.988)
  blocking collectives: 0 us -> 8.56 us
  waiting for transfers between devices: 51.9 us -> 46.6 us
  Pallas kernels: 34.6 us -> 32.2 us
  local copies, waits for them, and re-layouts: 10.7 us -> 8.88 us
    all_gather x0 -> x1, blocking collectives: none -> 8.56 us  [on_device(): lax.all_gather(pooled, 'dp', axis=0, tiled=True, axis_index_groups=siblings)]
    ppermute x0 -> x2, starting transfers between devices: none -> 7.97 us  [the longest x1 5.7 us: on_device(): other = lax.ppermute(code, 'dp', [(i, i ^ 1) for i in range(dp_count)])]
    all_to_all x1, starting transfers between devices: 14.4 us -> 6.6 us  [on_device(): lax.all_to_all(sent.reshape(chips, PACK, width), 'dp', split_axis=0, conc...]
    all_to_all x1, waiting for transfers between devices: 9.05 us -> 2.56 us  [on_device(): lax.all_to_all(pooled, 'sub', split_axis=0, concat_axis=0, tiled=True)]
    ppermute x0 -> x2, waiting for transfers between devices: none -> 5.5 us  [the longest x1 4.84 us: on_device(): lax.ppermute(piece, 'sub', [(i, (i + (half - 1 if i % 2 else 1 - half)) %...]
    all_to_all x1, waiting for transfers between devices: 11.5 us -> 8.11 us  [on_device(): lax.all_to_all(sent.reshape(chips, PACK, width), 'dp', split_axis=0, conc...]
    pallas_call x8 -> x11, Pallas kernels: 9.95 us -> 7.41 us  [small_call(): pl.pallas_call(kernel, in_specs=specs, out_specs=pl.BlockSpec(memory_spac...]
    ppermute x19 -> x18, waiting for transfers between devices: 21.5 us -> 19.5 us  [move(): lax.ppermute(array, 'sub', [(i, (i + by) % sub_count) for i in range(sub_...]
  transfers between devices with their start and end apart: 24 -> 25, of which waited for: 17 -> 17; matrix products, arithmetic and copies ran while one was open for 4% -> 3% of each run, Pallas kernels for 12% -> 11%
where the time goes in v4:
time: 170 us; the launch traced here: 169 us
  starting transfers between devices  57 us (34%)
  waiting for transfers between devices  46.6 us (27%)
  Pallas kernels  32.2 us (19%)
  between operations  14.4 us (8%)
  local copies, waits for them, and re-layouts  8.88 us (5%)
  blocking collectives  8.56 us (5%)
    ppermute x18, starting transfers between devices, move(): lax.ppermute(array, 'sub', [(i, (i + by) % sub_count) for i in range(sub_...  34 us
    ppermute x18, waiting for transfers between devices, move(): lax.ppermute(array, 'sub', [(i, (i + by) % sub_count) for i in range(sub_...  19.5 us
    pallas_call x5, Pallas kernels, attention(): pl.pallas_call(functools.partial(attention_kernel, offsets, parts, chunk,...  16.5 us
    ppermute x2, waiting for transfers between devices, swap(): return lax.ppermute(array, 'sub', [(i, i ^ 1) for i in range(sub_count)])  9.54 us
    all_gather x1, blocking collectives, on_device(): lax.all_gather(pooled, 'dp', axis=0, tiled=True, axis_index_groups=siblings)  8.56 us
    pallas_call x1, Pallas kernels, feed(): pl.pallas_call(feed_kernel, in_specs=[vmem, vmem, vmem, hbm, hbm, hbm], o...  8.24 us
    all_to_all x1, waiting for transfers between devices, on_device(): lax.all_to_all(sent.reshape(chips, PACK, width), 'dp', split_axis=0, conc...  8.11 us
    pallas_call x11, Pallas kernels, small_call(): pl.pallas_call(kernel, in_specs=specs, out_specs=pl.BlockSpec(memory_spac...  7.41 us
  transfers between devices with their start and end apart: 25, of which 17 were waited for; matrix products, arithmetic and copies ran while one was open for 3% of the time, Pallas kernels for 11%

profile of v4, /device:TPU:1, one launch (start us, length us, event | category | flops | bytes accessed | tf_op | source)
XLA Modules:
  0.0 169.3 jit_solution(1302708251783263488)
XLA Ops:
  10.9 4.0 %collective-permute-start = (bf16[1024,128]{1,0:T(8,128)(2,1)}, bf16[1024,128]{1,0:T(8,128)(2,1)}, u32[]{:S(2)}, u32[]{:S(2)}) collective-permute-start(bf16[1024,128]{1,0:T(8,128)(2,1)} %refs_0_.4), channel_id=1, source_target_pairs={{0,7},{1,0},{2,1},{3,2},{4,3},{5,4},{6,5},{7,6},{8,15},{9,8},{10,9... | collective-permute-start | bytes 786440 | tf_op jit(solution)/shard_map/ppermute | solution.py:350
  14.9 3.6 %collective-permute-start.18 = (bf16[64,1024]{1,0:T(8,128)(2,1)S(1)}, bf16[64,1024]{1,0:T(8,128)(2,1)S(1)}, u32[]{:S(2)}, u32[]{:S(2)}) collective-permute-start(bf16[64,1024]{1,0:T(8,128)(2,1)S(1)} %pad_maximum_fusion.1), channel_id=1, source_target_pairs={{0,6},{1,7},{2,0},{3,1},{4,2},{5,3},{6,4},{7,5},{8,14},{9,15},{10,... | collective-permute-start | bytes 393224 | tf_op jit(solution)/shard_map/ppermute | solution.py:350
  20.7 4.8 %collective-permute-done.17 = bf16[64,1024]{1,0:T(8,128)(2,1)S(1)} collective-permute-done((bf16[64,1024]{1,0:T(8,128)(2,1)S(1)}, bf16[64,1024]{1,0:T(8,128)(2,1)S(1)}, u32[]{:S(2)}, u32[]{:S(2)}) %collective-permute-start.17) | collective-permute-done | bytes 131104 | tf_op jit(solution)/shard_map/ppermute | solution.py:350
  26.5 4.8 %collective-permute-done.19 = bf16[64,1024]{1,0:T(8,128)(2,1)S(1)} collective-permute-done((bf16[64,1024]{1,0:T(8,128)(2,1)S(1)}, bf16[64,1024]{1,0:T(8,128)(2,1)S(1)}, u32[]{:S(2)}, u32[]{:S(2)}) %collective-permute-start.19) | collective-permute-done | bytes 131104 | tf_op jit(solution)/shard_map/ppermute | solution.py:360
  33.1 4.3 %collective-permute-start.4 = (bf16[1024,128]{1,0:T(8,128)(2,1)}, bf16[1024,128]{1,0:T(8,128)(2,1)}, u32[]{:S(2)}, u32[]{:S(2)}) collective-permute-start(bf16[1024,128]{1,0:T(8,128)(2,1)} %collective-permute-done.3.refs_6_), channel_id=1, source_target_pairs={{0,1},{1,2},{2,3},{3,4},{4,5},{5,6},{6,7},{7,0},{8,9},{9,10},{10,1... | collective-permute-start | bytes 786440 | tf_op jit(solution)/shard_map/ppermute | solution.py:350
  44.8 3.0 %collective-permute-done.5.refs_8_ = bf16[1024,128]{1,0:T(8,128)(2,1)S(1)} collective-permute-done((bf16[1024,128]{1,0:T(8,128)(2,1)}, bf16[1024,128]{1,0:T(8,128)(2,1)S(1)}, u32[]{:S(2)}, u32[]{:S(2)}) %collective-permute-start.5) | collective-permute-done | bytes 262176 | tf_op jit(solution)/shard_map/ppermute | solution.py:350
  55.1 2.7 %attention.9.context_ref = bf16[128,128]{1,0:T(8,128)(2,1)S(1)} custom-call(s32[1]{0:T(128)} %bitcast.3.me_ref, s32[32,2]{1,0:T(8,128)S(1)} %reduce_window_sum.11.ends_ref, bf16[1024,128]{1,0:T(8,128)(2,1)} %refs_0_.4, bf16[1024,128]{1,0:T(8,128)(2,1)} %collective-permute-done.refs_1_, bf16[1024,128]{1,0:T(8,128)(2,1)} %collective-permute-done.1.refs_2_, ...), custom_call_target="tpu_custom_call" | custom-call | flops 5368709120 | bytes 3145728 | tf_op jit(solution)/shard_map/attention/pallas_call | solution.py:130
  58.1 3.0 %collective-permute-start.12 = (bf16[64,1024]{1,0:T(8,128)(2,1)S(1)}, bf16[64,1024]{1,0:T(8,128)(2,1)S(1)}, u32[]{:S(2)}, u32[]{:S(2)}) collective-permute-start(bf16[64,1024]{1,0:T(8,128)(2,1)S(1)} %get-tuple-element.15), channel_id=1, source_target_pairs={{0,7},{1,0},{2,1},{3,2},{4,3},{5,4},{6,5},{7,6},{8,15},{9,8},{10,9... | collective-permute-start | bytes 393224 | tf_op jit(solution)/shard_map/ppermute | solution.py:350
  61.1 3.6 %attention.8.context_ref = bf16[256,128]{1,0:T(8,128)(2,1)S(1)} custom-call(s32[1]{0:T(128)} %bitcast.3.me_ref, s32[32,2]{1,0:T(8,128)S(1)} %reduce_window_sum.11.ends_ref, bf16[1024,128]{1,0:T(8,128)(2,1)} %refs_0_.4, bf16[1024,128]{1,0:T(8,128)(2,1)} %collective-permute-done.refs_1_, bf16[1024,128]{1,0:T(8,128)(2,1)} %collective-permute-done.1.refs_2_, ...), custom_call_target="tpu_custom_call" | custom-call | flops 10737418240 | bytes 3145728 | tf_op jit(solution)/shard_map/attention/pallas_call | solution.py:130
  65.0 2.7 %collective-permute-start.13 = (bf16[128,1024]{1,0:T(8,128)(2,1)S(1)}, bf16[128,1024]{1,0:T(8,128)(2,1)S(1)}, u32[]{:S(2)}, u32[]{:S(2)}) collective-permute-start(bf16[128,1024]{1,0:T(8,128)(2,1)S(1)} %join.11), channel_id=1, source_target_pairs={{0,7},{1,0},{2,1},{3,2},{4,3},{5,4},{6,5},{7,6},{8,15},{9,8},{10,9... | collective-permute-start | bytes 786440 | tf_op jit(solution)/shard_map/ppermute | solution.py:350
  68.0 3.6 %attention.7.context_ref = bf16[256,128]{1,0:T(8,128)(2,1)S(1)} custom-call(s32[1]{0:T(128)} %bitcast.3.me_ref, s32[32,2]{1,0:T(8,128)S(1)} %reduce_window_sum.11.ends_ref, bf16[1024,128]{1,0:T(8,128)(2,1)} %refs_0_.4, bf16[1024,128]{1,0:T(8,128)(2,1)} %collective-permute-done.refs_1_, bf16[1024,128]{1,0:T(8,128)(2,1)} %collective-permute-done.1.refs_2_, ...), custom_call_target="tpu_custom_call" | custom-call | flops 10737418240 | bytes 3145728 | tf_op jit(solution)/shard_map/attention/pallas_call | solution.py:130
  71.9 3.2 %collective-permute-start.14 = (bf16[128,1024]{1,0:T(8,128)(2,1)S(1)}, bf16[128,1024]{1,0:T(8,128)(2,1)S(1)}, u32[]{:S(2)}, u32[]{:S(2)}) collective-permute-start(bf16[128,1024]{1,0:T(8,128)(2,1)S(1)} %join.12), channel_id=1, source_target_pairs={{0,7},{1,0},{2,1},{3,2},{4,3},{5,4},{6,5},{7,6},{8,15},{9,8},{10,9... | collective-permute-start | bytes 786440 | tf_op jit(solution)/shard_map/ppermute | solution.py:350
  75.4 3.6 %attention.6.context_ref = bf16[256,128]{1,0:T(8,128)(2,1)S(1)} custom-call(s32[1]{0:T(128)} %bitcast.3.me_ref, s32[32,2]{1,0:T(8,128)S(1)} %reduce_window_sum.11.ends_ref, bf16[1024,128]{1,0:T(8,128)(2,1)} %refs_0_.4, bf16[1024,128]{1,0:T(8,128)(2,1)} %collective-permute-done.refs_1_, bf16[1024,128]{1,0:T(8,128)(2,1)} %collective-permute-done.1.refs_2_, ...), custom_call_target="tpu_custom_call" | custom-call | flops 10737418240 | bytes 3145728 | tf_op jit(solution)/shard_map/attention/pallas_call | solution.py:130
  80.4 3.6 %collective-permute-start.15 = (bf16[128,1024]{1,0:T(8,128)(2,1)S(1)}, bf16[128,1024]{1,0:T(8,128)(2,1)S(1)}, u32[]{:S(2)}, u32[]{:S(2)}) collective-permute-start(bf16[128,1024]{1,0:T(8,128)(2,1)S(1)} %join.13), channel_id=1, source_target_pairs={{0,7},{1,0},{2,1},{3,2},{4,3},{5,4},{6,5},{7,6},{8,15},{9,8},{10,9... | collective-permute-start | bytes 786440 | tf_op jit(solution)/shard_map/ppermute | solution.py:350
  85.8 2.9 %attention.5.base_ref = f32[128,1024]{1,0:T(8,128)S(1)} custom-call(s32[1]{0:T(128)} %bitcast.3.me_ref, s32[32,2]{1,0:T(8,128)S(1)} %reduce_window_sum.11.ends_ref, bf16[1024,128]{1,0:T(8,128)(2,1)} %refs_0_.4, bf16[1024,128]{1,0:T(8,128)(2,1)} %collective-permute-done.refs_1_, bf16[1024,128]{1,0:T(8,128)(2,1)} %collective-permute-done.1.refs_2_, ...), custom_call_target="tpu_custom_call" | custom-call | flops 5368709120 | bytes 3145728 | tf_op jit(solution)/shard_map/attention/pallas_call | solution.py:130
  89.9 4.2 %collective-permute-done.11.right_ref = bf16[128,1024]{1,0:T(8,128)(2,1)S(1)} collective-permute-done((bf16[128,1024]{1,0:T(8,128)(2,1)S(1)}, bf16[128,1024]{1,0:T(8,128)(2,1)S(1)}, u32[]{:S(2)}, u32[]{:S(2)}) %collective-permute-start.11) | collective-permute-done | bytes 262176 | tf_op jit(solution)/shard_map/ppermute | solution.py:350
  94.8 5.7 %collective-permute-done.16.pair_ref = bf16[128,1024]{1,0:T(8,128)(2,1)S(1)} collective-permute-done((bf16[128,1024]{1,0:T(8,128)(2,1)S(1)}, bf16[128,1024]{1,0:T(8,128)(2,1)S(1)}, u32[]{:S(2)}, u32[]{:S(2)}) %collective-permute-start.16) | collective-permute-done | bytes 262176 | tf_op jit(solution)/shard_map/ppermute | solution.py:353
  103.7 8.2 %feed.1 = (f32[128,1024]{1,0:T(8,128)S(1)}, bf16[128,1024]{1,0:T(8,128)(2,1)}) custom-call(bf16[128,1024]{1,0:T(8,128)(2,1)S(1)} %get-tuple-element.16.own_ref, bf16[128,1024]{1,0:T(8,128)(2,1)S(1)} %copy-done.3, f32[128,1024]{1,0:T(8,128)S(1)} %get-tuple-element.17.hidden_ref, bf16[1024,1024]{1,0:T(8,128)(2,1)} %up_ref.1, bf16[1024,1024]{1,0:T(8,128)(2,1)} %down_ref.1, ...), custom_call_target="tpu_custom_call" | custom-call | flops 4294967296 | bytes 16777216 | tf_op jit(solution)/shard_map/feed/pallas_call | solution.py:205
  113.7 3.8 %collective-permute-done.20.pair_ref = bf16[128,1024]{1,0:T(8,128)(2,1)S(1)} collective-permute-done((bf16[128,1024]{1,0:T(8,128)(2,1)}, bf16[128,1024]{1,0:T(8,128)(2,1)S(1)}, u32[]{:S(2)}, u32[]{:S(2)}) %collective-permute-start.20) | collective-permute-done | bytes 262176 | tf_op jit(solution)/shard_map/ppermute | solution.py:353
  118.7 6.7 %all-to-all-start = ((f32[8,8,1024]{2,1,0:T(8,128)}), f32[8,8,1024]{2,1,0:T(8,128)S(1)}, u32[]{:S(2)}, u32[]{:S(2)}) async-start(f32[8,8,1024]{2,1,0:T(8,128)} %pool.1), calls=%async_computation | async-start | bytes 524288 | tf_op jit(solution)/shard_map/all_to_all | solution.py:439
  125.6 5.7 %collective-permute-start.21 = (s32[1,64]{1,0:T(1,128)S(1)}, s32[1,64]{1,0:T(1,128)S(1)}, u32[]{:S(2)}, u32[]{:S(2)}) collective-permute-start(s32[1,64]{1,0:T(1,128)S(1)} %concatenate.36), channel_id=1, source_target_pairs={{0,8},{8,0},{16,24},{24,16},{32,40},{40,32},{48,56},{56,48},{64,72... | collective-permute-start | bytes 776 | tf_op jit(solution)/shard_map/ppermute | solution.py:384
  134.7 8.6 %all_gather.7.pooled_ref = f32[16,8,1024]{2,1,0:T(8,128)S(1)} all-gather(f32[8,8,1024]{2,1,0:T(8,128)S(1)} %all-to-all-done), channel_id=1, replica_groups={{0,8},{16,24},{32,40},{48,56},{64,72},{80,88},{96,104},{112,120},{128,1..., dimensions={0}, use_global_device_ids=true | all-gather | bytes 786432 | tf_op jit(solution)/shard_map/all_gather | solution.py:440
  145.7 6.6 %all-to-all-start.1 = ((bf16[16,8,1024]{2,1,0:T(8,128)(2,1)}), bf16[16,8,1024]{2,1,0:T(8,128)(2,1)S(1)}, u32[]{:S(2)}, u32[]{:S(2)}) async-start(bf16[16,8,1024]{2,1,0:T(8,128)(2,1)} %bitcast.6), calls=%async_computation.1 | async-start | bytes 524288 | tf_op jit(solution)/shard_map/all_to_all | solution.py:450
  152.3 8.1 %all-to-all-done.1 = bf16[16,8,1024]{2,1,0:T(8,128)(2,1)S(1)} async-done(((bf16[16,8,1024]{2,1,0:T(8,128)(2,1)}), bf16[16,8,1024]{2,1,0:T(8,128)(2,1)S(1)}, u32[]{:S(2)}, u32[]{:S(2)}) %all-to-all-start.1) | async-done | bytes 262176 | tf_op jit(solution)/shard_map/all_to_all | solution.py:450
  (99 shorter events, 43.5 us)
Async XLA Ops:
  7.2 95.5 %all-gather.2.cloned.1.call-start = ((), (), s32[]{:S(2)}) async-start(), calls=%async_computation.2 | async-start | bytes 12976128 | tf_op jit(solution)/shard_map/all_gather | solution.py:403
  8.3 23.0 %collective-permute-start.3 = (bf16[1024,128]{1,0:T(8,128)(2,1)}, bf16[1024,128]{1,0:T(8,128)(2,1)}, u32[]{:S(2)}, u32[]{:S(2)}) collective-permute-start(bf16[1024,128]{1,0:T(8,128)(2,1)} %refs_0_.4), channel_id=1, source_target_pairs={{0,1},{1,2},{2,3},{3,4},{4,5},{5,6},{6,7},{7,0},{8,9},{9,10},{10,1... | collective-permute-start | bytes 786440 | tf_op jit(solution)/shard_map/ppermute | solution.py:350
  10.9 20.5 %collective-permute-start = (bf16[1024,128]{1,0:T(8,128)(2,1)}, bf16[1024,128]{1,0:T(8,128)(2,1)}, u32[]{:S(2)}, u32[]{:S(2)}) collective-permute-start(bf16[1024,128]{1,0:T(8,128)(2,1)} %refs_0_.4), channel_id=1, source_target_pairs={{0,7},{1,0},{2,1},{3,2},{4,3},{5,4},{6,5},{7,6},{8,15},{9,8},{10,9... | collective-permute-start | bytes 786440 | tf_op jit(solution)/shard_map/ppermute | solution.py:350
  14.9 10.7 %collective-permute-start.17 = (bf16[64,1024]{1,0:T(8,128)(2,1)S(1)}, bf16[64,1024]{1,0:T(8,128)(2,1)S(1)}, u32[]{:S(2)}, u32[]{:S(2)}) collective-permute-start(bf16[64,1024]{1,0:T(8,128)(2,1)S(1)} %pad_maximum_fusion.1), channel_id=1, source_target_pairs={{0,2},{1,3},{2,4},{3,5},{4,6},{5,7},{6,0},{7,1},{8,10},{9,11},{10,... | collective-permute-start | bytes 393224 | tf_op jit(solution)/shard_map/ppermute | solution.py:350
  14.9 11.6 %collective-permute-start.18 = (bf16[64,1024]{1,0:T(8,128)(2,1)S(1)}, bf16[64,1024]{1,0:T(8,128)(2,1)S(1)}, u32[]{:S(2)}, u32[]{:S(2)}) collective-permute-start(bf16[64,1024]{1,0:T(8,128)(2,1)S(1)} %pad_maximum_fusion.1), channel_id=1, source_target_pairs={{0,6},{1,7},{2,0},{3,1},{4,2},{5,3},{6,4},{7,5},{8,14},{9,15},{10,... | collective-permute-start | bytes 393224 | tf_op jit(solution)/shard_map/ppermute | solution.py:350
  18.5 12.8 %collective-permute-start.19 = (bf16[64,1024]{1,0:T(8,128)(2,1)S(1)}, bf16[64,1024]{1,0:T(8,128)(2,1)S(1)}, u32[]{:S(2)}, u32[]{:S(2)}) collective-permute-start(bf16[64,1024]{1,0:T(8,128)(2,1)S(1)} %pad_maximum_fusion.1), channel_id=1, source_target_pairs={{0,5},{1,4},{2,7},{3,6},{4,1},{5,0},{6,3},{7,2},{8,13},{9,12},{10,... | collective-permute-start | bytes 393224 | tf_op jit(solution)/shard_map/ppermute | solution.py:360
  33.1 8.1 %collective-permute-start.4 = (bf16[1024,128]{1,0:T(8,128)(2,1)}, bf16[1024,128]{1,0:T(8,128)(2,1)}, u32[]{:S(2)}, u32[]{:S(2)}) collective-permute-start(bf16[1024,128]{1,0:T(8,128)(2,1)} %collective-permute-done.3.refs_6_), channel_id=1, source_target_pairs={{0,1},{1,2},{2,3},{3,4},{4,5},{5,6},{6,7},{7,0},{8,9},{9,10},{10,1... | collective-permute-start | bytes 786440 | tf_op jit(solution)/shard_map/ppermute | solution.py:350
  37.5 6.0 %collective-permute-start.1 = (bf16[1024,128]{1,0:T(8,128)(2,1)}, bf16[1024,128]{1,0:T(8,128)(2,1)}, u32[]{:S(2)}, u32[]{:S(2)}) collective-permute-start(bf16[1024,128]{1,0:T(8,128)(2,1)} %collective-permute-done.refs_1_), channel_id=1, source_target_pairs={{0,7},{1,0},{2,1},{3,2},{4,3},{5,4},{6,5},{7,6},{8,15},{9,8},{10,9... | collective-permute-start | bytes 786440 | tf_op jit(solution)/shard_map/ppermute | solution.py:350
  41.2 6.6 %collective-permute-start.5 = (bf16[1024,128]{1,0:T(8,128)(2,1)}, bf16[1024,128]{1,0:T(8,128)(2,1)S(1)}, u32[]{:S(2)}, u32[]{:S(2)}) collective-permute-start(bf16[1024,128]{1,0:T(8,128)(2,1)} %collective-permute-done.4.refs_7_), channel_id=1, source_target_pairs={{0,1},{1,2},{2,3},{3,4},{4,5},{5,6},{6,7},{7,0},{8,9},{9,10},{10,1... | collective-permute-start | bytes 786440 | tf_op jit(solution)/shard_map/ppermute | solution.py:350
  43.4 5.7 %collective-permute-start.2 = (bf16[1024,128]{1,0:T(8,128)(2,1)}, bf16[1024,128]{1,0:T(8,128)(2,1)}, u32[]{:S(2)}, u32[]{:S(2)}) collective-permute-start(bf16[1024,128]{1,0:T(8,128)(2,1)} %collective-permute-done.1.refs_2_), channel_id=1, source_target_pairs={{0,7},{1,0},{2,1},{3,2},{4,3},{5,4},{6,5},{7,6},{8,15},{9,8},{10,9... | collective-permute-start | bytes 786440 | tf_op jit(solution)/shard_map/ppermute | solution.py:350
  47.9 5.6 %collective-permute-start.6 = (bf16[512,128]{1,0:T(8,128)(2,1)S(1)}, bf16[512,128]{1,0:T(8,128)(2,1)S(1)}, u32[]{:S(2)}, u32[]{:S(2)}) collective-permute-start(bf16[512,128]{1,0:T(8,128)(2,1)S(1)} %slice.8), channel_id=1, source_target_pairs={{0,1},{1,2},{2,3},{3,4},{4,5},{5,6},{6,7},{7,0},{8,9},{9,10},{10,1... | collective-permute-start | bytes 393224 | tf_op jit(solution)/shard_map/ppermute | solution.py:350
  58.1 6.6 %collective-permute-start.12 = (bf16[64,1024]{1,0:T(8,128)(2,1)S(1)}, bf16[64,1024]{1,0:T(8,128)(2,1)S(1)}, u32[]{:S(2)}, u32[]{:S(2)}) collective-permute-start(bf16[64,1024]{1,0:T(8,128)(2,1)S(1)} %get-tuple-element.15), channel_id=1, source_target_pairs={{0,7},{1,0},{2,1},{3,2},{4,3},{5,4},{6,5},{7,6},{8,15},{9,8},{10,9... | collective-permute-start | bytes 393224 | tf_op jit(solution)/shard_map/ppermute | solution.py:350
  61.1 6.6 %collective-permute-start.8 = (bf16[64,1024]{1,0:T(8,128)(2,1)S(1)}, bf16[64,1024]{1,0:T(8,128)(2,1)S(1)}, u32[]{:S(2)}, u32[]{:S(2)}) collective-permute-start(bf16[64,1024]{1,0:T(8,128)(2,1)S(1)} %get-tuple-element.14), channel_id=1, source_target_pairs={{0,1},{1,2},{2,3},{3,4},{4,5},{5,6},{6,7},{7,0},{8,9},{9,10},{10,1... | collective-permute-start | bytes 393224 | tf_op jit(solution)/shard_map/ppermute | solution.py:350
  65.0 6.7 %collective-permute-start.13 = (bf16[128,1024]{1,0:T(8,128)(2,1)S(1)}, bf16[128,1024]{1,0:T(8,128)(2,1)S(1)}, u32[]{:S(2)}, u32[]{:S(2)}) collective-permute-start(bf16[128,1024]{1,0:T(8,128)(2,1)S(1)} %join.11), channel_id=1, source_target_pairs={{0,7},{1,0},{2,1},{3,2},{4,3},{5,4},{6,5},{7,6},{8,15},{9,8},{10,9... | collective-permute-start | bytes 786440 | tf_op jit(solution)/shard_map/ppermute | solution.py:350
  67.9 7.1 %collective-permute-start.9 = (bf16[128,1024]{1,0:T(8,128)(2,1)S(1)}, bf16[128,1024]{1,0:T(8,128)(2,1)S(1)}, u32[]{:S(2)}, u32[]{:S(2)}) collective-permute-start(bf16[128,1024]{1,0:T(8,128)(2,1)S(1)} %join.8), channel_id=1, source_target_pairs={{0,1},{1,2},{2,3},{3,4},{4,5},{5,6},{6,7},{7,0},{8,9},{9,10},{10,1... | collective-permute-start | bytes 786440 | tf_op jit(solution)/shard_map/ppermute | solution.py:350
  71.9 8.3 %collective-permute-start.14 = (bf16[128,1024]{1,0:T(8,128)(2,1)S(1)}, bf16[128,1024]{1,0:T(8,128)(2,1)S(1)}, u32[]{:S(2)}, u32[]{:S(2)}) collective-permute-start(bf16[128,1024]{1,0:T(8,128)(2,1)S(1)} %join.12), channel_id=1, source_target_pairs={{0,7},{1,0},{2,1},{3,2},{4,3},{5,4},{6,5},{7,6},{8,15},{9,8},{10,9... | collective-permute-start | bytes 786440 | tf_op jit(solution)/shard_map/ppermute | solution.py:350
  75.3 9.0 %collective-permute-start.10 = (bf16[128,1024]{1,0:T(8,128)(2,1)S(1)}, bf16[128,1024]{1,0:T(8,128)(2,1)S(1)}, u32[]{:S(2)}, u32[]{:S(2)}) collective-permute-start(bf16[128,1024]{1,0:T(8,128)(2,1)S(1)} %join.9), channel_id=1, source_target_pairs={{0,1},{1,2},{2,3},{3,4},{4,5},{5,6},{6,7},{7,0},{8,9},{9,10},{10,1... | collective-permute-start | bytes 786440 | tf_op jit(solution)/shard_map/ppermute | solution.py:350
  80.4 9.5 %collective-permute-start.15 = (bf16[128,1024]{1,0:T(8,128)(2,1)S(1)}, bf16[128,1024]{1,0:T(8,128)(2,1)S(1)}, u32[]{:S(2)}, u32[]{:S(2)}) collective-permute-start(bf16[128,1024]{1,0:T(8,128)(2,1)S(1)} %join.13), channel_id=1, source_target_pairs={{0,7},{1,0},{2,1},{3,2},{4,3},{5,4},{6,5},{7,6},{8,15},{9,8},{10,9... | collective-permute-start | bytes 786440 | tf_op jit(solution)/shard_map/ppermute | solution.py:350
  84.5 9.6 %collective-permute-start.11 = (bf16[128,1024]{1,0:T(8,128)(2,1)S(1)}, bf16[128,1024]{1,0:T(8,128)(2,1)S(1)}, u32[]{:S(2)}, u32[]{:S(2)}) collective-permute-start(bf16[128,1024]{1,0:T(8,128)(2,1)S(1)} %join.10), channel_id=1, source_target_pairs={{0,1},{1,2},{2,3},{3,4},{4,5},{5,6},{6,7},{7,0},{8,9},{9,10},{10,1... | collective-permute-start | bytes 786440 | tf_op jit(solution)/shard_map/ppermute | solution.py:350
  94.4 6.1 %collective-permute-start.16 = (bf16[128,1024]{1,0:T(8,128)(2,1)S(1)}, bf16[128,1024]{1,0:T(8,128)(2,1)S(1)}, u32[]{:S(2)}, u32[]{:S(2)}) collective-permute-start(bf16[128,1024]{1,0:T(8,128)(2,1)S(1)} %get-tuple-element.16.own_ref), channel_id=1, source_target_pairs={{0,1},{1,0},{2,3},{3,2},{4,5},{5,4},{6,7},{7,6},{8,9},{9,8},{10,11... | collective-permute-start | bytes 786440 | tf_op jit(solution)/shard_map/ppermute | solution.py:353
  111.9 5.5 %collective-permute-start.20 = (bf16[128,1024]{1,0:T(8,128)(2,1)}, bf16[128,1024]{1,0:T(8,128)(2,1)S(1)}, u32[]{:S(2)}, u32[]{:S(2)}) collective-permute-start(bf16[128,1024]{1,0:T(8,128)(2,1)} %get-tuple-element.23), channel_id=1, source_target_pairs={{0,1},{1,0},{2,3},{3,2},{4,5},{5,4},{6,7},{7,6},{8,9},{9,8},{10,11... | collective-permute-start | bytes 786440 | tf_op jit(solution)/shard_map/ppermute | solution.py:353
  118.7 16.0 %all-to-all-start = ((f32[8,8,1024]{2,1,0:T(8,128)}), f32[8,8,1024]{2,1,0:T(8,128)S(1)}, u32[]{:S(2)}, u32[]{:S(2)}) async-start(f32[8,8,1024]{2,1,0:T(8,128)} %pool.1), calls=%async_computation | async-start | bytes 524288 | tf_op jit(solution)/shard_map/all_to_all | solution.py:439
  125.6 6.5 %collective-permute-start.21 = (s32[1,64]{1,0:T(1,128)S(1)}, s32[1,64]{1,0:T(1,128)S(1)}, u32[]{:S(2)}, u32[]{:S(2)}) collective-permute-start(s32[1,64]{1,0:T(1,128)S(1)} %concatenate.36), channel_id=1, source_target_pairs={{0,8},{8,0},{16,24},{24,16},{32,40},{40,32},{48,56},{56,48},{64,72... | collective-permute-start | bytes 776 | tf_op jit(solution)/shard_map/ppermute | solution.py:384
  145.7 14.7 %all-to-all-start.1 = ((bf16[16,8,1024]{2,1,0:T(8,128)(2,1)}), bf16[16,8,1024]{2,1,0:T(8,128)(2,1)S(1)}, u32[]{:S(2)}, u32[]{:S(2)}) async-start(bf16[16,8,1024]{2,1,0:T(8,128)(2,1)} %bitcast.6), calls=%async_computation.1 | async-start | bytes 524288 | tf_op jit(solution)/shard_map/all_to_all | solution.py:450
  (14 other events, 337.3 us)
Sparse Core Ops, SparseCore 0:
  32.3 70.4 all-gather.1

commit v5 on v4

--- a/solution.py
+++ b/solution.py
@@ -43,7 +43,8 @@
 
 
 def attention_kernel(offsets, parts, chunk, with_base, me_ref, ends_ref, *refs):
-    pieces, (w_ref, wo_ref), (out_ref, rows_ref, sems) = refs[:parts + 1], refs[parts + 1:parts + 3], refs[parts + 3:]
+    pieces, (wq_ref, wk_ref, wv_ref, wo_ref), rest = refs[:parts + 1], refs[parts + 1:parts + 5], refs[parts + 5:]
+    out_ref, rows_ref, sems = rest
     me = me_ref[0]
     half = parts // 2
     part = pieces[0].shape[1]
@@ -80,19 +81,21 @@
     count = len(offsets)
     rows = rows_ref[...].reshape(count * chunk, -1).astype(F32)
     normed = normalize(rows).astype(BF)
-    projected = dot(normed, w_ref[...]).astype(BF)
+    w_qkv = jnp.concatenate([wq_ref[...], wk_ref[...], wv_ref[...]], axis=1)
+    projected = dot(normed, w_qkv).astype(BF)
     local = wo_ref.shape[0]
-    block_rows = chunk * parts // ends_ref.shape[0]
+    block_rows = chunk * parts // ends_ref.shape[1]
     blocks = chunk // block_rows
-    per_block = ends_ref.shape[1]
+    per_block = ends_ref.shape[0]
 
     def keys(c, shape, axis):
         row = lax.broadcasted_iota(jnp.int32, shape, axis)
         block = row // block_rows
         key = block * per_block
         for b in range(blocks):
+            end = b * block_rows
             for e in range(per_block - 1):
-                end = ends_ref[c * blocks + b, e] + b * block_rows
+                end = end + ends_ref[e, c * blocks + b]
                 key = key + jnp.where((block == b) & (row >= end), 1, 0)
         return key
 
@@ -117,7 +120,7 @@
         out_ref[...] = context
 
 
-def attention(pieces, w_qkv, w_out, ends, me, offsets, with_base=False):
+def attention(pieces, weights, w_out, ends, me, offsets, with_base=False):
     parts = len(pieces) - 1
     count, part = pieces[0].shape
     chunk = count // parts
@@ -129,14 +132,14 @@
     pieces = [pltpu.with_memory_space_constraint(p, pltpu.HBM) for p in pieces]
     return pl.pallas_call(
         functools.partial(attention_kernel, offsets, parts, chunk, with_base),
-        in_specs=[smem, smem] + [hbm] * len(pieces) + [vmem] * 2,
+        in_specs=[smem, smem] + [hbm] * len(pieces) + [vmem] * 4,
         out_specs=vmem,
         out_shape=jax.ShapeDtypeStruct((size * chunk, width if with_base else local), F32 if with_base else BF),
         scratch_shapes=[pltpu.VMEM((size, chunk, width), BF), pltpu.SemaphoreType.DMA((size, parts))],
         compiler_params=pltpu.CompilerParams(vmem_limit_bytes=16 << 20),
         cost_estimate=cost(40 * size * 2 * chunk * width * 4 * local, 3 << 20),
         name="attention",
-    )(me, ends, *pieces, w_qkv, w_out)
+    )(me, ends, *pieces, *weights, w_out)
 
 
 def first_join_kernel(context_ref, wo_ref, right_ref, left_ref):
@@ -162,8 +165,8 @@
     normed_ref[...] = normalize(hidden).astype(BF)
 
 
-def feed_kernel(own_ref, pair_ref, hidden_ref, up_ref, down_ref, gathered_ref, out_ref, send_ref, ups, downs, sems):
-    count = own_ref.shape[0]
+def feed_kernel(rows_ref, *refs):
+    (up_ref, down_ref, gathered_ref, out_ref, ups, downs, sems), hidden = refs[-7:], refs[:-7]
     planes = gathered_ref.shape[1]
     rows = gathered_ref.shape[2] // 2
     copies = [(pltpu.make_async_copy(up_ref, ups.at[0], sems.at[0, 0]),
@@ -181,22 +184,20 @@
     for up, down in copies:
         up.start()
         down.start()
-    both = jnp.concatenate([own_ref[...], pair_ref[...]], axis=0)
-    total = None
+    normed = rows_ref[...]
+    total = hidden[0][...] if hidden else None
     for p, (up, down) in enumerate(copies):
         up.wait()
-        inner = jnp.maximum(dot(both, ups[p]), 0.0).astype(BF)
+        inner = jnp.maximum(dot(normed, ups[p]), 0.0).astype(BF)
         down.wait()
         part = dot(inner, downs[p])
         total = part if total is None else total + part
-    out_ref[...] = hidden_ref[...] + total[:count]
-    send_ref[...] = total[count:].astype(BF)
-
-
-def feed(own, pair, hidden1, w_up, w_down, gathered):
+    out_ref[...] = total.astype(out_ref.dtype)
+
+
+def feed(normed, hidden, w_up, w_down, gathered):
     planes = gathered.shape[1]
-    count, width = own.shape
-    hidden = w_up.shape[1]
+    count, width = normed.shape
     vmem = pl.BlockSpec(memory_space=pltpu.VMEM)
     hbm = pl.BlockSpec(memory_space=pltpu.HBM)
     w_up, w_down, gathered = (
@@ -204,18 +205,20 @@
     )
     return pl.pallas_call(
         feed_kernel,
-        in_specs=[vmem, vmem, vmem, hbm, hbm, hbm],
-        out_specs=[vmem, vmem],
-        out_shape=[jax.ShapeDtypeStruct(own.shape, F32), jax.ShapeDtypeStruct(own.shape, BF)],
+        in_specs=[vmem] * (1 + len(hidden)) + [hbm] * 3,
+        out_specs=vmem,
+        out_shape=jax.ShapeDtypeStruct(normed.shape, F32 if hidden else BF),
         scratch_shapes=[
             pltpu.VMEM((planes + 1,) + w_up.shape, BF),
             pltpu.VMEM((planes + 1,) + w_down.shape, BF),
             pltpu.SemaphoreType.DMA((planes + 1, 2)),
         ],
         compiler_params=pltpu.CompilerParams(vmem_limit_bytes=24 << 20),
-        cost_estimate=cost(8 * count * width * hidden * (planes + 1), 4 * (planes + 1) * width * hidden),
+        cost_estimate=cost(
+            4 * count * width * w_up.shape[1] * (planes + 1), 4 * (planes + 1) * width * w_up.shape[1]
+        ),
         name="feed",
-    )(own, pair, hidden1, w_up, w_down, gathered)
+    )(normed, *hidden, w_up, w_down, gathered)
 
 
 def pool_kernel(hidden_ref, pair_ref, gain_ref, member_ref, length_ref, out_ref):
@@ -384,7 +387,6 @@
     other = lax.ppermute(code, "dp", [(i, i ^ 1) for i in range(dp_count)])
     core = dp_at % CORES
     code = jnp.where(core == 0, jnp.concatenate((code, other), axis=1), jnp.concatenate((other, code), axis=1))
-    w_qkv = jnp.concatenate((w_query, w_key, w_value), axis=1)
     columns = width // sub_count
     proj = lax.dynamic_slice_in_dim(projection, sub_at * columns, columns, 1)
 
@@ -403,7 +405,7 @@
     gathered = lax.all_gather(jnp.concatenate(others, axis=0), "dp", axis=0, tiled=True)
     gathered = gathered.reshape(dp_count, planes, 2 * rows, width)
 
-    attend = functools.partial(attention, pieces, w_qkv, w_out, ends, sub_at.reshape(1))
+    attend = functools.partial(attention, pieces, (w_query, w_key, w_value), w_out, lengths.T, sub_at.reshape(1))
     own_shape = (own_rows, width)
     half_shape = (own_rows // 2, width)
     right, left = small_call(
@@ -429,7 +431,8 @@
         (base, right, left),
         name="middle",
     )
-    hidden2, sent = feed(normed2, swap(normed2), hidden1, w_up, w_down, gathered)
+    sent = feed(swap(normed2), (), w_up, w_down, gathered)
+    hidden2 = feed(normed2, (hidden1,), w_up, w_down, gathered)
     pooled = small_call(
         pool_kernel,
         jax.ShapeDtypeStruct((sub_count, own_sentences, width), F32),

time: 170 us -> 166 us (0.976)
  waiting for transfers between devices: 46.6 us -> 56.8 us
  starting transfers between devices: 57 us -> 47.7 us
  local copies, waits for them, and re-layouts: 8.88 us -> 3.2 us
  blocking collectives: 8.56 us -> 4.96 us
  Pallas kernels: 32.2 us -> 35.4 us
    ppermute x18, waiting for transfers between devices: 19.5 us -> 26 us  [move(): lax.ppermute(array, 'sub', [(i, (i + by) % sub_count) for i in range(sub_...]
    unnamed x29 -> x24, local copies, waits for them, and re-layouts: 5.33 us -> 0.74 us
    pallas_call x1 -> x2, Pallas kernels: 8.24 us -> 12.7 us  [feed(): pl.pallas_call(feed_kernel, in_specs=[vmem] * (1 + len(hidden)) + [hbm] *...]
    all_to_all x1, waiting for transfers between devices: 2.56 us -> 6.78 us  [on_device(): lax.all_to_all(pooled, 'sub', split_axis=0, concat_axis=0, tiled=True)]
    ppermute x18, starting transfers between devices: 34 us -> 29.9 us  [move(): lax.ppermute(array, 'sub', [(i, (i + by) % sub_count) for i in range(sub_...]
    ppermute x1, starting transfers between devices: 5.7 us -> 1.81 us  [on_device(): other = lax.ppermute(code, 'dp', [(i, i ^ 1) for i in range(dp_count)])]
    all_gather x1, waiting for transfers between devices: 1.43 us -> 5.03 us  [on_device(): lax.all_gather(jnp.concatenate(others, axis=0), 'dp', axis=0, tiled=True)]
    all_gather x1, blocking collectives: 8.56 us -> 4.96 us  [on_device(): lax.all_gather(pooled, 'dp', axis=0, tiled=True, axis_index_groups=siblings)]
  transfers between devices with their start and end apart: 25 -> 25, of which waited for: 17 -> 15; matrix products, arithmetic and copies ran while one was open for 3% -> 2% of each run, Pallas kernels for 11% -> 14%
where the time goes in v5:
time: 166 us; the launch traced here: 165 us
  waiting for transfers between devices  56.8 us (34%)
  starting transfers between devices  47.7 us (29%)
  Pallas kernels  35.4 us (21%)
  between operations  14.4 us (9%)
  blocking collectives  4.96 us (3%)
  local copies, waits for them, and re-layouts  3.2 us (2%)
  other arithmetic  3.03 us (2%)
    ppermute x18, starting transfers between devices, move(): lax.ppermute(array, 'sub', [(i, (i + by) % sub_count) for i in range(sub_...  29.9 us
    ppermute x18, waiting for transfers between devices, move(): lax.ppermute(array, 'sub', [(i, (i + by) % sub_count) for i in range(sub_...  26 us
    pallas_call x5, Pallas kernels, attention(): pl.pallas_call(functools.partial(attention_kernel, offsets, parts, chunk,...  15.2 us
    pallas_call x2, Pallas kernels, feed(): pl.pallas_call(feed_kernel, in_specs=[vmem] * (1 + len(hidden)) + [hbm] *...  12.7 us
    all_to_all x1, waiting for transfers between devices, on_device(): lax.all_to_all(sent.reshape(chips, PACK, width), 'dp', split_axis=0, conc...  8.11 us
    pallas_call x11, Pallas kernels, small_call(): pl.pallas_call(kernel, in_specs=specs, out_specs=pl.BlockSpec(memory_spac...  7.39 us
    ppermute x2, waiting for transfers between devices, swap(): return lax.ppermute(array, 'sub', [(i, i ^ 1) for i in range(sub_count)])  7.33 us
    all_to_all x1, waiting for transfers between devices, on_device(): lax.all_to_all(pooled, 'sub', split_axis=0, concat_axis=0, tiled=True)  6.78 us
  transfers between devices with their start and end apart: 25, of which 15 were waited for; matrix products, arithmetic and copies ran while one was open for 2% of the time, Pallas kernels for 14%

profile of v5, /device:TPU:1, one launch (start us, length us, event | category | flops | bytes accessed | tf_op | source)
XLA Modules:
  0.0 165.4 jit_solution(6881397190984358723)
XLA Ops:
  8.4 6.5 %collective-permute-start = (bf16[1024,128]{1,0:T(8,128)(2,1)}, bf16[1024,128]{1,0:T(8,128)(2,1)S(1)}, u32[]{:S(2)}, u32[]{:S(2)}) collective-permute-start(bf16[1024,128]{1,0:T(8,128)(2,1)} %refs_0_.5), channel_id=1, source_target_pairs={{0,7},{1,0},{2,1},{3,2},{4,3},{5,4},{6,5},{7,6},{8,15},{9,8},{10,9... | collective-permute-start | bytes 786440 | tf_op jit(solution)/shard_map/ppermute | solution.py:353
  14.8 3.6 %collective-permute-start.17 = (bf16[64,1024]{1,0:T(8,128)(2,1)S(1)}, bf16[64,1024]{1,0:T(8,128)(2,1)S(1)}, u32[]{:S(2)}, u32[]{:S(2)}) collective-permute-start(bf16[64,1024]{1,0:T(8,128)(2,1)S(1)} %pad_maximum_fusion.1), channel_id=1, source_target_pairs={{0,6},{1,7},{2,0},{3,1},{4,2},{5,3},{6,4},{7,5},{8,14},{9,15},{10,... | collective-permute-start | bytes 393224 | tf_op jit(solution)/shard_map/ppermute | solution.py:353
  20.8 5.2 %collective-permute-done.16 = bf16[64,1024]{1,0:T(8,128)(2,1)S(1)} collective-permute-done((bf16[64,1024]{1,0:T(8,128)(2,1)S(1)}, bf16[64,1024]{1,0:T(8,128)(2,1)S(1)}, u32[]{:S(2)}, u32[]{:S(2)}) %collective-permute-start.16) | collective-permute-done | bytes 131104 | tf_op jit(solution)/shard_map/ppermute | solution.py:353
  28.4 2.8 %collective-permute-done.18 = bf16[64,1024]{1,0:T(8,128)(2,1)S(1)} collective-permute-done((bf16[64,1024]{1,0:T(8,128)(2,1)S(1)}, bf16[64,1024]{1,0:T(8,128)(2,1)S(1)}, u32[]{:S(2)}, u32[]{:S(2)}) %collective-permute-start.18) | collective-permute-done | bytes 131104 | tf_op jit(solution)/shard_map/ppermute | solution.py:363
  36.7 2.9 %collective-permute-done.1.refs_2_ = bf16[1024,128]{1,0:T(8,128)(2,1)} collective-permute-done((bf16[1024,128]{1,0:T(8,128)(2,1)S(1)}, bf16[1024,128]{1,0:T(8,128)(2,1)}, u32[]{:S(2)}, u32[]{:S(2)}) %collective-permute-start.1) | collective-permute-done | bytes 262176 | tf_op jit(solution)/shard_map/ppermute | solution.py:353
  42.0 6.6 %collective-permute-done.5.refs_8_ = bf16[1024,128]{1,0:T(8,128)(2,1)} collective-permute-done((bf16[1024,128]{1,0:T(8,128)(2,1)}, bf16[1024,128]{1,0:T(8,128)(2,1)}, u32[]{:S(2)}, u32[]{:S(2)}) %collective-permute-start.5) | collective-permute-done | bytes 262176 | tf_op jit(solution)/shard_map/ppermute | solution.py:353
  49.7 2.7 %collective-permute-start.7 = (bf16[512,128]{1,0:T(8,128)(2,1)S(1)}, bf16[512,128]{1,0:T(8,128)(2,1)S(1)}, u32[]{:S(2)}, u32[]{:S(2)}) collective-permute-start(bf16[512,128]{1,0:T(8,128)(2,1)S(1)} %slice.9), channel_id=1, source_target_pairs={{0,7},{1,0},{2,1},{3,2},{4,3},{5,4},{6,5},{7,6},{8,15},{9,8},{10,9... | collective-permute-start | bytes 393224 | tf_op jit(solution)/shard_map/ppermute | solution.py:353
  58.2 2.8 %collective-permute-start.12 = (bf16[64,1024]{1,0:T(8,128)(2,1)S(1)}, bf16[64,1024]{1,0:T(8,128)(2,1)S(1)}, u32[]{:S(2)}, u32[]{:S(2)}) collective-permute-start(bf16[64,1024]{1,0:T(8,128)(2,1)S(1)} %get-tuple-element.13), channel_id=1, source_target_pairs={{0,7},{1,0},{2,1},{3,2},{4,3},{5,4},{6,5},{7,6},{8,15},{9,8},{10,9... | collective-permute-start | bytes 393224 | tf_op jit(solution)/shard_map/ppermute | solution.py:353
  61.0 3.3 %attention.8.context_ref = bf16[256,128]{1,0:T(8,128)(2,1)S(1)} custom-call(s32[1]{0:T(128)} %bitcast.3.me_ref, s32[2,32]{1,0:T(2,128)S(1)} %bitcast.12, bf16[1024,128]{1,0:T(8,128)(2,1)} %refs_0_.5, bf16[1024,128]{1,0:T(8,128)(2,1)} %copy-done.8, bf16[1024,128]{1,0:T(8,128)(2,1)} %collective-permute-done.1.refs_2_, bf16[1024,128]{1,0:T(8,128)(2,1)} %copy-done.7, ...), custom_call_target="tpu_custom_call" | custom-call | flops 10737418240 | bytes 3145728 | tf_op jit(solution)/shard_map/attention/pallas_call | solution.py:133
  65.1 2.7 %collective-permute-start.13 = (bf16[128,1024]{1,0:T(8,128)(2,1)S(1)}, bf16[128,1024]{1,0:T(8,128)(2,1)S(1)}, u32[]{:S(2)}, u32[]{:S(2)}) collective-permute-start(bf16[128,1024]{1,0:T(8,128)(2,1)S(1)} %join.11), channel_id=1, source_target_pairs={{0,7},{1,0},{2,1},{3,2},{4,3},{5,4},{6,5},{7,6},{8,15},{9,8},{10,9... | collective-permute-start | bytes 786440 | tf_op jit(solution)/shard_map/ppermute | solution.py:353
  67.8 3.3 %attention.7.context_ref = bf16[256,128]{1,0:T(8,128)(2,1)S(1)} custom-call(s32[1]{0:T(128)} %bitcast.3.me_ref, s32[2,32]{1,0:T(2,128)S(1)} %bitcast.13, bf16[1024,128]{1,0:T(8,128)(2,1)} %refs_0_.5, bf16[1024,128]{1,0:T(8,128)(2,1)} %copy-done.8, bf16[1024,128]{1,0:T(8,128)(2,1)} %collective-permute-done.1.refs_2_, bf16[1024,128]{1,0:T(8,128)(2,1)} %copy-done.7, ...), custom_call_target="tpu_custom_call" | custom-call | flops 10737418240 | bytes 3145728 | tf_op jit(solution)/shard_map/attention/pallas_call | solution.py:133
  72.4 2.8 %collective-permute-start.14 = (bf16[128,1024]{1,0:T(8,128)(2,1)S(1)}, bf16[128,1024]{1,0:T(8,128)(2,1)S(1)}, u32[]{:S(2)}, u32[]{:S(2)}) collective-permute-start(bf16[128,1024]{1,0:T(8,128)(2,1)S(1)} %join.12), channel_id=1, source_target_pairs={{0,7},{1,0},{2,1},{3,2},{4,3},{5,4},{6,5},{7,6},{8,15},{9,8},{10,9... | collective-permute-start | bytes 786440 | tf_op jit(solution)/shard_map/ppermute | solution.py:353
  75.2 3.3 %attention.6.context_ref = bf16[256,128]{1,0:T(8,128)(2,1)S(1)} custom-call(s32[1]{0:T(128)} %bitcast.3.me_ref, s32[2,32]{1,0:T(2,128)S(1)} %bitcast.14, bf16[1024,128]{1,0:T(8,128)(2,1)} %refs_0_.5, bf16[1024,128]{1,0:T(8,128)(2,1)} %copy-done.8, bf16[1024,128]{1,0:T(8,128)(2,1)} %collective-permute-done.1.refs_2_, bf16[1024,128]{1,0:T(8,128)(2,1)} %copy-done.7, ...), custom_call_target="tpu_custom_call" | custom-call | flops 10737418240 | bytes 3145728 | tf_op jit(solution)/shard_map/attention/pallas_call | solution.py:133
  81.4 3.0 %collective-permute-start.15 = (bf16[128,1024]{1,0:T(8,128)(2,1)S(1)}, bf16[128,1024]{1,0:T(8,128)(2,1)S(1)}, u32[]{:S(2)}, u32[]{:S(2)}) collective-permute-start(bf16[128,1024]{1,0:T(8,128)(2,1)S(1)} %join.13), channel_id=1, source_target_pairs={{0,7},{1,0},{2,1},{3,2},{4,3},{5,4},{6,5},{7,6},{8,15},{9,8},{10,9... | collective-permute-start | bytes 786440 | tf_op jit(solution)/shard_map/ppermute | solution.py:353
  87.1 3.5 %collective-permute-done.11.right_ref = bf16[128,1024]{1,0:T(8,128)(2,1)S(1)} collective-permute-done((bf16[128,1024]{1,0:T(8,128)(2,1)S(1)}, bf16[128,1024]{1,0:T(8,128)(2,1)S(1)}, u32[]{:S(2)}, u32[]{:S(2)}) %collective-permute-start.11) | collective-permute-done | bytes 262176 | tf_op jit(solution)/shard_map/ppermute | solution.py:353
  91.3 7.3 %collective-permute-done.19.rows_ref = bf16[128,1024]{1,0:T(8,128)(2,1)S(1)} collective-permute-done((bf16[128,1024]{1,0:T(8,128)(2,1)S(1)}, bf16[128,1024]{1,0:T(8,128)(2,1)S(1)}, u32[]{:S(2)}, u32[]{:S(2)}) %collective-permute-start.19) | collective-permute-done | bytes 262176 | tf_op jit(solution)/shard_map/ppermute | solution.py:356
  98.6 5.0 %all-gather.2.cloned.1.call-done = bf16[6144,1024]{1,0:T(8,128)(2,1)} async-done(((bf16[192,1024]{1,0:T(8,128)(2,1)}), bf16[6144,1024]{1,0:T(8,128)(2,1)}) %all-gather.2.cloned.1.call-update) | async-done | bytes 12582928 | tf_op jit(solution)/shard_map/all_gather | solution.py:405
  103.6 6.4 %feed.3 = bf16[128,1024]{1,0:T(8,128)(2,1)S(1)} custom-call(bf16[128,1024]{1,0:T(8,128)(2,1)S(1)} %collective-permute-done.19.rows_ref, bf16[1024,1024]{1,0:T(8,128)(2,1)} %refs_0_.6, bf16[1024,1024]{1,0:T(8,128)(2,1)} %refs_1_.3, bf16[32,3,64,1024]{3,2,1,0:T(8,128)(2,1)} %bitcast.16), custom_call_target="tpu_custom_call" | custom-call | flops 2147483648 | bytes 16777216 | tf_op jit(solution)/shard_map/feed/pallas_call | solution.py:206
  111.8 6.4 %feed.2.hidden_ref = f32[128,1024]{1,0:T(8,128)S(1)} custom-call(bf16[128,1024]{1,0:T(8,128)(2,1)S(1)} %get-tuple-element.14.rows_ref, f32[128,1024]{1,0:T(8,128)S(1)} %get-tuple-element.15.refs_0_, bf16[1024,1024]{1,0:T(8,128)(2,1)} %refs_0_.6, bf16[1024,1024]{1,0:T(8,128)(2,1)} %refs_1_.3, bf16[32,3,64,1024]{3,2,1,0:T(8,128)(2,1)} %bitcast.17), custom_call_target="tpu_custom_call" | custom-call | flops 2147483648 | bytes 16777216 | tf_op jit(solution)/shard_map/feed/pallas_call | solution.py:206
  119.5 6.1 %all-to-all-start = ((f32[8,8,1024]{2,1,0:T(8,128)}), f32[8,8,1024]{2,1,0:T(8,128)S(1)}, u32[]{:S(2)}, u32[]{:S(2)}) async-start(f32[8,8,1024]{2,1,0:T(8,128)} %pool.1), calls=%async_computation | async-start | bytes 524288 | tf_op jit(solution)/shard_map/all_to_all | solution.py:442
  128.5 6.8 %all-to-all-done = f32[8,8,1024]{2,1,0:T(8,128)S(1)} async-done(((f32[8,8,1024]{2,1,0:T(8,128)}), f32[8,8,1024]{2,1,0:T(8,128)S(1)}, u32[]{:S(2)}, u32[]{:S(2)}) %all-to-all-start) | async-done | bytes 262176 | tf_op jit(solution)/shard_map/all_to_all | solution.py:442
  135.3 5.0 %all_gather.7.pooled_ref = f32[16,8,1024]{2,1,0:T(8,128)S(1)} all-gather(f32[8,8,1024]{2,1,0:T(8,128)S(1)} %all-to-all-done), channel_id=1, replica_groups={{0,8},{16,24},{32,40},{48,56},{64,72},{80,88},{96,104},{112,120},{128,1..., dimensions={0}, use_global_device_ids=true | all-gather | bytes 786432 | tf_op jit(solution)/shard_map/all_gather | solution.py:443
  142.6 5.8 %all-to-all-start.1 = ((bf16[16,8,1024]{2,1,0:T(8,128)(2,1)}), bf16[16,8,1024]{2,1,0:T(8,128)(2,1)S(1)}, u32[]{:S(2)}, u32[]{:S(2)}) async-start(bf16[16,8,1024]{2,1,0:T(8,128)(2,1)} %bitcast.7), calls=%async_computation.1 | async-start | bytes 524288 | tf_op jit(solution)/shard_map/all_to_all | solution.py:453
  148.4 8.1 %all-to-all-done.1 = bf16[16,8,1024]{2,1,0:T(8,128)(2,1)S(1)} async-done(((bf16[16,8,1024]{2,1,0:T(8,128)(2,1)}), bf16[16,8,1024]{2,1,0:T(8,128)(2,1)S(1)}, u32[]{:S(2)}, u32[]{:S(2)}) %all-to-all-start.1) | async-done | bytes 262176 | tf_op jit(solution)/shard_map/all_to_all | solution.py:453
  (93 shorter events, 38.9 us)
Async XLA Ops:
  7.2 96.4 %all-gather.2.cloned.1.call-start = ((), (), s32[]{:S(2)}) async-start(), calls=%async_computation.2 | async-start | bytes 12976128 | tf_op jit(solution)/shard_map/all_gather | solution.py:405
  8.4 22.9 %collective-permute-start = (bf16[1024,128]{1,0:T(8,128)(2,1)}, bf16[1024,128]{1,0:T(8,128)(2,1)S(1)}, u32[]{:S(2)}, u32[]{:S(2)}) collective-permute-start(bf16[1024,128]{1,0:T(8,128)(2,1)} %refs_0_.5), channel_id=1, source_target_pairs={{0,7},{1,0},{2,1},{3,2},{4,3},{5,4},{6,5},{7,6},{8,15},{9,8},{10,9... | collective-permute-start | bytes 786440 | tf_op jit(solution)/shard_map/ppermute | solution.py:353
  14.8 16.4 %collective-permute-start.3 = (bf16[1024,128]{1,0:T(8,128)(2,1)}, bf16[1024,128]{1,0:T(8,128)(2,1)}, u32[]{:S(2)}, u32[]{:S(2)}) collective-permute-start(bf16[1024,128]{1,0:T(8,128)(2,1)} %refs_0_.5), channel_id=1, source_target_pairs={{0,1},{1,2},{2,3},{3,4},{4,5},{5,6},{6,7},{7,0},{8,9},{9,10},{10,1... | collective-permute-start | bytes 786440 | tf_op jit(solution)/shard_map/ppermute | solution.py:353
  14.8 11.2 %collective-permute-start.16 = (bf16[64,1024]{1,0:T(8,128)(2,1)S(1)}, bf16[64,1024]{1,0:T(8,128)(2,1)S(1)}, u32[]{:S(2)}, u32[]{:S(2)}) collective-permute-start(bf16[64,1024]{1,0:T(8,128)(2,1)S(1)} %pad_maximum_fusion.1), channel_id=1, source_target_pairs={{0,2},{1,3},{2,4},{3,5},{4,6},{5,7},{6,0},{7,1},{8,10},{9,11},{10,... | collective-permute-start | bytes 393224 | tf_op jit(solution)/shard_map/ppermute | solution.py:353
  14.8 13.6 %collective-permute-start.17 = (bf16[64,1024]{1,0:T(8,128)(2,1)S(1)}, bf16[64,1024]{1,0:T(8,128)(2,1)S(1)}, u32[]{:S(2)}, u32[]{:S(2)}) collective-permute-start(bf16[64,1024]{1,0:T(8,128)(2,1)S(1)} %pad_maximum_fusion.1), channel_id=1, source_target_pairs={{0,6},{1,7},{2,0},{3,1},{4,2},{5,3},{6,4},{7,5},{8,14},{9,15},{10,... | collective-permute-start | bytes 393224 | tf_op jit(solution)/shard_map/ppermute | solution.py:353
  18.4 12.8 %collective-permute-start.18 = (bf16[64,1024]{1,0:T(8,128)(2,1)S(1)}, bf16[64,1024]{1,0:T(8,128)(2,1)S(1)}, u32[]{:S(2)}, u32[]{:S(2)}) collective-permute-start(bf16[64,1024]{1,0:T(8,128)(2,1)S(1)} %pad_maximum_fusion.1), channel_id=1, source_target_pairs={{0,5},{1,4},{2,7},{3,6},{4,1},{5,0},{6,3},{7,2},{8,13},{9,12},{10,... | collective-permute-start | bytes 393224 | tf_op jit(solution)/shard_map/ppermute | solution.py:363
  32.2 7.4 %collective-permute-start.1 = (bf16[1024,128]{1,0:T(8,128)(2,1)S(1)}, bf16[1024,128]{1,0:T(8,128)(2,1)}, u32[]{:S(2)}, u32[]{:S(2)}) collective-permute-start(bf16[1024,128]{1,0:T(8,128)(2,1)S(1)} %collective-permute-done.refs_1_), channel_id=1, source_target_pairs={{0,7},{1,0},{2,1},{3,2},{4,3},{5,4},{6,5},{7,6},{8,15},{9,8},{10,9... | collective-permute-start | bytes 786440 | tf_op jit(solution)/shard_map/ppermute | solution.py:353
  34.6 7.3 %collective-permute-start.4 = (bf16[1024,128]{1,0:T(8,128)(2,1)}, bf16[1024,128]{1,0:T(8,128)(2,1)}, u32[]{:S(2)}, u32[]{:S(2)}) collective-permute-start(bf16[1024,128]{1,0:T(8,128)(2,1)} %collective-permute-done.3.refs_6_), channel_id=1, source_target_pairs={{0,1},{1,2},{2,3},{3,4},{4,5},{5,6},{6,7},{7,0},{8,9},{9,10},{10,1... | collective-permute-start | bytes 786440 | tf_op jit(solution)/shard_map/ppermute | solution.py:353
  39.6 10.1 %collective-permute-start.2 = (bf16[1024,128]{1,0:T(8,128)(2,1)}, bf16[1024,128]{1,0:T(8,128)(2,1)S(1)}, u32[]{:S(2)}, u32[]{:S(2)}) collective-permute-start(bf16[1024,128]{1,0:T(8,128)(2,1)} %collective-permute-done.1.refs_2_), channel_id=1, source_target_pairs={{0,7},{1,0},{2,1},{3,2},{4,3},{5,4},{6,5},{7,6},{8,15},{9,8},{10,9... | collective-permute-start | bytes 786440 | tf_op jit(solution)/shard_map/ppermute | solution.py:353
  41.9 6.7 %collective-permute-start.5 = (bf16[1024,128]{1,0:T(8,128)(2,1)}, bf16[1024,128]{1,0:T(8,128)(2,1)}, u32[]{:S(2)}, u32[]{:S(2)}) collective-permute-start(bf16[1024,128]{1,0:T(8,128)(2,1)} %collective-permute-done.4.refs_7_), channel_id=1, source_target_pairs={{0,1},{1,2},{2,3},{3,4},{4,5},{5,6},{6,7},{7,0},{8,9},{9,10},{10,1... | collective-permute-start | bytes 786440 | tf_op jit(solution)/shard_map/ppermute | solution.py:353
  49.6 5.1 %collective-permute-start.6 = (bf16[512,128]{1,0:T(8,128)(2,1)S(1)}, bf16[512,128]{1,0:T(8,128)(2,1)S(1)}, u32[]{:S(2)}, u32[]{:S(2)}) collective-permute-start(bf16[512,128]{1,0:T(8,128)(2,1)S(1)} %slice.8), channel_id=1, source_target_pairs={{0,1},{1,2},{2,3},{3,4},{4,5},{5,6},{6,7},{7,0},{8,9},{9,10},{10,1... | collective-permute-start | bytes 393224 | tf_op jit(solution)/shard_map/ppermute | solution.py:353
  49.7 5.0 %collective-permute-start.7 = (bf16[512,128]{1,0:T(8,128)(2,1)S(1)}, bf16[512,128]{1,0:T(8,128)(2,1)S(1)}, u32[]{:S(2)}, u32[]{:S(2)}) collective-permute-start(bf16[512,128]{1,0:T(8,128)(2,1)S(1)} %slice.9), channel_id=1, source_target_pairs={{0,7},{1,0},{2,1},{3,2},{4,3},{5,4},{6,5},{7,6},{8,15},{9,8},{10,9... | collective-permute-start | bytes 393224 | tf_op jit(solution)/shard_map/ppermute | solution.py:353
  58.1 6.2 %collective-permute-start.8 = (bf16[64,1024]{1,0:T(8,128)(2,1)S(1)}, bf16[64,1024]{1,0:T(8,128)(2,1)S(1)}, u32[]{:S(2)}, u32[]{:S(2)}) collective-permute-start(bf16[64,1024]{1,0:T(8,128)(2,1)S(1)} %get-tuple-element.12), channel_id=1, source_target_pairs={{0,1},{1,2},{2,3},{3,4},{4,5},{5,6},{6,7},{7,0},{8,9},{9,10},{10,1... | collective-permute-start | bytes 393224 | tf_op jit(solution)/shard_map/ppermute | solution.py:353
  58.2 6.7 %collective-permute-start.12 = (bf16[64,1024]{1,0:T(8,128)(2,1)S(1)}, bf16[64,1024]{1,0:T(8,128)(2,1)S(1)}, u32[]{:S(2)}, u32[]{:S(2)}) collective-permute-start(bf16[64,1024]{1,0:T(8,128)(2,1)S(1)} %get-tuple-element.13), channel_id=1, source_target_pairs={{0,7},{1,0},{2,1},{3,2},{4,3},{5,4},{6,5},{7,6},{8,15},{9,8},{10,9... | collective-permute-start | bytes 393224 | tf_op jit(solution)/shard_map/ppermute | solution.py:353
  64.6 7.2 %collective-permute-start.9 = (bf16[128,1024]{1,0:T(8,128)(2,1)S(1)}, bf16[128,1024]{1,0:T(8,128)(2,1)S(1)}, u32[]{:S(2)}, u32[]{:S(2)}) collective-permute-start(bf16[128,1024]{1,0:T(8,128)(2,1)S(1)} %join.8), channel_id=1, source_target_pairs={{0,1},{1,2},{2,3},{3,4},{4,5},{5,6},{6,7},{7,0},{8,9},{9,10},{10,1... | collective-permute-start | bytes 786440 | tf_op jit(solution)/shard_map/ppermute | solution.py:353
  65.1 7.1 %collective-permute-start.13 = (bf16[128,1024]{1,0:T(8,128)(2,1)S(1)}, bf16[128,1024]{1,0:T(8,128)(2,1)S(1)}, u32[]{:S(2)}, u32[]{:S(2)}) collective-permute-start(bf16[128,1024]{1,0:T(8,128)(2,1)S(1)} %join.11), channel_id=1, source_target_pairs={{0,7},{1,0},{2,1},{3,2},{4,3},{5,4},{6,5},{7,6},{8,15},{9,8},{10,9... | collective-permute-start | bytes 786440 | tf_op jit(solution)/shard_map/ppermute | solution.py:353
  72.1 8.8 %collective-permute-start.10 = (bf16[128,1024]{1,0:T(8,128)(2,1)S(1)}, bf16[128,1024]{1,0:T(8,128)(2,1)S(1)}, u32[]{:S(2)}, u32[]{:S(2)}) collective-permute-start(bf16[128,1024]{1,0:T(8,128)(2,1)S(1)} %join.9), channel_id=1, source_target_pairs={{0,1},{1,2},{2,3},{3,4},{4,5},{5,6},{6,7},{7,0},{8,9},{9,10},{10,1... | collective-permute-start | bytes 786440 | tf_op jit(solution)/shard_map/ppermute | solution.py:353
  72.4 8.8 %collective-permute-start.14 = (bf16[128,1024]{1,0:T(8,128)(2,1)S(1)}, bf16[128,1024]{1,0:T(8,128)(2,1)S(1)}, u32[]{:S(2)}, u32[]{:S(2)}) collective-permute-start(bf16[128,1024]{1,0:T(8,128)(2,1)S(1)} %join.12), channel_id=1, source_target_pairs={{0,7},{1,0},{2,1},{3,2},{4,3},{5,4},{6,5},{7,6},{8,15},{9,8},{10,9... | collective-permute-start | bytes 786440 | tf_op jit(solution)/shard_map/ppermute | solution.py:353
  81.1 9.6 %collective-permute-start.11 = (bf16[128,1024]{1,0:T(8,128)(2,1)S(1)}, bf16[128,1024]{1,0:T(8,128)(2,1)S(1)}, u32[]{:S(2)}, u32[]{:S(2)}) collective-permute-start(bf16[128,1024]{1,0:T(8,128)(2,1)S(1)} %join.10), channel_id=1, source_target_pairs={{0,1},{1,2},{2,3},{3,4},{4,5},{5,6},{6,7},{7,0},{8,9},{9,10},{10,1... | collective-permute-start | bytes 786440 | tf_op jit(solution)/shard_map/ppermute | solution.py:353
  81.4 9.3 %collective-permute-start.15 = (bf16[128,1024]{1,0:T(8,128)(2,1)S(1)}, bf16[128,1024]{1,0:T(8,128)(2,1)S(1)}, u32[]{:S(2)}, u32[]{:S(2)}) collective-permute-start(bf16[128,1024]{1,0:T(8,128)(2,1)S(1)} %join.13), channel_id=1, source_target_pairs={{0,7},{1,0},{2,1},{3,2},{4,3},{5,4},{6,5},{7,6},{8,15},{9,8},{10,9... | collective-permute-start | bytes 786440 | tf_op jit(solution)/shard_map/ppermute | solution.py:353
  90.9 7.7 %collective-permute-start.19 = (bf16[128,1024]{1,0:T(8,128)(2,1)S(1)}, bf16[128,1024]{1,0:T(8,128)(2,1)S(1)}, u32[]{:S(2)}, u32[]{:S(2)}) collective-permute-start(bf16[128,1024]{1,0:T(8,128)(2,1)S(1)} %get-tuple-element.14.rows_ref), channel_id=1, source_target_pairs={{0,1},{1,0},{2,3},{3,2},{4,5},{5,4},{6,7},{7,6},{8,9},{9,8},{10,11... | collective-permute-start | bytes 786440 | tf_op jit(solution)/shard_map/ppermute | solution.py:356
  110.0 8.2 %collective-permute-start.20 = (bf16[128,1024]{1,0:T(8,128)(2,1)S(1)}, bf16[128,1024]{1,0:T(8,128)(2,1)S(1)}, u32[]{:S(2)}, u32[]{:S(2)}) collective-permute-start(bf16[128,1024]{1,0:T(8,128)(2,1)S(1)} %feed.3), channel_id=1, source_target_pairs={{0,1},{1,0},{2,3},{3,2},{4,5},{5,4},{6,7},{7,6},{8,9},{9,8},{10,11... | collective-permute-start | bytes 786440 | tf_op jit(solution)/shard_map/ppermute | solution.py:356
  119.5 15.7 %all-to-all-start = ((f32[8,8,1024]{2,1,0:T(8,128)}), f32[8,8,1024]{2,1,0:T(8,128)S(1)}, u32[]{:S(2)}, u32[]{:S(2)}) async-start(f32[8,8,1024]{2,1,0:T(8,128)} %pool.1), calls=%async_computation | async-start | bytes 524288 | tf_op jit(solution)/shard_map/all_to_all | solution.py:442
  142.6 13.9 %all-to-all-start.1 = ((bf16[16,8,1024]{2,1,0:T(8,128)(2,1)}), bf16[16,8,1024]{2,1,0:T(8,128)(2,1)S(1)}, u32[]{:S(2)}, u32[]{:S(2)}) async-start(bf16[16,8,1024]{2,1,0:T(8,128)(2,1)} %bitcast.7), calls=%async_computation.1 | async-start | bytes 524288 | tf_op jit(solution)/shard_map/all_to_all | solution.py:453
  (13 other events, 427.4 us)
Sparse Core Ops, SparseCore 0:
  32.3 71.3 all-gather.1

commit v6 on v5

--- a/solution.py
+++ b/solution.py
@@ -238,30 +238,30 @@
     mean = jnp.mean(pooled, axis=0, keepdims=True)
     large, small = split(pooled - mean)
     feature = lax.broadcasted_iota(jnp.int32, (width, total), 0)
-    wanted = lax.broadcasted_iota(jnp.int32, (width, total), 1)
-    chosen = (wanted // PACK) * per_chip + first + wanted % PACK
-    pick = jnp.where((feature == chosen) & (wanted % PACK < own), 1.0, 0.0).astype(BF)
+    wanted = lax.broadcasted_iota(jnp.int32, (1, total), 1)
+    chosen = jnp.where(wanted % PACK < own, (wanted // PACK) * per_chip + first + wanted % PACK, -1)
+    pick = jnp.where(feature == chosen, 1.0, 0.0).astype(BF)
     picked_large, picked_small = dot(large, pick).astype(BF), dot(small, pick).astype(BF)
     rows = ((0,), (0,))
     moments = dot(picked_large, large, rows) + (dot(picked_large, small, rows) + dot(picked_small, large, rows))
     rotated = dot(large, proj_ref[...]).astype(BF)
     lanes = rotated.shape[1]
-    row = lax.broadcasted_iota(jnp.int32, (total, sentences), 0)
-    column = lax.broadcasted_iota(jnp.int32, (total, sentences), 1)
-    target = ((row // PACK) * CORES + core) * KINDS
-    half = sentences // CORES
-    ones = jnp.ones((sentences, lanes), BF)
-    sides = []
-    for a in range(CORES):
-        mine = (column // half == a) & (row % PACK == own + 2)
-        there = (column // half == a) & (row % PACK == own + 3)
-        for k in range(KINDS):
-            hit = target + k == code_ref[...]
-            sides.append(
-                dot(jnp.where(mine & hit, 1.0, 0.0).astype(BF), rotated)
-                + dot(jnp.where(there & hit, 1.0, 0.0).astype(BF), ones)
-            )
-    sides = jnp.concatenate(sides, axis=-1)
+    chips = total // PACK
+    row = lax.broadcasted_iota(jnp.int32, (CORES * KINDS * chips, 1), 0)
+    column = lax.broadcasted_iota(jnp.int32, (1, sentences), 1)
+    kind = row // chips
+    target = ((row % chips) * CORES + core) * KINDS + kind % KINDS
+    hit = (target == code_ref[...]) & (column // (sentences // CORES) == kind // KINDS)
+    place = jnp.where(hit, 1.0, 0.0)
+    there = jnp.broadcast_to(jnp.sum(place, axis=1, keepdims=True), (place.shape[0], lanes))
+    wide = [
+        jnp.concatenate([part[k * chips:(k + 1) * chips] for k in range(CORES * KINDS)], axis=-1)
+        for part in (dot(place.astype(BF), rotated), there)
+    ]
+    row = lax.broadcasted_iota(jnp.int32, (total, 1), 0)
+    column = lax.broadcasted_iota(jnp.int32, (1, CORES * chips), 1)
+    spread = (row // PACK == column % chips) & (row % PACK == own + 2 + column // chips)
+    sides = dot(jnp.where(spread, 1.0, 0.0).astype(BF), jnp.concatenate(wide, axis=0).astype(BF))
     high = mean.astype(BF).astype(F32)
     low = mean - high
     line = lax.broadcasted_iota(jnp.int32, (total, 1), 0) % PACK
@@ -277,17 +277,22 @@
     chips = total // PACK
     sentences = pq_ref.shape[1]
     each = float(CORES * sentences)
-    source = lax.broadcasted_iota(jnp.int32, (chips, total), 0)
-    line = lax.broadcasted_iota(jnp.int32, (chips, total), 1) - source * PACK
-    means = dot(jnp.where((line == own) | (line == own + 1), 1.0, 0.0).astype(BF), recv)
-    sides = dot(jnp.where(line == own + 2, 1.0, 0.0).astype(BF), recv).astype(BF)
-    there = dot(jnp.where(line == own + 3, 1.0, 0.0).astype(BF), recv).astype(BF)
-    line = lax.broadcasted_iota(jnp.int32, (PACK, total), 1) % PACK
-    within = dot(jnp.where(line == lax.broadcasted_iota(jnp.int32, (PACK, total), 0), 1.0, 0.0).astype(BF), recv)
+    row = lax.broadcasted_iota(jnp.int32, (3 * chips + PACK, 1), 0)
+    line = lax.broadcasted_iota(jnp.int32, (1, total), 1)
+    kind, source = row // chips, row % chips
+    away = line - source * PACK
+    taken = (kind == 0) & ((away == own) | (away == own + 1))
+    taken = taken | ((kind == 1) & (away == own + 2)) | ((kind == 2) & (away == own + 3))
+    taken = taken | ((kind == 3) & (line % PACK == source))
+    parts = dot(jnp.where(taken, 1.0, 0.0).astype(BF), recv)
+    means = parts[:chips]
+    sides = parts[chips:2 * chips].astype(BF)
+    there = parts[2 * chips:3 * chips].astype(BF)
+    within = parts[3 * chips:]
     away = means - jnp.mean(means, axis=0, keepdims=True)
     feature = lax.broadcasted_iota(jnp.int32, (width, LANES), 0)
-    lane = lax.broadcasted_iota(jnp.int32, (width, LANES), 1)
-    pick = jnp.where((feature == first + lane) & (lane < own), 1.0, 0.0).astype(BF)
+    lane = lax.broadcasted_iota(jnp.int32, (1, LANES), 1)
+    pick = jnp.where(feature == jnp.where(lane < own, first + lane, -1), 1.0, 0.0).astype(BF)
     large, small = split(away)
     picked_large, picked_small = dot(large, pick).astype(BF), dot(small, pick).astype(BF)
     rows = ((0,), (0,))
@@ -296,23 +301,24 @@
     shift = dot(large, proj_ref[...]) + dot(small, proj_ref[...])
     shift_large, shift_small = split(shift)
     lanes = shift.shape[1]
-    one = lax.broadcasted_iota(jnp.int32, (chips, chips), 0)
-    other = lax.broadcasted_iota(jnp.int32, (chips, chips), 1)
-    ahead = jnp.where(one < other, 1.0, 0.0).astype(BF)
+    kinds = CORES * KINDS
+    stack = lambda wide: jnp.concatenate([wide[:, k * lanes:(k + 1) * lanes] for k in range(kinds)], axis=0)
+    size = kinds * chips
+    one = lax.broadcasted_iota(jnp.int32, (size, 1), 0)
+    other = lax.broadcasted_iota(jnp.int32, (1, size), 1)
+    one_kind, one_chip, other_kind, other_chip = one // chips, one % chips, other // chips, other % chips
+    ahead = (one_chip < other_chip) | ((one_chip == other_chip) & (one_kind // 2 < other_kind // 2))
+    ahead = jnp.where(ahead & (one_kind % 2 == 0), 1.0, 0.0).astype(BF)
     same = jnp.where(one == other, 1.0, 0.0).astype(BF)
-    kinds = [a * KINDS + 2 * c for a in range(CORES) for c in range(SLOTS)]
-    filled = [there[:, k * lanes:(k + 1) * lanes] for k in kinds]
-    flat = [dot(f, same, ((0,), (0,)))[:1] for f in filled]
-    before = sum(dot(f, ahead, ((0,), (0,)))[:1] for f in filled)
-    place = lax.broadcasted_iota(jnp.int32, (sentences, chips), 0)
-    result = jnp.zeros((sentences, lanes), F32)
-    for kind, here in zip(kinds, flat):
-        for k in range(2):
-            position = (2.0 * before + float(k)).astype(jnp.int32)
-            chosen = jnp.where((place == position) & (here > 0.5), 1.0, 0.0).astype(BF)
-            block = sides[:, (kind + k) * lanes:(kind + k + 1) * lanes]
-            result = result + (dot(chosen, block) + (dot(chosen, shift_large) + dot(chosen, shift_small)))
-        before = before + here
+    flags = stack(there)[:, :8]
+    before = dot(flags, ahead, ((0,), (0,)))[:1]
+    here = dot(flags, same, ((0,), (0,)))[:1]
+    place = lax.broadcasted_iota(jnp.int32, (sentences, size), 0)
+    odd = (lax.broadcasted_iota(jnp.int32, (1, size), 1) // chips) % 2
+    position = 2 * before.astype(jnp.int32) + odd
+    chosen = jnp.where((place == position) & (here > 0.5), 1.0, 0.0).astype(BF)
+    tiled = lambda array: jnp.concatenate([array] * kinds, axis=0)
+    result = dot(chosen, stack(sides)) + (dot(chosen, tiled(shift_large)) + dot(chosen, tiled(shift_small)))
     for q in range(pq_ref.shape[0]):
         pq_ref[q] = result[:, q * SUBW:(q + 1) * SUBW]
 
@@ -359,7 +365,6 @@
     piece = jnp.concatenate(
         [lax.dynamic_slice_in_dim(w, dp_at * rows, rows, 0) for w in (w_up, w_down)], axis=0
     )
-    piece, tokens = lax.optimization_barrier((piece, tokens))
     across = lax.ppermute(
         piece, "sub", [(i, (i + (half - 1 if i % 2 else 1 - half)) % sub_count) for i in range(sub_count)]
     )

time: 166 us -> 165 us (level)
  waiting for transfers between devices: 56.8 us -> 55 us
    ppermute x18, waiting for transfers between devices: 26 us -> 23.6 us  [move(): lax.ppermute(array, 'sub', [(i, (i + by) % sub_count) for i in range(sub_...]
  transfers between devices with their start and end apart: 25 -> 25, of which waited for: 15 -> 15; matrix products, arithmetic and copies ran while one was open for 2% -> 3% of each run, Pallas kernels for 14% -> 14%
where the time goes in v6:
time: 165 us; the launch traced here: 164 us
  waiting for transfers between devices  55 us (33%)
  starting transfers between devices  48.5 us (29%)
  Pallas kernels  35.1 us (21%)
  between operations  14.4 us (9%)
  blocking collectives  4.94 us (3%)
  local copies, waits for them, and re-layouts  3.04 us (2%)
  other arithmetic  3.03 us (2%)
    ppermute x18, starting transfers between devices, move(): lax.ppermute(array, 'sub', [(i, (i + by) % sub_count) for i in range(sub_...  30.8 us
    ppermute x18, waiting for transfers between devices, move(): lax.ppermute(array, 'sub', [(i, (i + by) % sub_count) for i in range(sub_...  23.6 us
    pallas_call x5, Pallas kernels, attention(): pl.pallas_call(functools.partial(attention_kernel, offsets, parts, chunk,...  15.2 us
    pallas_call x2, Pallas kernels, feed(): pl.pallas_call(feed_kernel, in_specs=[vmem] * (1 + len(hidden)) + [hbm] *...  12.8 us
    all_to_all x1, waiting for transfers between devices, on_device(): lax.all_to_all(sent.reshape(chips, PACK, width), 'dp', split_axis=0, conc...  8.1 us
    ppermute x2, waiting for transfers between devices, swap(): return lax.ppermute(array, 'sub', [(i, i ^ 1) for i in range(sub_count)])  7.34 us
    pallas_call x11, Pallas kernels, small_call(): pl.pallas_call(kernel, in_specs=specs, out_specs=pl.BlockSpec(memory_spac...  7.1 us
    all_to_all x1, waiting for transfers between devices, on_device(): lax.all_to_all(pooled, 'sub', split_axis=0, concat_axis=0, tiled=True)  6.82 us
  transfers between devices with their start and end apart: 25, of which 15 were waited for; matrix products, arithmetic and copies ran while one was open for 3% of the time, Pallas kernels for 14%

profile of v6, /device:TPU:1, one launch (start us, length us, event | category | flops | bytes accessed | tf_op | source)
XLA Modules:
  0.0 164.0 jit_solution(11802511509895065858)
XLA Ops:
  7.3 6.5 %collective-permute-start = (bf16[1024,128]{1,0:T(8,128)(2,1)}, bf16[1024,128]{1,0:T(8,128)(2,1)S(1)}, u32[]{:S(2)}, u32[]{:S(2)}) collective-permute-start(bf16[1024,128]{1,0:T(8,128)(2,1)} %refs_0_.10), channel_id=1, source_target_pairs={{0,7},{1,0},{2,1},{3,2},{4,3},{5,4},{6,5},{7,6},{8,15},{9,8},{10,9... | collective-permute-start | bytes 786440 | tf_op jit(solution)/shard_map/ppermute | solution.py:359
  14.8 3.6 %collective-permute-start.17 = (bf16[64,1024]{1,0:T(8,128)(2,1)S(1)}, bf16[64,1024]{1,0:T(8,128)(2,1)S(1)}, u32[]{:S(2)}, u32[]{:S(2)}) collective-permute-start(bf16[64,1024]{1,0:T(8,128)(2,1)S(1)} %pad_maximum_fusion.1), channel_id=1, source_target_pairs={{0,6},{1,7},{2,0},{3,1},{4,2},{5,3},{6,4},{7,5},{8,14},{9,15},{10,... | collective-permute-start | bytes 393224 | tf_op jit(solution)/shard_map/ppermute | solution.py:359
  20.7 4.3 %collective-permute-done.16 = bf16[64,1024]{1,0:T(8,128)(2,1)S(1)} collective-permute-done((bf16[64,1024]{1,0:T(8,128)(2,1)S(1)}, bf16[64,1024]{1,0:T(8,128)(2,1)S(1)}, u32[]{:S(2)}, u32[]{:S(2)}) %collective-permute-start.16) | collective-permute-done | bytes 131104 | tf_op jit(solution)/shard_map/ppermute | solution.py:359
  26.7 3.5 %collective-permute-done.18 = bf16[64,1024]{1,0:T(8,128)(2,1)S(1)} collective-permute-done((bf16[64,1024]{1,0:T(8,128)(2,1)S(1)}, bf16[64,1024]{1,0:T(8,128)(2,1)S(1)}, u32[]{:S(2)}, u32[]{:S(2)}) %collective-permute-start.18) | collective-permute-done | bytes 131104 | tf_op jit(solution)/shard_map/ppermute | solution.py:368
  37.3 3.5 %collective-permute-start.2 = (bf16[1024,128]{1,0:T(8,128)(2,1)}, bf16[1024,128]{1,0:T(8,128)(2,1)S(1)}, u32[]{:S(2)}, u32[]{:S(2)}) collective-permute-start(bf16[1024,128]{1,0:T(8,128)(2,1)} %collective-permute-done.1.refs_2_), channel_id=1, source_target_pairs={{0,7},{1,0},{2,1},{3,2},{4,3},{5,4},{6,5},{7,6},{8,15},{9,8},{10,9... | collective-permute-start | bytes 786440 | tf_op jit(solution)/shard_map/ppermute | solution.py:359
  41.0 6.6 %collective-permute-done.5.refs_8_ = bf16[1024,128]{1,0:T(8,128)(2,1)} collective-permute-done((bf16[1024,128]{1,0:T(8,128)(2,1)}, bf16[1024,128]{1,0:T(8,128)(2,1)}, u32[]{:S(2)}, u32[]{:S(2)}) %collective-permute-start.5) | collective-permute-done | bytes 262176 | tf_op jit(solution)/shard_map/ppermute | solution.py:359
  48.6 2.7 %collective-permute-start.7 = (bf16[512,128]{1,0:T(8,128)(2,1)S(1)}, bf16[512,128]{1,0:T(8,128)(2,1)S(1)}, u32[]{:S(2)}, u32[]{:S(2)}) collective-permute-start(bf16[512,128]{1,0:T(8,128)(2,1)S(1)} %slice.9), channel_id=1, source_target_pairs={{0,7},{1,0},{2,1},{3,2},{4,3},{5,4},{6,5},{7,6},{8,15},{9,8},{10,9... | collective-permute-start | bytes 393224 | tf_op jit(solution)/shard_map/ppermute | solution.py:359
  57.1 2.8 %collective-permute-start.12 = (bf16[64,1024]{1,0:T(8,128)(2,1)S(1)}, bf16[64,1024]{1,0:T(8,128)(2,1)S(1)}, u32[]{:S(2)}, u32[]{:S(2)}) collective-permute-start(bf16[64,1024]{1,0:T(8,128)(2,1)S(1)} %get-tuple-element.10), channel_id=1, source_target_pairs={{0,7},{1,0},{2,1},{3,2},{4,3},{5,4},{6,5},{7,6},{8,15},{9,8},{10,9... | collective-permute-start | bytes 393224 | tf_op jit(solution)/shard_map/ppermute | solution.py:359
  59.9 3.3 %attention.8.context_ref = bf16[256,128]{1,0:T(8,128)(2,1)S(1)} custom-call(s32[1]{0:T(128)} %bitcast.3.me_ref, s32[2,32]{1,0:T(2,128)S(1)} %bitcast.12, bf16[1024,128]{1,0:T(8,128)(2,1)} %refs_0_.10, bf16[1024,128]{1,0:T(8,128)(2,1)} %copy-done.8, bf16[1024,128]{1,0:T(8,128)(2,1)} %collective-permute-done.1.refs_2_, bf16[1024,128]{1,0:T(8,128)(2,1)} %copy-done.7, ...), custom_call_target="tpu_custom_call" | custom-call | flops 10737418240 | bytes 3145728 | tf_op jit(solution)/shard_map/attention/pallas_call | solution.py:133
  64.0 2.7 %collective-permute-start.13 = (bf16[128,1024]{1,0:T(8,128)(2,1)S(1)}, bf16[128,1024]{1,0:T(8,128)(2,1)S(1)}, u32[]{:S(2)}, u32[]{:S(2)}) collective-permute-start(bf16[128,1024]{1,0:T(8,128)(2,1)S(1)} %join.11), channel_id=1, source_target_pairs={{0,7},{1,0},{2,1},{3,2},{4,3},{5,4},{6,5},{7,6},{8,15},{9,8},{10,9... | collective-permute-start | bytes 786440 | tf_op jit(solution)/shard_map/ppermute | solution.py:359
  66.8 3.3 %attention.7.context_ref = bf16[256,128]{1,0:T(8,128)(2,1)S(1)} custom-call(s32[1]{0:T(128)} %bitcast.3.me_ref, s32[2,32]{1,0:T(2,128)S(1)} %bitcast.13, bf16[1024,128]{1,0:T(8,128)(2,1)} %refs_0_.10, bf16[1024,128]{1,0:T(8,128)(2,1)} %copy-done.8, bf16[1024,128]{1,0:T(8,128)(2,1)} %collective-permute-done.1.refs_2_, bf16[1024,128]{1,0:T(8,128)(2,1)} %copy-done.7, ...), custom_call_target="tpu_custom_call" | custom-call | flops 10737418240 | bytes 3145728 | tf_op jit(solution)/shard_map/attention/pallas_call | solution.py:133
  71.3 2.8 %collective-permute-start.14 = (bf16[128,1024]{1,0:T(8,128)(2,1)S(1)}, bf16[128,1024]{1,0:T(8,128)(2,1)S(1)}, u32[]{:S(2)}, u32[]{:S(2)}) collective-permute-start(bf16[128,1024]{1,0:T(8,128)(2,1)S(1)} %join.12), channel_id=1, source_target_pairs={{0,7},{1,0},{2,1},{3,2},{4,3},{5,4},{6,5},{7,6},{8,15},{9,8},{10,9... | collective-permute-start | bytes 786440 | tf_op jit(solution)/shard_map/ppermute | solution.py:359
  74.1 3.3 %attention.6.context_ref = bf16[256,128]{1,0:T(8,128)(2,1)S(1)} custom-call(s32[1]{0:T(128)} %bitcast.3.me_ref, s32[2,32]{1,0:T(2,128)S(1)} %bitcast.14, bf16[1024,128]{1,0:T(8,128)(2,1)} %refs_0_.10, bf16[1024,128]{1,0:T(8,128)(2,1)} %copy-done.8, bf16[1024,128]{1,0:T(8,128)(2,1)} %collective-permute-done.1.refs_2_, bf16[1024,128]{1,0:T(8,128)(2,1)} %copy-done.7, ...), custom_call_target="tpu_custom_call" | custom-call | flops 10737418240 | bytes 3145728 | tf_op jit(solution)/shard_map/attention/pallas_call | solution.py:133
  80.3 3.0 %collective-permute-start.15 = (bf16[128,1024]{1,0:T(8,128)(2,1)S(1)}, bf16[128,1024]{1,0:T(8,128)(2,1)S(1)}, u32[]{:S(2)}, u32[]{:S(2)}) collective-permute-start(bf16[128,1024]{1,0:T(8,128)(2,1)S(1)} %join.13), channel_id=1, source_target_pairs={{0,7},{1,0},{2,1},{3,2},{4,3},{5,4},{6,5},{7,6},{8,15},{9,8},{10,9... | collective-permute-start | bytes 786440 | tf_op jit(solution)/shard_map/ppermute | solution.py:359
  86.1 3.5 %collective-permute-done.11.right_ref = bf16[128,1024]{1,0:T(8,128)(2,1)S(1)} collective-permute-done((bf16[128,1024]{1,0:T(8,128)(2,1)S(1)}, bf16[128,1024]{1,0:T(8,128)(2,1)S(1)}, u32[]{:S(2)}, u32[]{:S(2)}) %collective-permute-start.11) | collective-permute-done | bytes 262176 | tf_op jit(solution)/shard_map/ppermute | solution.py:359
  90.2 7.3 %collective-permute-done.19.rows_ref = bf16[128,1024]{1,0:T(8,128)(2,1)S(1)} collective-permute-done((bf16[128,1024]{1,0:T(8,128)(2,1)S(1)}, bf16[128,1024]{1,0:T(8,128)(2,1)S(1)}, u32[]{:S(2)}, u32[]{:S(2)}) %collective-permute-start.19) | collective-permute-done | bytes 262176 | tf_op jit(solution)/shard_map/ppermute | solution.py:362
  97.5 5.0 %all-gather.2.cloned.1.call-done = bf16[6144,1024]{1,0:T(8,128)(2,1)} async-done(((bf16[192,1024]{1,0:T(8,128)(2,1)}), bf16[6144,1024]{1,0:T(8,128)(2,1)}) %all-gather.2.cloned.1.call-update) | async-done | bytes 12582928 | tf_op jit(solution)/shard_map/all_gather | solution.py:410
  102.6 6.4 %feed.3 = bf16[128,1024]{1,0:T(8,128)(2,1)S(1)} custom-call(bf16[128,1024]{1,0:T(8,128)(2,1)S(1)} %collective-permute-done.19.rows_ref, bf16[1024,1024]{1,0:T(8,128)(2,1)} %refs_0_.11, bf16[1024,1024]{1,0:T(8,128)(2,1)} %refs_1_.3, bf16[32,3,64,1024]{3,2,1,0:T(8,128)(2,1)} %bitcast.16), custom_call_target="tpu_custom_call" | custom-call | flops 2147483648 | bytes 16777216 | tf_op jit(solution)/shard_map/feed/pallas_call | solution.py:206
  110.8 6.4 %feed.2.hidden_ref = f32[128,1024]{1,0:T(8,128)S(1)} custom-call(bf16[128,1024]{1,0:T(8,128)(2,1)S(1)} %get-tuple-element.11.rows_ref, f32[128,1024]{1,0:T(8,128)S(1)} %get-tuple-element.12.refs_0_, bf16[1024,1024]{1,0:T(8,128)(2,1)} %refs_0_.11, bf16[1024,1024]{1,0:T(8,128)(2,1)} %refs_1_.3, bf16[32,3,64,1024]{3,2,1,0:T(8,128)(2,1)} %bitcast.17), custom_call_target="tpu_custom_call" | custom-call | flops 2147483648 | bytes 16777216 | tf_op jit(solution)/shard_map/feed/pallas_call | solution.py:206
  118.5 6.1 %all-to-all-start = ((f32[8,8,1024]{2,1,0:T(8,128)}), f32[8,8,1024]{2,1,0:T(8,128)S(1)}, u32[]{:S(2)}, u32[]{:S(2)}) async-start(f32[8,8,1024]{2,1,0:T(8,128)} %pool.1), calls=%async_computation | async-start | bytes 524288 | tf_op jit(solution)/shard_map/all_to_all | solution.py:447
  127.4 6.8 %all-to-all-done = f32[8,8,1024]{2,1,0:T(8,128)S(1)} async-done(((f32[8,8,1024]{2,1,0:T(8,128)}), f32[8,8,1024]{2,1,0:T(8,128)S(1)}, u32[]{:S(2)}, u32[]{:S(2)}) %all-to-all-start) | async-done | bytes 262176 | tf_op jit(solution)/shard_map/all_to_all | solution.py:447
  134.2 4.9 %all_gather.7.pooled_ref = f32[16,8,1024]{2,1,0:T(8,128)S(1)} all-gather(f32[8,8,1024]{2,1,0:T(8,128)S(1)} %all-to-all-done), channel_id=1, replica_groups={{0,8},{16,24},{32,40},{48,56},{64,72},{80,88},{96,104},{112,120},{128,1..., dimensions={0}, use_global_device_ids=true | all-gather | bytes 786432 | tf_op jit(solution)/shard_map/all_gather | solution.py:448
  141.6 5.8 %all-to-all-start.1 = ((bf16[16,8,1024]{2,1,0:T(8,128)(2,1)}), bf16[16,8,1024]{2,1,0:T(8,128)(2,1)S(1)}, u32[]{:S(2)}, u32[]{:S(2)}) async-start(bf16[16,8,1024]{2,1,0:T(8,128)(2,1)} %bitcast.7), calls=%async_computation.1 | async-start | bytes 524288 | tf_op jit(solution)/shard_map/all_to_all | solution.py:458
  147.4 8.1 %all-to-all-done.1 = bf16[16,8,1024]{2,1,0:T(8,128)(2,1)S(1)} async-done(((bf16[16,8,1024]{2,1,0:T(8,128)(2,1)}), bf16[16,8,1024]{2,1,0:T(8,128)(2,1)S(1)}, u32[]{:S(2)}, u32[]{:S(2)}) %all-to-all-start.1) | async-done | bytes 262176 | tf_op jit(solution)/shard_map/all_to_all | solution.py:458
  (93 shorter events, 37.2 us)
Async XLA Ops:
  7.2 95.3 %all-gather.2.cloned.1.call-start = ((), (), s32[]{:S(2)}) async-start(), calls=%async_computation.2 | async-start | bytes 12976128 | tf_op jit(solution)/shard_map/all_gather | solution.py:410
  7.3 22.9 %collective-permute-start = (bf16[1024,128]{1,0:T(8,128)(2,1)}, bf16[1024,128]{1,0:T(8,128)(2,1)S(1)}, u32[]{:S(2)}, u32[]{:S(2)}) collective-permute-start(bf16[1024,128]{1,0:T(8,128)(2,1)} %refs_0_.10), channel_id=1, source_target_pairs={{0,7},{1,0},{2,1},{3,2},{4,3},{5,4},{6,5},{7,6},{8,15},{9,8},{10,9... | collective-permute-start | bytes 786440 | tf_op jit(solution)/shard_map/ppermute | solution.py:359
  13.8 16.4 %collective-permute-start.3 = (bf16[1024,128]{1,0:T(8,128)(2,1)}, bf16[1024,128]{1,0:T(8,128)(2,1)}, u32[]{:S(2)}, u32[]{:S(2)}) collective-permute-start(bf16[1024,128]{1,0:T(8,128)(2,1)} %refs_0_.10), channel_id=1, source_target_pairs={{0,1},{1,2},{2,3},{3,4},{4,5},{5,6},{6,7},{7,0},{8,9},{9,10},{10,1... | collective-permute-start | bytes 786440 | tf_op jit(solution)/shard_map/ppermute | solution.py:359
  14.7 10.3 %collective-permute-start.16 = (bf16[64,1024]{1,0:T(8,128)(2,1)S(1)}, bf16[64,1024]{1,0:T(8,128)(2,1)S(1)}, u32[]{:S(2)}, u32[]{:S(2)}) collective-permute-start(bf16[64,1024]{1,0:T(8,128)(2,1)S(1)} %pad_maximum_fusion.1), channel_id=1, source_target_pairs={{0,2},{1,3},{2,4},{3,5},{4,6},{5,7},{6,0},{7,1},{8,10},{9,11},{10,... | collective-permute-start | bytes 393224 | tf_op jit(solution)/shard_map/ppermute | solution.py:359
  14.8 12.0 %collective-permute-start.17 = (bf16[64,1024]{1,0:T(8,128)(2,1)S(1)}, bf16[64,1024]{1,0:T(8,128)(2,1)S(1)}, u32[]{:S(2)}, u32[]{:S(2)}) collective-permute-start(bf16[64,1024]{1,0:T(8,128)(2,1)S(1)} %pad_maximum_fusion.1), channel_id=1, source_target_pairs={{0,6},{1,7},{2,0},{3,1},{4,2},{5,3},{6,4},{7,5},{8,14},{9,15},{10,... | collective-permute-start | bytes 393224 | tf_op jit(solution)/shard_map/ppermute | solution.py:359
  18.3 11.9 %collective-permute-start.18 = (bf16[64,1024]{1,0:T(8,128)(2,1)S(1)}, bf16[64,1024]{1,0:T(8,128)(2,1)S(1)}, u32[]{:S(2)}, u32[]{:S(2)}) collective-permute-start(bf16[64,1024]{1,0:T(8,128)(2,1)S(1)} %pad_maximum_fusion.1), channel_id=1, source_target_pairs={{0,5},{1,4},{2,7},{3,6},{4,1},{5,0},{6,3},{7,2},{8,13},{9,12},{10,... | collective-permute-start | bytes 393224 | tf_op jit(solution)/shard_map/ppermute | solution.py:368
  31.1 6.2 %collective-permute-start.1 = (bf16[1024,128]{1,0:T(8,128)(2,1)S(1)}, bf16[1024,128]{1,0:T(8,128)(2,1)}, u32[]{:S(2)}, u32[]{:S(2)}) collective-permute-start(bf16[1024,128]{1,0:T(8,128)(2,1)S(1)} %collective-permute-done.refs_1_), channel_id=1, source_target_pairs={{0,7},{1,0},{2,1},{3,2},{4,3},{5,4},{6,5},{7,6},{8,15},{9,8},{10,9... | collective-permute-start | bytes 786440 | tf_op jit(solution)/shard_map/ppermute | solution.py:359
  33.5 7.3 %collective-permute-start.4 = (bf16[1024,128]{1,0:T(8,128)(2,1)}, bf16[1024,128]{1,0:T(8,128)(2,1)}, u32[]{:S(2)}, u32[]{:S(2)}) collective-permute-start(bf16[1024,128]{1,0:T(8,128)(2,1)} %collective-permute-done.3.refs_6_), channel_id=1, source_target_pairs={{0,1},{1,2},{2,3},{3,4},{4,5},{5,6},{6,7},{7,0},{8,9},{9,10},{10,1... | collective-permute-start | bytes 786440 | tf_op jit(solution)/shard_map/ppermute | solution.py:359
  37.3 11.4 %collective-permute-start.2 = (bf16[1024,128]{1,0:T(8,128)(2,1)}, bf16[1024,128]{1,0:T(8,128)(2,1)S(1)}, u32[]{:S(2)}, u32[]{:S(2)}) collective-permute-start(bf16[1024,128]{1,0:T(8,128)(2,1)} %collective-permute-done.1.refs_2_), channel_id=1, source_target_pairs={{0,7},{1,0},{2,1},{3,2},{4,3},{5,4},{6,5},{7,6},{8,15},{9,8},{10,9... | collective-permute-start | bytes 786440 | tf_op jit(solution)/shard_map/ppermute | solution.py:359
  40.8 6.7 %collective-permute-start.5 = (bf16[1024,128]{1,0:T(8,128)(2,1)}, bf16[1024,128]{1,0:T(8,128)(2,1)}, u32[]{:S(2)}, u32[]{:S(2)}) collective-permute-start(bf16[1024,128]{1,0:T(8,128)(2,1)} %collective-permute-done.4.refs_7_), channel_id=1, source_target_pairs={{0,1},{1,2},{2,3},{3,4},{4,5},{5,6},{6,7},{7,0},{8,9},{9,10},{10,1... | collective-permute-start | bytes 786440 | tf_op jit(solution)/shard_map/ppermute | solution.py:359
  48.5 5.1 %collective-permute-start.6 = (bf16[512,128]{1,0:T(8,128)(2,1)S(1)}, bf16[512,128]{1,0:T(8,128)(2,1)S(1)}, u32[]{:S(2)}, u32[]{:S(2)}) collective-permute-start(bf16[512,128]{1,0:T(8,128)(2,1)S(1)} %slice.8), channel_id=1, source_target_pairs={{0,1},{1,2},{2,3},{3,4},{4,5},{5,6},{6,7},{7,0},{8,9},{9,10},{10,1... | collective-permute-start | bytes 393224 | tf_op jit(solution)/shard_map/ppermute | solution.py:359
  48.6 5.0 %collective-permute-start.7 = (bf16[512,128]{1,0:T(8,128)(2,1)S(1)}, bf16[512,128]{1,0:T(8,128)(2,1)S(1)}, u32[]{:S(2)}, u32[]{:S(2)}) collective-permute-start(bf16[512,128]{1,0:T(8,128)(2,1)S(1)} %slice.9), channel_id=1, source_target_pairs={{0,7},{1,0},{2,1},{3,2},{4,3},{5,4},{6,5},{7,6},{8,15},{9,8},{10,9... | collective-permute-start | bytes 393224 | tf_op jit(solution)/shard_map/ppermute | solution.py:359
  57.1 6.2 %collective-permute-start.8 = (bf16[64,1024]{1,0:T(8,128)(2,1)S(1)}, bf16[64,1024]{1,0:T(8,128)(2,1)S(1)}, u32[]{:S(2)}, u32[]{:S(2)}) collective-permute-start(bf16[64,1024]{1,0:T(8,128)(2,1)S(1)} %get-tuple-element.9), channel_id=1, source_target_pairs={{0,1},{1,2},{2,3},{3,4},{4,5},{5,6},{6,7},{7,0},{8,9},{9,10},{10,1... | collective-permute-start | bytes 393224 | tf_op jit(solution)/shard_map/ppermute | solution.py:359
  57.1 6.7 %collective-permute-start.12 = (bf16[64,1024]{1,0:T(8,128)(2,1)S(1)}, bf16[64,1024]{1,0:T(8,128)(2,1)S(1)}, u32[]{:S(2)}, u32[]{:S(2)}) collective-permute-start(bf16[64,1024]{1,0:T(8,128)(2,1)S(1)} %get-tuple-element.10), channel_id=1, source_target_pairs={{0,7},{1,0},{2,1},{3,2},{4,3},{5,4},{6,5},{7,6},{8,15},{9,8},{10,9... | collective-permute-start | bytes 393224 | tf_op jit(solution)/shard_map/ppermute | solution.py:359
  63.5 7.2 %collective-permute-start.9 = (bf16[128,1024]{1,0:T(8,128)(2,1)S(1)}, bf16[128,1024]{1,0:T(8,128)(2,1)S(1)}, u32[]{:S(2)}, u32[]{:S(2)}) collective-permute-start(bf16[128,1024]{1,0:T(8,128)(2,1)S(1)} %join.8), channel_id=1, source_target_pairs={{0,1},{1,2},{2,3},{3,4},{4,5},{5,6},{6,7},{7,0},{8,9},{9,10},{10,1... | collective-permute-start | bytes 786440 | tf_op jit(solution)/shard_map/ppermute | solution.py:359
  64.0 7.1 %collective-permute-start.13 = (bf16[128,1024]{1,0:T(8,128)(2,1)S(1)}, bf16[128,1024]{1,0:T(8,128)(2,1)S(1)}, u32[]{:S(2)}, u32[]{:S(2)}) collective-permute-start(bf16[128,1024]{1,0:T(8,128)(2,1)S(1)} %join.11), channel_id=1, source_target_pairs={{0,7},{1,0},{2,1},{3,2},{4,3},{5,4},{6,5},{7,6},{8,15},{9,8},{10,9... | collective-permute-start | bytes 786440 | tf_op jit(solution)/shard_map/ppermute | solution.py:359
  71.0 8.8 %collective-permute-start.10 = (bf16[128,1024]{1,0:T(8,128)(2,1)S(1)}, bf16[128,1024]{1,0:T(8,128)(2,1)S(1)}, u32[]{:S(2)}, u32[]{:S(2)}) collective-permute-start(bf16[128,1024]{1,0:T(8,128)(2,1)S(1)} %join.9), channel_id=1, source_target_pairs={{0,1},{1,2},{2,3},{3,4},{4,5},{5,6},{6,7},{7,0},{8,9},{9,10},{10,1... | collective-permute-start | bytes 786440 | tf_op jit(solution)/shard_map/ppermute | solution.py:359
  71.3 8.8 %collective-permute-start.14 = (bf16[128,1024]{1,0:T(8,128)(2,1)S(1)}, bf16[128,1024]{1,0:T(8,128)(2,1)S(1)}, u32[]{:S(2)}, u32[]{:S(2)}) collective-permute-start(bf16[128,1024]{1,0:T(8,128)(2,1)S(1)} %join.12), channel_id=1, source_target_pairs={{0,7},{1,0},{2,1},{3,2},{4,3},{5,4},{6,5},{7,6},{8,15},{9,8},{10,9... | collective-permute-start | bytes 786440 | tf_op jit(solution)/shard_map/ppermute | solution.py:359
  80.0 9.6 %collective-permute-start.11 = (bf16[128,1024]{1,0:T(8,128)(2,1)S(1)}, bf16[128,1024]{1,0:T(8,128)(2,1)S(1)}, u32[]{:S(2)}, u32[]{:S(2)}) collective-permute-start(bf16[128,1024]{1,0:T(8,128)(2,1)S(1)} %join.10), channel_id=1, source_target_pairs={{0,1},{1,2},{2,3},{3,4},{4,5},{5,6},{6,7},{7,0},{8,9},{9,10},{10,1... | collective-permute-start | bytes 786440 | tf_op jit(solution)/shard_map/ppermute | solution.py:359
  80.3 9.3 %collective-permute-start.15 = (bf16[128,1024]{1,0:T(8,128)(2,1)S(1)}, bf16[128,1024]{1,0:T(8,128)(2,1)S(1)}, u32[]{:S(2)}, u32[]{:S(2)}) collective-permute-start(bf16[128,1024]{1,0:T(8,128)(2,1)S(1)} %join.13), channel_id=1, source_target_pairs={{0,7},{1,0},{2,1},{3,2},{4,3},{5,4},{6,5},{7,6},{8,15},{9,8},{10,9... | collective-permute-start | bytes 786440 | tf_op jit(solution)/shard_map/ppermute | solution.py:359
  89.9 7.7 %collective-permute-start.19 = (bf16[128,1024]{1,0:T(8,128)(2,1)S(1)}, bf16[128,1024]{1,0:T(8,128)(2,1)S(1)}, u32[]{:S(2)}, u32[]{:S(2)}) collective-permute-start(bf16[128,1024]{1,0:T(8,128)(2,1)S(1)} %get-tuple-element.11.rows_ref), channel_id=1, source_target_pairs={{0,1},{1,0},{2,3},{3,2},{4,5},{5,4},{6,7},{7,6},{8,9},{9,8},{10,11... | collective-permute-start | bytes 786440 | tf_op jit(solution)/shard_map/ppermute | solution.py:362
  109.0 8.2 %collective-permute-start.20 = (bf16[128,1024]{1,0:T(8,128)(2,1)S(1)}, bf16[128,1024]{1,0:T(8,128)(2,1)S(1)}, u32[]{:S(2)}, u32[]{:S(2)}) collective-permute-start(bf16[128,1024]{1,0:T(8,128)(2,1)S(1)} %feed.3), channel_id=1, source_target_pairs={{0,1},{1,0},{2,3},{3,2},{4,5},{5,4},{6,7},{7,6},{8,9},{9,8},{10,11... | collective-permute-start | bytes 786440 | tf_op jit(solution)/shard_map/ppermute | solution.py:362
  118.5 15.8 %all-to-all-start = ((f32[8,8,1024]{2,1,0:T(8,128)}), f32[8,8,1024]{2,1,0:T(8,128)S(1)}, u32[]{:S(2)}, u32[]{:S(2)}) async-start(f32[8,8,1024]{2,1,0:T(8,128)} %pool.1), calls=%async_computation | async-start | bytes 524288 | tf_op jit(solution)/shard_map/all_to_all | solution.py:447
  141.6 13.9 %all-to-all-start.1 = ((bf16[16,8,1024]{2,1,0:T(8,128)(2,1)}), bf16[16,8,1024]{2,1,0:T(8,128)(2,1)S(1)}, u32[]{:S(2)}, u32[]{:S(2)}) async-start(bf16[16,8,1024]{2,1,0:T(8,128)(2,1)} %bitcast.7), calls=%async_computation.1 | async-start | bytes 524288 | tf_op jit(solution)/shard_map/all_to_all | solution.py:458
  (13 other events, 419.6 us)
Sparse Core Ops, SparseCore 0:
  31.2 71.3 all-gather.1

commit v7 on v6

--- a/solution.py
+++ b/solution.py
@@ -129,10 +129,13 @@
     smem = pl.BlockSpec(memory_space=pltpu.SMEM)
     vmem = pl.BlockSpec(memory_space=pltpu.VMEM)
     hbm = pl.BlockSpec(memory_space=pltpu.HBM)
-    pieces = [pltpu.with_memory_space_constraint(p, pltpu.HBM) for p in pieces]
+    half = parts // 2
+    pieces = [
+        p if k in (half, half + 1) else pltpu.with_memory_space_constraint(p, pltpu.HBM) for k, p in enumerate(pieces)
+    ]
     return pl.pallas_call(
         functools.partial(attention_kernel, offsets, parts, chunk, with_base),
-        in_specs=[smem, smem] + [hbm] * len(pieces) + [vmem] * 4,
+        in_specs=[smem, smem] + [hbm if k not in (half, half + 1) else pl.BlockSpec(memory_space=pl.ANY) for k in range(parts + 1)] + [vmem] * 4,
         out_specs=vmem,
         out_shape=jax.ShapeDtypeStruct((size * chunk, width if with_base else local), F32 if with_base else BF),
         scratch_shapes=[pltpu.VMEM((size, chunk, width), BF), pltpu.SemaphoreType.DMA((size, parts))],

time: 165 us -> 164 us (level)
  no operation moved by 1% of the time
where the time goes in v7:
time: 164 us; the launch traced here: 163 us
  waiting for transfers between devices  55.3 us (34%)
  starting transfers between devices  48.2 us (29%)
  Pallas kernels  35 us (21%)
  between operations  14.4 us (9%)
  blocking collectives  4.84 us (3%)
  other arithmetic  3.03 us (2%)
  local copies, waits for them, and re-layouts  2.35 us (1%)
    ppermute x18, starting transfers between devices, move(): lax.ppermute(array, 'sub', [(i, (i + by) % sub_count) for i in range(sub_...  30.6 us
    ppermute x18, waiting for transfers between devices, move(): lax.ppermute(array, 'sub', [(i, (i + by) % sub_count) for i in range(sub_...  24 us
    pallas_call x5, Pallas kernels, attention(): pl.pallas_call(functools.partial(attention_kernel, offsets, parts, chunk,...  15.1 us
    pallas_call x2, Pallas kernels, feed(): pl.pallas_call(feed_kernel, in_specs=[vmem] * (1 + len(hidden)) + [hbm] *...  12.8 us
    all_to_all x1, waiting for transfers between devices, on_device(): lax.all_to_all(sent.reshape(chips, PACK, width), 'dp', split_axis=0, conc...  8.1 us
    ppermute x2, waiting for transfers between devices, swap(): return lax.ppermute(array, 'sub', [(i, i ^ 1) for i in range(sub_count)])  7.52 us
    pallas_call x11, Pallas kernels, small_call(): pl.pallas_call(kernel, in_specs=specs, out_specs=pl.BlockSpec(memory_spac...  7.11 us
    all_to_all x1, waiting for transfers between devices, on_device(): lax.all_to_all(pooled, 'sub', split_axis=0, concat_axis=0, tiled=True)  7.01 us
  transfers between devices with their start and end apart: 25, of which 15 were waited for; matrix products, arithmetic and copies ran while one was open for 3% of the time, Pallas kernels for 14%

profile of v7, /device:TPU:1, one launch (start us, length us, event | category | flops | bytes accessed | tf_op | source)
XLA Modules:
  0.0 163.2 jit_solution(17173838533777103084)
XLA Ops:
  7.3 6.5 %collective-permute-start = (bf16[1024,128]{1,0:T(8,128)(2,1)}, bf16[1024,128]{1,0:T(8,128)(2,1)S(1)}, u32[]{:S(2)}, u32[]{:S(2)}) collective-permute-start(bf16[1024,128]{1,0:T(8,128)(2,1)} %refs_0_.10), channel_id=1, source_target_pairs={{0,7},{1,0},{2,1},{3,2},{4,3},{5,4},{6,5},{7,6},{8,15},{9,8},{10,9... | collective-permute-start | bytes 786440 | tf_op jit(solution)/shard_map/ppermute | solution.py:362
  14.8 3.6 %collective-permute-start.17 = (bf16[64,1024]{1,0:T(8,128)(2,1)S(1)}, bf16[64,1024]{1,0:T(8,128)(2,1)S(1)}, u32[]{:S(2)}, u32[]{:S(2)}) collective-permute-start(bf16[64,1024]{1,0:T(8,128)(2,1)S(1)} %pad_maximum_fusion.1), channel_id=1, source_target_pairs={{0,6},{1,7},{2,0},{3,1},{4,2},{5,3},{6,4},{7,5},{8,14},{9,15},{10,... | collective-permute-start | bytes 393224 | tf_op jit(solution)/shard_map/ppermute | solution.py:362
  20.7 4.3 %collective-permute-done.16 = bf16[64,1024]{1,0:T(8,128)(2,1)S(1)} collective-permute-done((bf16[64,1024]{1,0:T(8,128)(2,1)S(1)}, bf16[64,1024]{1,0:T(8,128)(2,1)S(1)}, u32[]{:S(2)}, u32[]{:S(2)}) %collective-permute-start.16) | collective-permute-done | bytes 131104 | tf_op jit(solution)/shard_map/ppermute | solution.py:362
  26.7 3.5 %collective-permute-done.18 = bf16[64,1024]{1,0:T(8,128)(2,1)S(1)} collective-permute-done((bf16[64,1024]{1,0:T(8,128)(2,1)S(1)}, bf16[64,1024]{1,0:T(8,128)(2,1)S(1)}, u32[]{:S(2)}, u32[]{:S(2)}) %collective-permute-start.18) | collective-permute-done | bytes 131104 | tf_op jit(solution)/shard_map/ppermute | solution.py:371
  37.3 3.5 %collective-permute-start.2 = (bf16[1024,128]{1,0:T(8,128)(2,1)}, bf16[1024,128]{1,0:T(8,128)(2,1)S(1)}, u32[]{:S(2)}, u32[]{:S(2)}) collective-permute-start(bf16[1024,128]{1,0:T(8,128)(2,1)} %collective-permute-done.1.refs_2_), channel_id=1, source_target_pairs={{0,7},{1,0},{2,1},{3,2},{4,3},{5,4},{6,5},{7,6},{8,15},{9,8},{10,9... | collective-permute-start | bytes 786440 | tf_op jit(solution)/shard_map/ppermute | solution.py:362
  41.0 6.6 %collective-permute-done.5.refs_8_ = bf16[1024,128]{1,0:T(8,128)(2,1)} collective-permute-done((bf16[1024,128]{1,0:T(8,128)(2,1)}, bf16[1024,128]{1,0:T(8,128)(2,1)}, u32[]{:S(2)}, u32[]{:S(2)}) %collective-permute-start.5) | collective-permute-done | bytes 262176 | tf_op jit(solution)/shard_map/ppermute | solution.py:362
  56.5 2.8 %collective-permute-start.12 = (bf16[64,1024]{1,0:T(8,128)(2,1)S(1)}, bf16[64,1024]{1,0:T(8,128)(2,1)S(1)}, u32[]{:S(2)}, u32[]{:S(2)}) collective-permute-start(bf16[64,1024]{1,0:T(8,128)(2,1)S(1)} %get-tuple-element.10), channel_id=1, source_target_pairs={{0,7},{1,0},{2,1},{3,2},{4,3},{5,4},{6,5},{7,6},{8,15},{9,8},{10,9... | collective-permute-start | bytes 393224 | tf_op jit(solution)/shard_map/ppermute | solution.py:362
  59.3 3.3 %attention.8.context_ref = bf16[256,128]{1,0:T(8,128)(2,1)S(1)} custom-call(s32[1]{0:T(128)} %bitcast.3.me_ref, s32[2,32]{1,0:T(2,128)S(1)} %bitcast.12, bf16[1024,128]{1,0:T(8,128)(2,1)} %refs_0_.10, bf16[1024,128]{1,0:T(8,128)(2,1)} %copy-done.8, bf16[1024,128]{1,0:T(8,128)(2,1)} %collective-permute-done.1.refs_2_, bf16[1024,128]{1,0:T(8,128)(2,1)} %copy-done.7, ...), custom_call_target="tpu_custom_call" | custom-call | flops 10737418240 | bytes 3145728 | tf_op jit(solution)/shard_map/attention/pallas_call | solution.py:136
  63.2 2.7 %collective-permute-start.13 = (bf16[128,1024]{1,0:T(8,128)(2,1)S(1)}, bf16[128,1024]{1,0:T(8,128)(2,1)S(1)}, u32[]{:S(2)}, u32[]{:S(2)}) collective-permute-start(bf16[128,1024]{1,0:T(8,128)(2,1)S(1)} %join.11), channel_id=1, source_target_pairs={{0,7},{1,0},{2,1},{3,2},{4,3},{5,4},{6,5},{7,6},{8,15},{9,8},{10,9... | collective-permute-start | bytes 786440 | tf_op jit(solution)/shard_map/ppermute | solution.py:362
  65.9 3.3 %attention.7.context_ref = bf16[256,128]{1,0:T(8,128)(2,1)S(1)} custom-call(s32[1]{0:T(128)} %bitcast.3.me_ref, s32[2,32]{1,0:T(2,128)S(1)} %bitcast.13, bf16[1024,128]{1,0:T(8,128)(2,1)} %refs_0_.10, bf16[1024,128]{1,0:T(8,128)(2,1)} %copy-done.8, bf16[1024,128]{1,0:T(8,128)(2,1)} %collective-permute-done.1.refs_2_, bf16[1024,128]{1,0:T(8,128)(2,1)} %copy-done.7, ...), custom_call_target="tpu_custom_call" | custom-call | flops 10737418240 | bytes 3145728 | tf_op jit(solution)/shard_map/attention/pallas_call | solution.py:136
  70.7 2.8 %collective-permute-start.14 = (bf16[128,1024]{1,0:T(8,128)(2,1)S(1)}, bf16[128,1024]{1,0:T(8,128)(2,1)S(1)}, u32[]{:S(2)}, u32[]{:S(2)}) collective-permute-start(bf16[128,1024]{1,0:T(8,128)(2,1)S(1)} %join.12), channel_id=1, source_target_pairs={{0,7},{1,0},{2,1},{3,2},{4,3},{5,4},{6,5},{7,6},{8,15},{9,8},{10,9... | collective-permute-start | bytes 786440 | tf_op jit(solution)/shard_map/ppermute | solution.py:362
  73.5 3.3 %attention.6.context_ref = bf16[256,128]{1,0:T(8,128)(2,1)S(1)} custom-call(s32[1]{0:T(128)} %bitcast.3.me_ref, s32[2,32]{1,0:T(2,128)S(1)} %bitcast.14, bf16[1024,128]{1,0:T(8,128)(2,1)} %refs_0_.10, bf16[1024,128]{1,0:T(8,128)(2,1)} %copy-done.8, bf16[1024,128]{1,0:T(8,128)(2,1)} %collective-permute-done.1.refs_2_, bf16[1024,128]{1,0:T(8,128)(2,1)} %copy-done.7, ...), custom_call_target="tpu_custom_call" | custom-call | flops 10737418240 | bytes 3145728 | tf_op jit(solution)/shard_map/attention/pallas_call | solution.py:136
  79.8 3.0 %collective-permute-start.15 = (bf16[128,1024]{1,0:T(8,128)(2,1)S(1)}, bf16[128,1024]{1,0:T(8,128)(2,1)S(1)}, u32[]{:S(2)}, u32[]{:S(2)}) collective-permute-start(bf16[128,1024]{1,0:T(8,128)(2,1)S(1)} %join.13), channel_id=1, source_target_pairs={{0,7},{1,0},{2,1},{3,2},{4,3},{5,4},{6,5},{7,6},{8,15},{9,8},{10,9... | collective-permute-start | bytes 786440 | tf_op jit(solution)/shard_map/ppermute | solution.py:362
  82.8 2.7 %attention.5.base_ref = f32[128,1024]{1,0:T(8,128)S(1)} custom-call(s32[1]{0:T(128)} %bitcast.3.me_ref, s32[2,32]{1,0:T(2,128)S(1)} %bitcast.15, bf16[1024,128]{1,0:T(8,128)(2,1)} %refs_0_.10, bf16[1024,128]{1,0:T(8,128)(2,1)} %copy-done.8, bf16[1024,128]{1,0:T(8,128)(2,1)} %collective-permute-done.1.refs_2_, bf16[1024,128]{1,0:T(8,128)(2,1)} %copy-done.7, ...), custom_call_target="tpu_custom_call" | custom-call | flops 5368709120 | bytes 3145728 | tf_op jit(solution)/shard_map/attention/pallas_call | solution.py:136
  85.5 3.6 %collective-permute-done.11.right_ref = bf16[128,1024]{1,0:T(8,128)(2,1)S(1)} collective-permute-done((bf16[128,1024]{1,0:T(8,128)(2,1)S(1)}, bf16[128,1024]{1,0:T(8,128)(2,1)S(1)}, u32[]{:S(2)}, u32[]{:S(2)}) %collective-permute-start.11) | collective-permute-done | bytes 262176 | tf_op jit(solution)/shard_map/ppermute | solution.py:362
  89.9 7.5 %collective-permute-done.19.rows_ref = bf16[128,1024]{1,0:T(8,128)(2,1)S(1)} collective-permute-done((bf16[128,1024]{1,0:T(8,128)(2,1)S(1)}, bf16[128,1024]{1,0:T(8,128)(2,1)S(1)}, u32[]{:S(2)}, u32[]{:S(2)}) %collective-permute-start.19) | collective-permute-done | bytes 262176 | tf_op jit(solution)/shard_map/ppermute | solution.py:365
  97.4 4.6 %all-gather.2.cloned.1.call-done = bf16[6144,1024]{1,0:T(8,128)(2,1)} async-done(((bf16[192,1024]{1,0:T(8,128)(2,1)}), bf16[6144,1024]{1,0:T(8,128)(2,1)}) %all-gather.2.cloned.1.call-update) | async-done | bytes 12582928 | tf_op jit(solution)/shard_map/all_gather | solution.py:413
  102.0 6.4 %feed.3 = bf16[128,1024]{1,0:T(8,128)(2,1)S(1)} custom-call(bf16[128,1024]{1,0:T(8,128)(2,1)S(1)} %collective-permute-done.19.rows_ref, bf16[1024,1024]{1,0:T(8,128)(2,1)} %refs_0_.11, bf16[1024,1024]{1,0:T(8,128)(2,1)} %refs_1_.3, bf16[32,3,64,1024]{3,2,1,0:T(8,128)(2,1)} %bitcast.16), custom_call_target="tpu_custom_call" | custom-call | flops 2147483648 | bytes 16777216 | tf_op jit(solution)/shard_map/feed/pallas_call | solution.py:209
  110.0 6.4 %feed.2.hidden_ref = f32[128,1024]{1,0:T(8,128)S(1)} custom-call(bf16[128,1024]{1,0:T(8,128)(2,1)S(1)} %get-tuple-element.11.rows_ref, f32[128,1024]{1,0:T(8,128)S(1)} %get-tuple-element.12.refs_0_, bf16[1024,1024]{1,0:T(8,128)(2,1)} %refs_0_.11, bf16[1024,1024]{1,0:T(8,128)(2,1)} %refs_1_.3, bf16[32,3,64,1024]{3,2,1,0:T(8,128)(2,1)} %bitcast.17), custom_call_target="tpu_custom_call" | custom-call | flops 2147483648 | bytes 16777216 | tf_op jit(solution)/shard_map/feed/pallas_call | solution.py:209
  117.7 6.2 %all-to-all-start = ((f32[8,8,1024]{2,1,0:T(8,128)}), f32[8,8,1024]{2,1,0:T(8,128)S(1)}, u32[]{:S(2)}, u32[]{:S(2)}) async-start(f32[8,8,1024]{2,1,0:T(8,128)} %pool.1), calls=%async_computation | async-start | bytes 524288 | tf_op jit(solution)/shard_map/all_to_all | solution.py:450
  126.6 7.0 %all-to-all-done = f32[8,8,1024]{2,1,0:T(8,128)S(1)} async-done(((f32[8,8,1024]{2,1,0:T(8,128)}), f32[8,8,1024]{2,1,0:T(8,128)S(1)}, u32[]{:S(2)}, u32[]{:S(2)}) %all-to-all-start) | async-done | bytes 262176 | tf_op jit(solution)/shard_map/all_to_all | solution.py:450
  133.7 4.8 %all_gather.7.pooled_ref = f32[16,8,1024]{2,1,0:T(8,128)S(1)} all-gather(f32[8,8,1024]{2,1,0:T(8,128)S(1)} %all-to-all-done), channel_id=1, replica_groups={{0,8},{16,24},{32,40},{48,56},{64,72},{80,88},{96,104},{112,120},{128,1..., dimensions={0}, use_global_device_ids=true | all-gather | bytes 786432 | tf_op jit(solution)/shard_map/all_gather | solution.py:451
  140.9 5.6 %all-to-all-start.1 = ((bf16[16,8,1024]{2,1,0:T(8,128)(2,1)}), bf16[16,8,1024]{2,1,0:T(8,128)(2,1)S(1)}, u32[]{:S(2)}, u32[]{:S(2)}) async-start(bf16[16,8,1024]{2,1,0:T(8,128)(2,1)} %bitcast.7), calls=%async_computation.1 | async-start | bytes 524288 | tf_op jit(solution)/shard_map/all_to_all | solution.py:461
  146.5 8.1 %all-to-all-done.1 = bf16[16,8,1024]{2,1,0:T(8,128)(2,1)S(1)} async-done(((bf16[16,8,1024]{2,1,0:T(8,128)(2,1)}), bf16[16,8,1024]{2,1,0:T(8,128)(2,1)S(1)}, u32[]{:S(2)}, u32[]{:S(2)}) %all-to-all-start.1) | async-done | bytes 262176 | tf_op jit(solution)/shard_map/all_to_all | solution.py:461
  (89 shorter events, 36.6 us)
Async XLA Ops:
  7.2 94.8 %all-gather.2.cloned.1.call-start = ((), (), s32[]{:S(2)}) async-start(), calls=%async_computation.2 | async-start | bytes 12976128 | tf_op jit(solution)/shard_map/all_gather | solution.py:413
  7.3 22.9 %collective-permute-start = (bf16[1024,128]{1,0:T(8,128)(2,1)}, bf16[1024,128]{1,0:T(8,128)(2,1)S(1)}, u32[]{:S(2)}, u32[]{:S(2)}) collective-permute-start(bf16[1024,128]{1,0:T(8,128)(2,1)} %refs_0_.10), channel_id=1, source_target_pairs={{0,7},{1,0},{2,1},{3,2},{4,3},{5,4},{6,5},{7,6},{8,15},{9,8},{10,9... | collective-permute-start | bytes 786440 | tf_op jit(solution)/shard_map/ppermute | solution.py:362
  13.8 16.4 %collective-permute-start.3 = (bf16[1024,128]{1,0:T(8,128)(2,1)}, bf16[1024,128]{1,0:T(8,128)(2,1)}, u32[]{:S(2)}, u32[]{:S(2)}) collective-permute-start(bf16[1024,128]{1,0:T(8,128)(2,1)} %refs_0_.10), channel_id=1, source_target_pairs={{0,1},{1,2},{2,3},{3,4},{4,5},{5,6},{6,7},{7,0},{8,9},{9,10},{10,1... | collective-permute-start | bytes 786440 | tf_op jit(solution)/shard_map/ppermute | solution.py:362
  14.7 10.3 %collective-permute-start.16 = (bf16[64,1024]{1,0:T(8,128)(2,1)S(1)}, bf16[64,1024]{1,0:T(8,128)(2,1)S(1)}, u32[]{:S(2)}, u32[]{:S(2)}) collective-permute-start(bf16[64,1024]{1,0:T(8,128)(2,1)S(1)} %pad_maximum_fusion.1), channel_id=1, source_target_pairs={{0,2},{1,3},{2,4},{3,5},{4,6},{5,7},{6,0},{7,1},{8,10},{9,11},{10,... | collective-permute-start | bytes 393224 | tf_op jit(solution)/shard_map/ppermute | solution.py:362
  14.8 12.0 %collective-permute-start.17 = (bf16[64,1024]{1,0:T(8,128)(2,1)S(1)}, bf16[64,1024]{1,0:T(8,128)(2,1)S(1)}, u32[]{:S(2)}, u32[]{:S(2)}) collective-permute-start(bf16[64,1024]{1,0:T(8,128)(2,1)S(1)} %pad_maximum_fusion.1), channel_id=1, source_target_pairs={{0,6},{1,7},{2,0},{3,1},{4,2},{5,3},{6,4},{7,5},{8,14},{9,15},{10,... | collective-permute-start | bytes 393224 | tf_op jit(solution)/shard_map/ppermute | solution.py:362
  18.3 11.9 %collective-permute-start.18 = (bf16[64,1024]{1,0:T(8,128)(2,1)S(1)}, bf16[64,1024]{1,0:T(8,128)(2,1)S(1)}, u32[]{:S(2)}, u32[]{:S(2)}) collective-permute-start(bf16[64,1024]{1,0:T(8,128)(2,1)S(1)} %pad_maximum_fusion.1), channel_id=1, source_target_pairs={{0,5},{1,4},{2,7},{3,6},{4,1},{5,0},{6,3},{7,2},{8,13},{9,12},{10,... | collective-permute-start | bytes 393224 | tf_op jit(solution)/shard_map/ppermute | solution.py:371
  31.1 6.2 %collective-permute-start.1 = (bf16[1024,128]{1,0:T(8,128)(2,1)S(1)}, bf16[1024,128]{1,0:T(8,128)(2,1)}, u32[]{:S(2)}, u32[]{:S(2)}) collective-permute-start(bf16[1024,128]{1,0:T(8,128)(2,1)S(1)} %collective-permute-done.refs_1_), channel_id=1, source_target_pairs={{0,7},{1,0},{2,1},{3,2},{4,3},{5,4},{6,5},{7,6},{8,15},{9,8},{10,9... | collective-permute-start | bytes 786440 | tf_op jit(solution)/shard_map/ppermute | solution.py:362
  33.5 7.3 %collective-permute-start.4 = (bf16[1024,128]{1,0:T(8,128)(2,1)}, bf16[1024,128]{1,0:T(8,128)(2,1)}, u32[]{:S(2)}, u32[]{:S(2)}) collective-permute-start(bf16[1024,128]{1,0:T(8,128)(2,1)} %collective-permute-done.3.refs_6_), channel_id=1, source_target_pairs={{0,1},{1,2},{2,3},{3,4},{4,5},{5,6},{6,7},{7,0},{8,9},{9,10},{10,1... | collective-permute-start | bytes 786440 | tf_op jit(solution)/shard_map/ppermute | solution.py:362
  37.3 11.4 %collective-permute-start.2 = (bf16[1024,128]{1,0:T(8,128)(2,1)}, bf16[1024,128]{1,0:T(8,128)(2,1)S(1)}, u32[]{:S(2)}, u32[]{:S(2)}) collective-permute-start(bf16[1024,128]{1,0:T(8,128)(2,1)} %collective-permute-done.1.refs_2_), channel_id=1, source_target_pairs={{0,7},{1,0},{2,1},{3,2},{4,3},{5,4},{6,5},{7,6},{8,15},{9,8},{10,9... | collective-permute-start | bytes 786440 | tf_op jit(solution)/shard_map/ppermute | solution.py:362
  40.9 6.7 %collective-permute-start.5 = (bf16[1024,128]{1,0:T(8,128)(2,1)}, bf16[1024,128]{1,0:T(8,128)(2,1)}, u32[]{:S(2)}, u32[]{:S(2)}) collective-permute-start(bf16[1024,128]{1,0:T(8,128)(2,1)} %collective-permute-done.4.refs_7_), channel_id=1, source_target_pairs={{0,1},{1,2},{2,3},{3,4},{4,5},{5,6},{6,7},{7,0},{8,9},{9,10},{10,1... | collective-permute-start | bytes 786440 | tf_op jit(solution)/shard_map/ppermute | solution.py:362
  48.5 5.1 %collective-permute-start.6 = (bf16[512,128]{1,0:T(8,128)(2,1)S(1)}, bf16[512,128]{1,0:T(8,128)(2,1)S(1)}, u32[]{:S(2)}, u32[]{:S(2)}) collective-permute-start(bf16[512,128]{1,0:T(8,128)(2,1)S(1)} %slice.8), channel_id=1, source_target_pairs={{0,1},{1,2},{2,3},{3,4},{4,5},{5,6},{6,7},{7,0},{8,9},{9,10},{10,1... | collective-permute-start | bytes 393224 | tf_op jit(solution)/shard_map/ppermute | solution.py:362
  48.7 5.0 %collective-permute-start.7 = (bf16[512,128]{1,0:T(8,128)(2,1)S(1)}, bf16[512,128]{1,0:T(8,128)(2,1)S(1)}, u32[]{:S(2)}, u32[]{:S(2)}) collective-permute-start(bf16[512,128]{1,0:T(8,128)(2,1)S(1)} %slice.9), channel_id=1, source_target_pairs={{0,7},{1,0},{2,1},{3,2},{4,3},{5,4},{6,5},{7,6},{8,15},{9,8},{10,9... | collective-permute-start | bytes 393224 | tf_op jit(solution)/shard_map/ppermute | solution.py:362
  56.4 6.3 %collective-permute-start.8 = (bf16[64,1024]{1,0:T(8,128)(2,1)S(1)}, bf16[64,1024]{1,0:T(8,128)(2,1)S(1)}, u32[]{:S(2)}, u32[]{:S(2)}) collective-permute-start(bf16[64,1024]{1,0:T(8,128)(2,1)S(1)} %get-tuple-element.9), channel_id=1, source_target_pairs={{0,1},{1,2},{2,3},{3,4},{4,5},{5,6},{6,7},{7,0},{8,9},{9,10},{10,1... | collective-permute-start | bytes 393224 | tf_op jit(solution)/shard_map/ppermute | solution.py:362
  56.5 6.5 %collective-permute-start.12 = (bf16[64,1024]{1,0:T(8,128)(2,1)S(1)}, bf16[64,1024]{1,0:T(8,128)(2,1)S(1)}, u32[]{:S(2)}, u32[]{:S(2)}) collective-permute-start(bf16[64,1024]{1,0:T(8,128)(2,1)S(1)} %get-tuple-element.10), channel_id=1, source_target_pairs={{0,7},{1,0},{2,1},{3,2},{4,3},{5,4},{6,5},{7,6},{8,15},{9,8},{10,9... | collective-permute-start | bytes 393224 | tf_op jit(solution)/shard_map/ppermute | solution.py:362
  62.9 7.3 %collective-permute-start.9 = (bf16[128,1024]{1,0:T(8,128)(2,1)S(1)}, bf16[128,1024]{1,0:T(8,128)(2,1)S(1)}, u32[]{:S(2)}, u32[]{:S(2)}) collective-permute-start(bf16[128,1024]{1,0:T(8,128)(2,1)S(1)} %join.8), channel_id=1, source_target_pairs={{0,1},{1,2},{2,3},{3,4},{4,5},{5,6},{6,7},{7,0},{8,9},{9,10},{10,1... | collective-permute-start | bytes 786440 | tf_op jit(solution)/shard_map/ppermute | solution.py:362
  63.2 7.3 %collective-permute-start.13 = (bf16[128,1024]{1,0:T(8,128)(2,1)S(1)}, bf16[128,1024]{1,0:T(8,128)(2,1)S(1)}, u32[]{:S(2)}, u32[]{:S(2)}) collective-permute-start(bf16[128,1024]{1,0:T(8,128)(2,1)S(1)} %join.11), channel_id=1, source_target_pairs={{0,7},{1,0},{2,1},{3,2},{4,3},{5,4},{6,5},{7,6},{8,15},{9,8},{10,9... | collective-permute-start | bytes 786440 | tf_op jit(solution)/shard_map/ppermute | solution.py:362
  70.3 8.9 %collective-permute-start.10 = (bf16[128,1024]{1,0:T(8,128)(2,1)S(1)}, bf16[128,1024]{1,0:T(8,128)(2,1)S(1)}, u32[]{:S(2)}, u32[]{:S(2)}) collective-permute-start(bf16[128,1024]{1,0:T(8,128)(2,1)S(1)} %join.9), channel_id=1, source_target_pairs={{0,1},{1,2},{2,3},{3,4},{4,5},{5,6},{6,7},{7,0},{8,9},{9,10},{10,1... | collective-permute-start | bytes 786440 | tf_op jit(solution)/shard_map/ppermute | solution.py:362
  70.7 8.9 %collective-permute-start.14 = (bf16[128,1024]{1,0:T(8,128)(2,1)S(1)}, bf16[128,1024]{1,0:T(8,128)(2,1)S(1)}, u32[]{:S(2)}, u32[]{:S(2)}) collective-permute-start(bf16[128,1024]{1,0:T(8,128)(2,1)S(1)} %join.12), channel_id=1, source_target_pairs={{0,7},{1,0},{2,1},{3,2},{4,3},{5,4},{6,5},{7,6},{8,15},{9,8},{10,9... | collective-permute-start | bytes 786440 | tf_op jit(solution)/shard_map/ppermute | solution.py:362
  79.4 9.6 %collective-permute-start.11 = (bf16[128,1024]{1,0:T(8,128)(2,1)S(1)}, bf16[128,1024]{1,0:T(8,128)(2,1)S(1)}, u32[]{:S(2)}, u32[]{:S(2)}) collective-permute-start(bf16[128,1024]{1,0:T(8,128)(2,1)S(1)} %join.10), channel_id=1, source_target_pairs={{0,1},{1,2},{2,3},{3,4},{4,5},{5,6},{6,7},{7,0},{8,9},{9,10},{10,1... | collective-permute-start | bytes 786440 | tf_op jit(solution)/shard_map/ppermute | solution.py:362
  79.8 9.3 %collective-permute-start.15 = (bf16[128,1024]{1,0:T(8,128)(2,1)S(1)}, bf16[128,1024]{1,0:T(8,128)(2,1)S(1)}, u32[]{:S(2)}, u32[]{:S(2)}) collective-permute-start(bf16[128,1024]{1,0:T(8,128)(2,1)S(1)} %join.13), channel_id=1, source_target_pairs={{0,7},{1,0},{2,1},{3,2},{4,3},{5,4},{6,5},{7,6},{8,15},{9,8},{10,9... | collective-permute-start | bytes 786440 | tf_op jit(solution)/shard_map/ppermute | solution.py:362
  89.3 8.1 %collective-permute-start.19 = (bf16[128,1024]{1,0:T(8,128)(2,1)S(1)}, bf16[128,1024]{1,0:T(8,128)(2,1)S(1)}, u32[]{:S(2)}, u32[]{:S(2)}) collective-permute-start(bf16[128,1024]{1,0:T(8,128)(2,1)S(1)} %get-tuple-element.11.rows_ref), channel_id=1, source_target_pairs={{0,1},{1,0},{2,3},{3,2},{4,5},{5,4},{6,7},{7,6},{8,9},{9,8},{10,11... | collective-permute-start | bytes 786440 | tf_op jit(solution)/shard_map/ppermute | solution.py:365
  108.4 8.0 %collective-permute-start.20 = (bf16[128,1024]{1,0:T(8,128)(2,1)S(1)}, bf16[128,1024]{1,0:T(8,128)(2,1)S(1)}, u32[]{:S(2)}, u32[]{:S(2)}) collective-permute-start(bf16[128,1024]{1,0:T(8,128)(2,1)S(1)} %feed.3), channel_id=1, source_target_pairs={{0,1},{1,0},{2,3},{3,2},{4,5},{5,4},{6,7},{7,6},{8,9},{9,8},{10,11... | collective-permute-start | bytes 786440 | tf_op jit(solution)/shard_map/ppermute | solution.py:365
  117.7 16.0 %all-to-all-start = ((f32[8,8,1024]{2,1,0:T(8,128)}), f32[8,8,1024]{2,1,0:T(8,128)S(1)}, u32[]{:S(2)}, u32[]{:S(2)}) async-start(f32[8,8,1024]{2,1,0:T(8,128)} %pool.1), calls=%async_computation | async-start | bytes 524288 | tf_op jit(solution)/shard_map/all_to_all | solution.py:450
  140.9 13.7 %all-to-all-start.1 = ((bf16[16,8,1024]{2,1,0:T(8,128)(2,1)}), bf16[16,8,1024]{2,1,0:T(8,128)(2,1)S(1)}, u32[]{:S(2)}, u32[]{:S(2)}) async-start(bf16[16,8,1024]{2,1,0:T(8,128)(2,1)} %bitcast.7), calls=%async_computation.1 | async-start | bytes 524288 | tf_op jit(solution)/shard_map/all_to_all | solution.py:461
  (11 other events, 414.0 us)
Sparse Core Ops, SparseCore 0:
  31.2 70.7 all-gather.1

commit v8 on v7

--- a/solution.py
+++ b/solution.py
@@ -422,16 +422,17 @@
         (attend([half]), w_out),
         name="join",
     )
-    right, left = move(right, 1), move(left, -1)
+    left, right = move(left, -1), move(right, 1)
     for away in range(half - 1, 0, -1):
-        context = attend([away, -away])
+        context = attend([-away, away])
         join = lambda at, start, recv: small_call(
             functools.partial(join_kernel, at, start),
             jax.ShapeDtypeStruct(own_shape, BF),
             (context, w_out, recv),
             name="join",
         )
-        right, left = move(join(0, 0, right), 1), move(join(1, own_rows - left.shape[0], left), -1)
+        left = move(join(0, own_rows - left.shape[0], left), -1)
+        right = move(join(1, 0, right), 1)
     base = attend([0], with_base=True)
     hidden1, normed2 = small_call(
         middle_kernel,

time: 164 us -> 164 us (level)
  no operation moved by 1% of the time
where the time goes in v8:
time: 164 us; the launch traced here: 163 us
  waiting for transfers between devices  55.3 us (34%)
  starting transfers between devices  48.2 us (29%)
  Pallas kernels  35 us (21%)
  between operations  14.4 us (9%)
  blocking collectives  4.84 us (3%)
  other arithmetic  3.03 us (2%)
  local copies, waits for them, and re-layouts  2.35 us (1%)
    ppermute x18, starting transfers between devices, move(): lax.ppermute(array, 'sub', [(i, (i + by) % sub_count) for i in range(sub_...  30.7 us
    ppermute x18, waiting for transfers between devices, move(): lax.ppermute(array, 'sub', [(i, (i + by) % sub_count) for i in range(sub_...  23.9 us
    pallas_call x5, Pallas kernels, attention(): pl.pallas_call(functools.partial(attention_kernel, offsets, parts, chunk,...  15.1 us
    pallas_call x2, Pallas kernels, feed(): pl.pallas_call(feed_kernel, in_specs=[vmem] * (1 + len(hidden)) + [hbm] *...  12.8 us
    all_to_all x1, waiting for transfers between devices, on_device(): lax.all_to_all(sent.reshape(chips, PACK, width), 'dp', split_axis=0, conc...  8.1 us
    ppermute x2, waiting for transfers between devices, swap(): return lax.ppermute(array, 'sub', [(i, i ^ 1) for i in range(sub_count)])  7.52 us
    pallas_call x11, Pallas kernels, small_call(): pl.pallas_call(kernel, in_specs=specs, out_specs=pl.BlockSpec(memory_spac...  7.1 us
    all_to_all x1, waiting for transfers between devices, on_device(): lax.all_to_all(pooled, 'sub', split_axis=0, concat_axis=0, tiled=True)  7.01 us
  transfers between devices with their start and end apart: 25, of which 15 were waited for; matrix products, arithmetic and copies ran while one was open for 3% of the time, Pallas kernels for 14%

profile of v8, /device:TPU:1, one launch (start us, length us, event | category | flops | bytes accessed | tf_op | source)
XLA Modules:
  0.0 163.2 jit_solution(11216070262204050040)
XLA Ops:
  7.3 6.5 %collective-permute-start = (bf16[1024,128]{1,0:T(8,128)(2,1)}, bf16[1024,128]{1,0:T(8,128)(2,1)S(1)}, u32[]{:S(2)}, u32[]{:S(2)}) collective-permute-start(bf16[1024,128]{1,0:T(8,128)(2,1)} %refs_0_.10), channel_id=1, source_target_pairs={{0,7},{1,0},{2,1},{3,2},{4,3},{5,4},{6,5},{7,6},{8,15},{9,8},{10,9... | collective-permute-start | bytes 786440 | tf_op jit(solution)/shard_map/ppermute | solution.py:362
  14.8 3.6 %collective-permute-start.17 = (bf16[64,1024]{1,0:T(8,128)(2,1)S(1)}, bf16[64,1024]{1,0:T(8,128)(2,1)S(1)}, u32[]{:S(2)}, u32[]{:S(2)}) collective-permute-start(bf16[64,1024]{1,0:T(8,128)(2,1)S(1)} %pad_maximum_fusion.1), channel_id=1, source_target_pairs={{0,6},{1,7},{2,0},{3,1},{4,2},{5,3},{6,4},{7,5},{8,14},{9,15},{10,... | collective-permute-start | bytes 393224 | tf_op jit(solution)/shard_map/ppermute | solution.py:362
  20.7 4.3 %collective-permute-done.16 = bf16[64,1024]{1,0:T(8,128)(2,1)S(1)} collective-permute-done((bf16[64,1024]{1,0:T(8,128)(2,1)S(1)}, bf16[64,1024]{1,0:T(8,128)(2,1)S(1)}, u32[]{:S(2)}, u32[]{:S(2)}) %collective-permute-start.16) | collective-permute-done | bytes 131104 | tf_op jit(solution)/shard_map/ppermute | solution.py:362
  26.7 3.5 %collective-permute-done.18 = bf16[64,1024]{1,0:T(8,128)(2,1)S(1)} collective-permute-done((bf16[64,1024]{1,0:T(8,128)(2,1)S(1)}, bf16[64,1024]{1,0:T(8,128)(2,1)S(1)}, u32[]{:S(2)}, u32[]{:S(2)}) %collective-permute-start.18) | collective-permute-done | bytes 131104 | tf_op jit(solution)/shard_map/ppermute | solution.py:371
  37.3 3.5 %collective-permute-start.2 = (bf16[1024,128]{1,0:T(8,128)(2,1)}, bf16[1024,128]{1,0:T(8,128)(2,1)S(1)}, u32[]{:S(2)}, u32[]{:S(2)}) collective-permute-start(bf16[1024,128]{1,0:T(8,128)(2,1)} %collective-permute-done.1.refs_2_), channel_id=1, source_target_pairs={{0,7},{1,0},{2,1},{3,2},{4,3},{5,4},{6,5},{7,6},{8,15},{9,8},{10,9... | collective-permute-start | bytes 786440 | tf_op jit(solution)/shard_map/ppermute | solution.py:362
  41.0 6.6 %collective-permute-done.5.refs_8_ = bf16[1024,128]{1,0:T(8,128)(2,1)} collective-permute-done((bf16[1024,128]{1,0:T(8,128)(2,1)}, bf16[1024,128]{1,0:T(8,128)(2,1)}, u32[]{:S(2)}, u32[]{:S(2)}) %collective-permute-start.5) | collective-permute-done | bytes 262176 | tf_op jit(solution)/shard_map/ppermute | solution.py:362
  48.7 2.7 %collective-permute-start.7 = (bf16[512,128]{1,0:T(8,128)(2,1)S(1)}, bf16[512,128]{1,0:T(8,128)(2,1)S(1)}, u32[]{:S(2)}, u32[]{:S(2)}) collective-permute-start(bf16[512,128]{1,0:T(8,128)(2,1)S(1)} %slice.9), channel_id=1, source_target_pairs={{0,7},{1,0},{2,1},{3,2},{4,3},{5,4},{6,5},{7,6},{8,15},{9,8},{10,9... | collective-permute-start | bytes 393224 | tf_op jit(solution)/shard_map/ppermute | solution.py:362
  56.5 2.8 %collective-permute-start.12 = (bf16[64,1024]{1,0:T(8,128)(2,1)S(1)}, bf16[64,1024]{1,0:T(8,128)(2,1)S(1)}, u32[]{:S(2)}, u32[]{:S(2)}) collective-permute-start(bf16[64,1024]{1,0:T(8,128)(2,1)S(1)} %get-tuple-element.10), channel_id=1, source_target_pairs={{0,7},{1,0},{2,1},{3,2},{4,3},{5,4},{6,5},{7,6},{8,15},{9,8},{10,9... | collective-permute-start | bytes 393224 | tf_op jit(solution)/shard_map/ppermute | solution.py:362
  59.3 3.3 %attention.8.context_ref = bf16[256,128]{1,0:T(8,128)(2,1)S(1)} custom-call(s32[1]{0:T(128)} %bitcast.3.me_ref, s32[2,32]{1,0:T(2,128)S(1)} %bitcast.12, bf16[1024,128]{1,0:T(8,128)(2,1)} %refs_0_.10, bf16[1024,128]{1,0:T(8,128)(2,1)} %copy-done.8, bf16[1024,128]{1,0:T(8,128)(2,1)} %collective-permute-done.1.refs_2_, bf16[1024,128]{1,0:T(8,128)(2,1)} %copy-done.7, ...), custom_call_target="tpu_custom_call" | custom-call | flops 10737418240 | bytes 3145728 | tf_op jit(solution)/shard_map/attention/pallas_call | solution.py:136
  63.2 2.7 %collective-permute-start.13 = (bf16[128,1024]{1,0:T(8,128)(2,1)S(1)}, bf16[128,1024]{1,0:T(8,128)(2,1)S(1)}, u32[]{:S(2)}, u32[]{:S(2)}) collective-permute-start(bf16[128,1024]{1,0:T(8,128)(2,1)S(1)} %join.11), channel_id=1, source_target_pairs={{0,7},{1,0},{2,1},{3,2},{4,3},{5,4},{6,5},{7,6},{8,15},{9,8},{10,9... | collective-permute-start | bytes 786440 | tf_op jit(solution)/shard_map/ppermute | solution.py:362
  65.9 3.3 %attention.7.context_ref = bf16[256,128]{1,0:T(8,128)(2,1)S(1)} custom-call(s32[1]{0:T(128)} %bitcast.3.me_ref, s32[2,32]{1,0:T(2,128)S(1)} %bitcast.13, bf16[1024,128]{1,0:T(8,128)(2,1)} %refs_0_.10, bf16[1024,128]{1,0:T(8,128)(2,1)} %copy-done.8, bf16[1024,128]{1,0:T(8,128)(2,1)} %collective-permute-done.1.refs_2_, bf16[1024,128]{1,0:T(8,128)(2,1)} %copy-done.7, ...), custom_call_target="tpu_custom_call" | custom-call | flops 10737418240 | bytes 3145728 | tf_op jit(solution)/shard_map/attention/pallas_call | solution.py:136
  70.7 2.8 %collective-permute-start.14 = (bf16[128,1024]{1,0:T(8,128)(2,1)S(1)}, bf16[128,1024]{1,0:T(8,128)(2,1)S(1)}, u32[]{:S(2)}, u32[]{:S(2)}) collective-permute-start(bf16[128,1024]{1,0:T(8,128)(2,1)S(1)} %join.12), channel_id=1, source_target_pairs={{0,7},{1,0},{2,1},{3,2},{4,3},{5,4},{6,5},{7,6},{8,15},{9,8},{10,9... | collective-permute-start | bytes 786440 | tf_op jit(solution)/shard_map/ppermute | solution.py:362
  73.5 3.3 %attention.6.context_ref = bf16[256,128]{1,0:T(8,128)(2,1)S(1)} custom-call(s32[1]{0:T(128)} %bitcast.3.me_ref, s32[2,32]{1,0:T(2,128)S(1)} %bitcast.14, bf16[1024,128]{1,0:T(8,128)(2,1)} %refs_0_.10, bf16[1024,128]{1,0:T(8,128)(2,1)} %copy-done.8, bf16[1024,128]{1,0:T(8,128)(2,1)} %collective-permute-done.1.refs_2_, bf16[1024,128]{1,0:T(8,128)(2,1)} %copy-done.7, ...), custom_call_target="tpu_custom_call" | custom-call | flops 10737418240 | bytes 3145728 | tf_op jit(solution)/shard_map/attention/pallas_call | solution.py:136
  79.7 3.0 %collective-permute-start.15 = (bf16[128,1024]{1,0:T(8,128)(2,1)S(1)}, bf16[128,1024]{1,0:T(8,128)(2,1)S(1)}, u32[]{:S(2)}, u32[]{:S(2)}) collective-permute-start(bf16[128,1024]{1,0:T(8,128)(2,1)S(1)} %join.13), channel_id=1, source_target_pairs={{0,7},{1,0},{2,1},{3,2},{4,3},{5,4},{6,5},{7,6},{8,15},{9,8},{10,9... | collective-permute-start | bytes 786440 | tf_op jit(solution)/shard_map/ppermute | solution.py:362
  85.5 3.6 %collective-permute-done.11.right_ref = bf16[128,1024]{1,0:T(8,128)(2,1)S(1)} collective-permute-done((bf16[128,1024]{1,0:T(8,128)(2,1)S(1)}, bf16[128,1024]{1,0:T(8,128)(2,1)S(1)}, u32[]{:S(2)}, u32[]{:S(2)}) %collective-permute-start.11) | collective-permute-done | bytes 262176 | tf_op jit(solution)/shard_map/ppermute | solution.py:362
  89.9 7.5 %collective-permute-done.19.rows_ref = bf16[128,1024]{1,0:T(8,128)(2,1)S(1)} collective-permute-done((bf16[128,1024]{1,0:T(8,128)(2,1)S(1)}, bf16[128,1024]{1,0:T(8,128)(2,1)S(1)}, u32[]{:S(2)}, u32[]{:S(2)}) %collective-permute-start.19) | collective-permute-done | bytes 262176 | tf_op jit(solution)/shard_map/ppermute | solution.py:365
  97.4 4.6 %all-gather.2.cloned.1.call-done = bf16[6144,1024]{1,0:T(8,128)(2,1)} async-done(((bf16[192,1024]{1,0:T(8,128)(2,1)}), bf16[6144,1024]{1,0:T(8,128)(2,1)}) %all-gather.2.cloned.1.call-update) | async-done | bytes 12582928 | tf_op jit(solution)/shard_map/all_gather | solution.py:413
  102.0 6.4 %feed.3 = bf16[128,1024]{1,0:T(8,128)(2,1)S(1)} custom-call(bf16[128,1024]{1,0:T(8,128)(2,1)S(1)} %collective-permute-done.19.rows_ref, bf16[1024,1024]{1,0:T(8,128)(2,1)} %refs_0_.11, bf16[1024,1024]{1,0:T(8,128)(2,1)} %refs_1_.3, bf16[32,3,64,1024]{3,2,1,0:T(8,128)(2,1)} %bitcast.16), custom_call_target="tpu_custom_call" | custom-call | flops 2147483648 | bytes 16777216 | tf_op jit(solution)/shard_map/feed/pallas_call | solution.py:209
  110.0 6.4 %feed.2.hidden_ref = f32[128,1024]{1,0:T(8,128)S(1)} custom-call(bf16[128,1024]{1,0:T(8,128)(2,1)S(1)} %get-tuple-element.11.rows_ref, f32[128,1024]{1,0:T(8,128)S(1)} %get-tuple-element.12.refs_0_, bf16[1024,1024]{1,0:T(8,128)(2,1)} %refs_0_.11, bf16[1024,1024]{1,0:T(8,128)(2,1)} %refs_1_.3, bf16[32,3,64,1024]{3,2,1,0:T(8,128)(2,1)} %bitcast.17), custom_call_target="tpu_custom_call" | custom-call | flops 2147483648 | bytes 16777216 | tf_op jit(solution)/shard_map/feed/pallas_call | solution.py:209
  117.7 6.2 %all-to-all-start = ((f32[8,8,1024]{2,1,0:T(8,128)}), f32[8,8,1024]{2,1,0:T(8,128)S(1)}, u32[]{:S(2)}, u32[]{:S(2)}) async-start(f32[8,8,1024]{2,1,0:T(8,128)} %pool.1), calls=%async_computation | async-start | bytes 524288 | tf_op jit(solution)/shard_map/all_to_all | solution.py:451
  126.6 7.0 %all-to-all-done = f32[8,8,1024]{2,1,0:T(8,128)S(1)} async-done(((f32[8,8,1024]{2,1,0:T(8,128)}), f32[8,8,1024]{2,1,0:T(8,128)S(1)}, u32[]{:S(2)}, u32[]{:S(2)}) %all-to-all-start) | async-done | bytes 262176 | tf_op jit(solution)/shard_map/all_to_all | solution.py:451
  133.7 4.8 %all_gather.7.pooled_ref = f32[16,8,1024]{2,1,0:T(8,128)S(1)} all-gather(f32[8,8,1024]{2,1,0:T(8,128)S(1)} %all-to-all-done), channel_id=1, replica_groups={{0,8},{16,24},{32,40},{48,56},{64,72},{80,88},{96,104},{112,120},{128,1..., dimensions={0}, use_global_device_ids=true | all-gather | bytes 786432 | tf_op jit(solution)/shard_map/all_gather | solution.py:452
  140.9 5.6 %all-to-all-start.1 = ((bf16[16,8,1024]{2,1,0:T(8,128)(2,1)}), bf16[16,8,1024]{2,1,0:T(8,128)(2,1)S(1)}, u32[]{:S(2)}, u32[]{:S(2)}) async-start(bf16[16,8,1024]{2,1,0:T(8,128)(2,1)} %bitcast.7), calls=%async_computation.1 | async-start | bytes 524288 | tf_op jit(solution)/shard_map/all_to_all | solution.py:462
  146.5 8.1 %all-to-all-done.1 = bf16[16,8,1024]{2,1,0:T(8,128)(2,1)S(1)} async-done(((bf16[16,8,1024]{2,1,0:T(8,128)(2,1)}), bf16[16,8,1024]{2,1,0:T(8,128)(2,1)S(1)}, u32[]{:S(2)}, u32[]{:S(2)}) %all-to-all-start.1) | async-done | bytes 262176 | tf_op jit(solution)/shard_map/all_to_all | solution.py:462
  (89 shorter events, 36.5 us)
Async XLA Ops:
  7.2 94.8 %all-gather.2.cloned.1.call-start = ((), (), s32[]{:S(2)}) async-start(), calls=%async_computation.2 | async-start | bytes 12976128 | tf_op jit(solution)/shard_map/all_gather | solution.py:413
  7.3 22.9 %collective-permute-start = (bf16[1024,128]{1,0:T(8,128)(2,1)}, bf16[1024,128]{1,0:T(8,128)(2,1)S(1)}, u32[]{:S(2)}, u32[]{:S(2)}) collective-permute-start(bf16[1024,128]{1,0:T(8,128)(2,1)} %refs_0_.10), channel_id=1, source_target_pairs={{0,7},{1,0},{2,1},{3,2},{4,3},{5,4},{6,5},{7,6},{8,15},{9,8},{10,9... | collective-permute-start | bytes 786440 | tf_op jit(solution)/shard_map/ppermute | solution.py:362
  13.8 16.4 %collective-permute-start.3 = (bf16[1024,128]{1,0:T(8,128)(2,1)}, bf16[1024,128]{1,0:T(8,128)(2,1)}, u32[]{:S(2)}, u32[]{:S(2)}) collective-permute-start(bf16[1024,128]{1,0:T(8,128)(2,1)} %refs_0_.10), channel_id=1, source_target_pairs={{0,1},{1,2},{2,3},{3,4},{4,5},{5,6},{6,7},{7,0},{8,9},{9,10},{10,1... | collective-permute-start | bytes 786440 | tf_op jit(solution)/shard_map/ppermute | solution.py:362
  14.7 10.3 %collective-permute-start.16 = (bf16[64,1024]{1,0:T(8,128)(2,1)S(1)}, bf16[64,1024]{1,0:T(8,128)(2,1)S(1)}, u32[]{:S(2)}, u32[]{:S(2)}) collective-permute-start(bf16[64,1024]{1,0:T(8,128)(2,1)S(1)} %pad_maximum_fusion.1), channel_id=1, source_target_pairs={{0,2},{1,3},{2,4},{3,5},{4,6},{5,7},{6,0},{7,1},{8,10},{9,11},{10,... | collective-permute-start | bytes 393224 | tf_op jit(solution)/shard_map/ppermute | solution.py:362
  14.8 12.0 %collective-permute-start.17 = (bf16[64,1024]{1,0:T(8,128)(2,1)S(1)}, bf16[64,1024]{1,0:T(8,128)(2,1)S(1)}, u32[]{:S(2)}, u32[]{:S(2)}) collective-permute-start(bf16[64,1024]{1,0:T(8,128)(2,1)S(1)} %pad_maximum_fusion.1), channel_id=1, source_target_pairs={{0,6},{1,7},{2,0},{3,1},{4,2},{5,3},{6,4},{7,5},{8,14},{9,15},{10,... | collective-permute-start | bytes 393224 | tf_op jit(solution)/shard_map/ppermute | solution.py:362
  18.3 11.9 %collective-permute-start.18 = (bf16[64,1024]{1,0:T(8,128)(2,1)S(1)}, bf16[64,1024]{1,0:T(8,128)(2,1)S(1)}, u32[]{:S(2)}, u32[]{:S(2)}) collective-permute-start(bf16[64,1024]{1,0:T(8,128)(2,1)S(1)} %pad_maximum_fusion.1), channel_id=1, source_target_pairs={{0,5},{1,4},{2,7},{3,6},{4,1},{5,0},{6,3},{7,2},{8,13},{9,12},{10,... | collective-permute-start | bytes 393224 | tf_op jit(solution)/shard_map/ppermute | solution.py:371
  31.1 6.2 %collective-permute-start.1 = (bf16[1024,128]{1,0:T(8,128)(2,1)S(1)}, bf16[1024,128]{1,0:T(8,128)(2,1)}, u32[]{:S(2)}, u32[]{:S(2)}) collective-permute-start(bf16[1024,128]{1,0:T(8,128)(2,1)S(1)} %collective-permute-done.refs_1_), channel_id=1, source_target_pairs={{0,7},{1,0},{2,1},{3,2},{4,3},{5,4},{6,5},{7,6},{8,15},{9,8},{10,9... | collective-permute-start | bytes 786440 | tf_op jit(solution)/shard_map/ppermute | solution.py:362
  33.5 7.3 %collective-permute-start.4 = (bf16[1024,128]{1,0:T(8,128)(2,1)}, bf16[1024,128]{1,0:T(8,128)(2,1)}, u32[]{:S(2)}, u32[]{:S(2)}) collective-permute-start(bf16[1024,128]{1,0:T(8,128)(2,1)} %collective-permute-done.3.refs_6_), channel_id=1, source_target_pairs={{0,1},{1,2},{2,3},{3,4},{4,5},{5,6},{6,7},{7,0},{8,9},{9,10},{10,1... | collective-permute-start | bytes 786440 | tf_op jit(solution)/shard_map/ppermute | solution.py:362
  37.3 11.4 %collective-permute-start.2 = (bf16[1024,128]{1,0:T(8,128)(2,1)}, bf16[1024,128]{1,0:T(8,128)(2,1)S(1)}, u32[]{:S(2)}, u32[]{:S(2)}) collective-permute-start(bf16[1024,128]{1,0:T(8,128)(2,1)} %collective-permute-done.1.refs_2_), channel_id=1, source_target_pairs={{0,7},{1,0},{2,1},{3,2},{4,3},{5,4},{6,5},{7,6},{8,15},{9,8},{10,9... | collective-permute-start | bytes 786440 | tf_op jit(solution)/shard_map/ppermute | solution.py:362
  40.9 6.7 %collective-permute-start.5 = (bf16[1024,128]{1,0:T(8,128)(2,1)}, bf16[1024,128]{1,0:T(8,128)(2,1)}, u32[]{:S(2)}, u32[]{:S(2)}) collective-permute-start(bf16[1024,128]{1,0:T(8,128)(2,1)} %collective-permute-done.4.refs_7_), channel_id=1, source_target_pairs={{0,1},{1,2},{2,3},{3,4},{4,5},{5,6},{6,7},{7,0},{8,9},{9,10},{10,1... | collective-permute-start | bytes 786440 | tf_op jit(solution)/shard_map/ppermute | solution.py:362
  48.5 5.1 %collective-permute-start.6 = (bf16[512,128]{1,0:T(8,128)(2,1)S(1)}, bf16[512,128]{1,0:T(8,128)(2,1)S(1)}, u32[]{:S(2)}, u32[]{:S(2)}) collective-permute-start(bf16[512,128]{1,0:T(8,128)(2,1)S(1)} %slice.8), channel_id=1, source_target_pairs={{0,1},{1,2},{2,3},{3,4},{4,5},{5,6},{6,7},{7,0},{8,9},{9,10},{10,1... | collective-permute-start | bytes 393224 | tf_op jit(solution)/shard_map/ppermute | solution.py:362
  48.7 5.0 %collective-permute-start.7 = (bf16[512,128]{1,0:T(8,128)(2,1)S(1)}, bf16[512,128]{1,0:T(8,128)(2,1)S(1)}, u32[]{:S(2)}, u32[]{:S(2)}) collective-permute-start(bf16[512,128]{1,0:T(8,128)(2,1)S(1)} %slice.9), channel_id=1, source_target_pairs={{0,7},{1,0},{2,1},{3,2},{4,3},{5,4},{6,5},{7,6},{8,15},{9,8},{10,9... | collective-permute-start | bytes 393224 | tf_op jit(solution)/shard_map/ppermute | solution.py:362
  56.4 6.3 %collective-permute-start.8 = (bf16[64,1024]{1,0:T(8,128)(2,1)S(1)}, bf16[64,1024]{1,0:T(8,128)(2,1)S(1)}, u32[]{:S(2)}, u32[]{:S(2)}) collective-permute-start(bf16[64,1024]{1,0:T(8,128)(2,1)S(1)} %get-tuple-element.9), channel_id=1, source_target_pairs={{0,1},{1,2},{2,3},{3,4},{4,5},{5,6},{6,7},{7,0},{8,9},{9,10},{10,1... | collective-permute-start | bytes 393224 | tf_op jit(solution)/shard_map/ppermute | solution.py:362
  56.5 6.5 %collective-permute-start.12 = (bf16[64,1024]{1,0:T(8,128)(2,1)S(1)}, bf16[64,1024]{1,0:T(8,128)(2,1)S(1)}, u32[]{:S(2)}, u32[]{:S(2)}) collective-permute-start(bf16[64,1024]{1,0:T(8,128)(2,1)S(1)} %get-tuple-element.10), channel_id=1, source_target_pairs={{0,7},{1,0},{2,1},{3,2},{4,3},{5,4},{6,5},{7,6},{8,15},{9,8},{10,9... | collective-permute-start | bytes 393224 | tf_op jit(solution)/shard_map/ppermute | solution.py:362
  62.9 7.3 %collective-permute-start.9 = (bf16[128,1024]{1,0:T(8,128)(2,1)S(1)}, bf16[128,1024]{1,0:T(8,128)(2,1)S(1)}, u32[]{:S(2)}, u32[]{:S(2)}) collective-permute-start(bf16[128,1024]{1,0:T(8,128)(2,1)S(1)} %join.8), channel_id=1, source_target_pairs={{0,1},{1,2},{2,3},{3,4},{4,5},{5,6},{6,7},{7,0},{8,9},{9,10},{10,1... | collective-permute-start | bytes 786440 | tf_op jit(solution)/shard_map/ppermute | solution.py:362
  63.2 7.3 %collective-permute-start.13 = (bf16[128,1024]{1,0:T(8,128)(2,1)S(1)}, bf16[128,1024]{1,0:T(8,128)(2,1)S(1)}, u32[]{:S(2)}, u32[]{:S(2)}) collective-permute-start(bf16[128,1024]{1,0:T(8,128)(2,1)S(1)} %join.11), channel_id=1, source_target_pairs={{0,7},{1,0},{2,1},{3,2},{4,3},{5,4},{6,5},{7,6},{8,15},{9,8},{10,9... | collective-permute-start | bytes 786440 | tf_op jit(solution)/shard_map/ppermute | solution.py:362
  70.3 8.9 %collective-permute-start.10 = (bf16[128,1024]{1,0:T(8,128)(2,1)S(1)}, bf16[128,1024]{1,0:T(8,128)(2,1)S(1)}, u32[]{:S(2)}, u32[]{:S(2)}) collective-permute-start(bf16[128,1024]{1,0:T(8,128)(2,1)S(1)} %join.9), channel_id=1, source_target_pairs={{0,1},{1,2},{2,3},{3,4},{4,5},{5,6},{6,7},{7,0},{8,9},{9,10},{10,1... | collective-permute-start | bytes 786440 | tf_op jit(solution)/shard_map/ppermute | solution.py:362
  70.7 8.9 %collective-permute-start.14 = (bf16[128,1024]{1,0:T(8,128)(2,1)S(1)}, bf16[128,1024]{1,0:T(8,128)(2,1)S(1)}, u32[]{:S(2)}, u32[]{:S(2)}) collective-permute-start(bf16[128,1024]{1,0:T(8,128)(2,1)S(1)} %join.12), channel_id=1, source_target_pairs={{0,7},{1,0},{2,1},{3,2},{4,3},{5,4},{6,5},{7,6},{8,15},{9,8},{10,9... | collective-permute-start | bytes 786440 | tf_op jit(solution)/shard_map/ppermute | solution.py:362
  79.4 9.6 %collective-permute-start.11 = (bf16[128,1024]{1,0:T(8,128)(2,1)S(1)}, bf16[128,1024]{1,0:T(8,128)(2,1)S(1)}, u32[]{:S(2)}, u32[]{:S(2)}) collective-permute-start(bf16[128,1024]{1,0:T(8,128)(2,1)S(1)} %join.10), channel_id=1, source_target_pairs={{0,1},{1,2},{2,3},{3,4},{4,5},{5,6},{6,7},{7,0},{8,9},{9,10},{10,1... | collective-permute-start | bytes 786440 | tf_op jit(solution)/shard_map/ppermute | solution.py:362
  79.7 9.3 %collective-permute-start.15 = (bf16[128,1024]{1,0:T(8,128)(2,1)S(1)}, bf16[128,1024]{1,0:T(8,128)(2,1)S(1)}, u32[]{:S(2)}, u32[]{:S(2)}) collective-permute-start(bf16[128,1024]{1,0:T(8,128)(2,1)S(1)} %join.13), channel_id=1, source_target_pairs={{0,7},{1,0},{2,1},{3,2},{4,3},{5,4},{6,5},{7,6},{8,15},{9,8},{10,9... | collective-permute-start | bytes 786440 | tf_op jit(solution)/shard_map/ppermute | solution.py:362
  89.3 8.1 %collective-permute-start.19 = (bf16[128,1024]{1,0:T(8,128)(2,1)S(1)}, bf16[128,1024]{1,0:T(8,128)(2,1)S(1)}, u32[]{:S(2)}, u32[]{:S(2)}) collective-permute-start(bf16[128,1024]{1,0:T(8,128)(2,1)S(1)} %get-tuple-element.11.rows_ref), channel_id=1, source_target_pairs={{0,1},{1,0},{2,3},{3,2},{4,5},{5,4},{6,7},{7,6},{8,9},{9,8},{10,11... | collective-permute-start | bytes 786440 | tf_op jit(solution)/shard_map/ppermute | solution.py:365
  108.4 8.0 %collective-permute-start.20 = (bf16[128,1024]{1,0:T(8,128)(2,1)S(1)}, bf16[128,1024]{1,0:T(8,128)(2,1)S(1)}, u32[]{:S(2)}, u32[]{:S(2)}) collective-permute-start(bf16[128,1024]{1,0:T(8,128)(2,1)S(1)} %feed.3), channel_id=1, source_target_pairs={{0,1},{1,0},{2,3},{3,2},{4,5},{5,4},{6,7},{7,6},{8,9},{9,8},{10,11... | collective-permute-start | bytes 786440 | tf_op jit(solution)/shard_map/ppermute | solution.py:365
  117.7 16.0 %all-to-all-start = ((f32[8,8,1024]{2,1,0:T(8,128)}), f32[8,8,1024]{2,1,0:T(8,128)S(1)}, u32[]{:S(2)}, u32[]{:S(2)}) async-start(f32[8,8,1024]{2,1,0:T(8,128)} %pool.1), calls=%async_computation | async-start | bytes 524288 | tf_op jit(solution)/shard_map/all_to_all | solution.py:451
  140.9 13.7 %all-to-all-start.1 = ((bf16[16,8,1024]{2,1,0:T(8,128)(2,1)}), bf16[16,8,1024]{2,1,0:T(8,128)(2,1)S(1)}, u32[]{:S(2)}, u32[]{:S(2)}) async-start(bf16[16,8,1024]{2,1,0:T(8,128)(2,1)} %bitcast.7), calls=%async_computation.1 | async-start | bytes 524288 | tf_op jit(solution)/shard_map/all_to_all | solution.py:462
  (11 other events, 414.0 us)
Sparse Core Ops, SparseCore 0:
  31.2 70.7 all-gather.1
